TPU v7x, 512 devices: a whole 4x4x16 slice. The times are simulated.
512 devices in a mesh: dp: 16 (over y_lo, x, core), expert: 32 (over z, y_hi).
Axes of the slice: x: 4, y: 4 (y_hi: 2, y_lo: 2; y = y_hi * 2 + y_lo), z: 16, core: 2. Of those that a mesh axis runs over, the one named last changes fastest.
Arguments:
- tokens: bfloat16 [65536, 2048], P(('dp', 'expert')), may hold values from -6 to 6
- target: bfloat16 [65536, 2048], P(('dp', 'expert')), may hold values from -6 to 6
- routes: int32 [65536, 2], P(('dp', 'expert')), may hold values from 0 to 15, all different within a row; in each aligned block of 128 rows (0 to 127, 128 to 255, ...) at most 20 rows name the same one
- gates: float32 [65536, 2], P(('dp', 'expert')), may hold values from 0.2 to 0.8
- w_gate: bfloat16 [2048, 12288], P('dp', 'expert'), may hold values from -0.125 to 0.125
- w_up: bfloat16 [2048, 12288], P('dp', 'expert'), may hold values from -0.125 to 0.125
- w_down: bfloat16 [12288, 2048], P('expert', 'dp'), may hold values from -0.21875 to 0.21875
- error: bfloat16 [196608, 2048], P(('dp', 'expert')), may hold values from -6 to 6
- q_start: float32 [2048, 512], P(None, 'expert'), may hold values from -6 to 6
Outputs:
- token_grad: bfloat16 [65536, 2048], P(('dp', 'expert'))
- p_factor: float32 [12288, 32], P('expert')
- q_factor: float32 [2048, 512], P('dp', 'expert')
- new_error: bfloat16 [196608, 2048], P(('dp', 'expert'))
Inputs may be any that keep to these rules, and one draw needn't show every extreme that they name: `routes`: each token names 2 different experts; in the 128 rows of one device no expert is named more than 20 times, a bound that some block reaches.
All inputs are finite; a program needn't handle non-finite values.
Results may differ from a plain program's by a relative error of at most 0.0085.
Values may be sent and summed in bfloat16 or wider, within the bound.
No kernel may reach another device: no remote copies, remote signals or barrier semaphores. Data moves between devices by JAX's collectives and lax.ppermute only.
A program may use at most 64 MiB of HBM per device.

v0:
```python
import jax
import jax.numpy as jnp
from jax import lax
from jax.sharding import PartitionSpec as P


def swapped(value, axis, bit):
    mask = 2**bit
    pairs = [(source, source ^ mask) for source in range(lax.axis_size(axis))]
    return lax.ppermute(value, axis, pairs)


def contract_first(left, right, precision=None):
    return lax.dot_general(
        left,
        right,
        (((0,), (0,)), ((), ())),
        precision=precision,
        preferred_element_type=jnp.float32,
    )


def contract_last(left, right):
    return lax.dot_general(
        left, right, (((1,), (1,)), ((), ())), preferred_element_type=jnp.float32
    )


def in_order(mine, other, parity, axis_dim):
    first = jnp.where(parity == 0, mine, other)
    second = jnp.where(parity == 0, other, mine)
    return jnp.concatenate([first, second], axis=axis_dim)


def shards(tokens, target, routes, gates, w_gate, w_up, w_down, error, q_start):
    groups = lax.axis_size("expert")
    experts = groups // 2
    parity = lax.axis_index("expert") % 2
    tok, width = tokens.shape
    top = routes.shape[1]
    capacity = max(2, min(tok, 2 * (5 * tok * top // (8 * experts))))
    slots = experts * capacity
    highest = lax.Precision.HIGHEST
    gate_cols, up_cols = (
        lax.all_gather(w_gate, "dp", axis=0, tiled=True),
        lax.all_gather(w_up, "dp", axis=0, tiled=True),
    )
    down_rows = lax.all_gather(w_down, "dp", axis=1, tiled=True)
    expert_ids = jnp.arange(experts, dtype=jnp.int32)
    hits = (routes[:, :, None] == expert_ids).astype(jnp.int32)
    per_token = jnp.sum(hits, axis=1)
    earlier = jnp.cumsum(per_token, axis=0) - per_token
    position = jnp.sum(hits * earlier[:, None, :], axis=2)
    slot_ids = routes * capacity + position
    select = (slot_ids[:, :, None] == jnp.arange(slots, dtype=jnp.int32)).astype(jnp.bfloat16)
    spread = jnp.sum(select, axis=1)
    select_flat = select.reshape(tok * top, slots)

    def deliver(rows):
        copies = jnp.broadcast_to(
            rows.reshape(experts, 1, capacity, width), (experts, 2, capacity, width)
        )
        received = lax.all_to_all(
            copies.reshape(groups, capacity, width),
            "expert",
            split_axis=0,
            concat_axis=0,
            tiled=True,
        )
        return received.reshape(groups * capacity, width)

    def collect(part):
        part = part.reshape(groups, capacity, width)
        back = lax.all_to_all(part, "expert", split_axis=0, concat_axis=0, tiled=True)
        pairs = back.reshape(experts, 2, capacity, width).astype(jnp.float32)
        summed = jnp.sum(pairs, axis=1).astype(jnp.bfloat16).reshape(slots, width)
        return lax.optimization_barrier(summed)

    send_rows = contract_first(spread, tokens).astype(jnp.bfloat16)
    inbox = deliver(send_rows)
    pre_gate = jnp.dot(inbox, gate_cols, preferred_element_type=jnp.float32)
    pre_up = jnp.dot(inbox, up_cols, preferred_element_type=jnp.float32)
    sig = jax.nn.sigmoid(pre_gate)
    act = pre_gate * sig
    hidden = (act * pre_up).astype(jnp.bfloat16)
    part_out = jnp.dot(hidden, down_rows, preferred_element_type=jnp.float32).astype(jnp.bfloat16)
    expert_out = collect(part_out)
    picked = jnp.dot(select_flat, expert_out, preferred_element_type=jnp.float32).reshape(
        tok, top, width
    )
    layer_sum = jnp.sum(gates[:, :, None] * picked, axis=1)
    slope = layer_sum - target.astype(jnp.float32)
    out_grad = (
        (gates[:, :, None] * slope[:, None, :]).astype(jnp.bfloat16).reshape(tok * top, width)
    )
    send_grad = contract_first(select_flat, out_grad).astype(jnp.bfloat16)
    grad_in = deliver(send_grad)
    hidden_grad = contract_last(grad_in, down_rows)
    weight_grad = contract_first(hidden, grad_in)
    gate_grad = (hidden_grad * pre_up * sig * (1.0 + pre_gate * (1.0 - sig))).astype(jnp.bfloat16)
    up_grad = (hidden_grad * act).astype(jnp.bfloat16)
    token_part = (contract_last(gate_grad, gate_cols) + contract_last(up_grad, up_cols)).astype(
        jnp.bfloat16
    )
    slot_grad = collect(token_part)
    gathered = jnp.dot(select_flat, slot_grad, preferred_element_type=jnp.float32).reshape(
        tok, top, width
    )
    token_grad = jnp.sum(gathered, axis=1).astype(jnp.bfloat16)
    merged = weight_grad + error.astype(jnp.float32)
    half_rows_count = merged.shape[0]
    rank = 2 * q_start.shape[1]
    q_partner = swapped(q_start, "expert", 0)
    q_full = in_order(q_start, q_partner, parity, 1)
    left_local = jnp.dot(merged, q_full, precision=highest)
    left = lax.psum(left_local, "dp")

    def column_step(index, basis):
        column = lax.dynamic_slice_in_dim(left, index, 1, 1)
        dots_local = contract_first(basis, column, precision=highest)
        dots_all = dots_local + swapped(dots_local, "expert", 0)
        resid = column - jnp.dot(basis, dots_all, precision=highest)
        size_local = jnp.sum(resid * resid, keepdims=True)
        size_all = size_local + swapped(size_local, "expert", 0)
        return lax.dynamic_update_slice_in_dim(basis, resid / jnp.sqrt(size_all), index, 1)

    p_hat = lax.fori_loop(0, rank, column_step, jnp.zeros((half_rows_count, rank), jnp.float32))
    right_local = contract_first(merged, p_hat, precision=highest)
    right_pair = right_local + swapped(right_local.astype(jnp.bfloat16), "expert", 0).astype(
        right_local.dtype
    )
    right_mean = lax.psum(right_pair, "dp") / lax.axis_size("dp")
    approx = lax.dot_general(
        p_hat,
        right_mean,
        (((1,), (1,)), ((), ())),
        precision=highest,
        preferred_element_type=jnp.float32,
    )
    new_error = (merged - approx).astype(jnp.bfloat16)
    q_columns = lax.dynamic_slice_in_dim(right_mean, parity * (rank // 2), rank // 2, 1)
    dp_rows = width // lax.axis_size("dp")
    q_factor = lax.dynamic_slice_in_dim(q_columns, lax.axis_index("dp") * dp_rows, dp_rows, 0)
    return (token_grad, p_hat, q_factor, new_error)


def solution(mesh):
    in_specs = (
        P(("dp", "expert"), None),
        P(("dp", "expert"), None),
        P(("dp", "expert"), None),
        P(("dp", "expert"), None),
        P("dp", "expert"),
        P("dp", "expert"),
        P("expert", "dp"),
        P(("dp", "expert"), None),
        P(None, "expert"),
    )
    out_specs = (
        P(("dp", "expert"), None),
        P("expert", None),
        P("dp", "expert"),
        P(("dp", "expert"), None),
    )
    return jax.shard_map(shards, mesh=mesh, in_specs=in_specs, out_specs=out_specs, check_vma=False)
```

profile of v0, /device:TPU:1, one launch (start us, length us, event | category | flops | bytes accessed | tf_op | source)
XLA Modules:
  0.0 1269.8 jit_solution(1503788168238587694)
XLA Ops:
  12.6 18.7 %all-to-all-start = ((bf16[32,20,2048]{2,1,0:T(8,128)(2,1)}), bf16[32,20,2048]{2,1,0:T(8,128)(2,1)S(1)}, u32[]{:S(2)}, u32[]{:S(2)}) async-start(bf16[32,20,2048]{2,1,0:T(8,128)(2,1)} %bitcast.5), calls=%async_computation | async-start | bytes 6291456 | tf_op jit(solution)/shard_map/all_to_all | solution.py:63
  33.5 138.6 %all-to-all-done = bf16[32,20,2048]{2,1,0:T(8,128)(2,1)S(1)} async-done(((bf16[32,20,2048]{2,1,0:T(8,128)(2,1)}), bf16[32,20,2048]{2,1,0:T(8,128)(2,1)S(1)}, u32[]{:S(2)}, u32[]{:S(2)}) %all-to-all-start) | async-done | bytes 2621472 | tf_op jit(solution)/shard_map/all_to_all | solution.py:63
  178.0 5.1 multiply_convert_fusion.4
  191.8 151.0 %all_to_all.20 = bf16[32,20,2048]{2,1,0:T(8,128)(2,1)S(1)} all-to-all(bf16[32,20,2048]{2,1,0:T(8,128)(2,1)S(1)} %reshape.101), channel_id=1, replica_groups=mesh['dp'=16,'expert'=32] {'expert'}, dimensions={0} | all-to-all | bytes 5242880 | tf_op jit(solution)/shard_map/all_to_all | solution.py:74
  348.1 7.8 all-to-all-start.2
  366.4 129.8 %all-to-all-done.2 = bf16[32,20,2048]{2,1,0:T(8,128)(2,1)S(1)} async-done(((bf16[32,20,2048]{2,1,0:T(8,128)(2,1)}), bf16[32,20,2048]{2,1,0:T(8,128)(2,1)S(1)}, u32[]{:S(2)}, u32[]{:S(2)}) %all-to-all-start.2) | async-done | bytes 2621472 | tf_op jit(solution)/shard_map/all_to_all | solution.py:63
  505.0 51.4 %psum.14 = f32[384,32]{0,1:T(8,128)S(1)} all-reduce(f32[384,32]{0,1:T(8,128)S(1)} %fusion.14), channel_id=1, replica_groups=mesh['dp'=16,'expert'=32] {'dp'}, use_global_device_ids=true, to_apply=%region_8.9 | all-reduce | flops 12288 | bytes 98304 | tf_op jit(solution)/shard_map/psum | solution.py:116
  565.2 5.2 reshape.106
  570.4 10.1 all-to-all-start.3
  580.5 454.7 %while.13 = (s32[]{:T(128)}, f32[384,32]{0,1:T(8,128)S(1)}, f32[384,32]{0,1:T(8,128)S(1)}, s32[]{:T(128)}, s32[]{:T(128)}) while((s32[]{:T(128)}, f32[384,32]{0,1:T(8,128)S(1)}, f32[384,32]{0,1:T(8,128)S(1)}, s32[]{:T(128)}, s32[]{:T(128)}) %tuple.40), condition=%wide.region_11.12_spmd, body=%wide.region_9.11_spmd.sunk | while | flops 296482 | bytes 110157 | solution.py:127
  698.3 4.9 collective-permute-start
  705.1 5.0 collective-permute-start.1
  713.1 4.9 collective-permute-start
  719.9 5.1 collective-permute-start.1
  727.5 4.9 collective-permute-start
  741.5 4.9 collective-permute-start
  755.5 4.9 collective-permute-start
  769.5 4.9 collective-permute-start
  783.5 4.9 collective-permute-start
  797.5 4.9 collective-permute-start
  804.1 4.9 collective-permute-start.1
  811.5 4.9 collective-permute-start
  818.0 4.9 collective-permute-start.1
  825.5 4.9 collective-permute-start
  832.0 4.9 collective-permute-start.1
  839.5 4.9 collective-permute-start
  846.0 4.9 collective-permute-start.1
  853.5 4.9 collective-permute-start
  860.0 4.9 collective-permute-start.1
  867.4 4.9 collective-permute-start
  874.0 4.9 collective-permute-start.1
  881.4 4.9 collective-permute-start
  895.4 4.9 collective-permute-start
  909.4 4.9 collective-permute-start
  923.4 4.9 collective-permute-start
  937.4 4.9 collective-permute-start
  951.4 4.9 collective-permute-start
  957.9 4.9 collective-permute-start.1
  965.4 4.9 collective-permute-start
  971.9 4.9 collective-permute-start.1
  979.4 4.9 collective-permute-start
  993.4 4.9 collective-permute-start
  1007.3 4.9 collective-permute-start
  1013.9 4.9 collective-permute-start.1
  1021.3 4.9 collective-permute-start
  1027.9 4.9 collective-permute-start.1
  1037.2 5.1 collective-permute-start.3
  1045.2 207.1 %all-reduce.2.cloned.1.call-done = f32[2048,32]{0,1:T(8,128)} async-done(((f32[2048,32]{0,1:T(8,128)}), f32[2048,32]{0,1:T(8,128)}) %all-reduce.2.cloned.1.call-update) | async-done | bytes 262160 | tf_op jit(solution)/shard_map/psum | solution.py:132
  (297 shorter events, 306.2 us)
Async XLA Ops:
  12.6 159.4 %all-to-all-start = ((bf16[32,20,2048]{2,1,0:T(8,128)(2,1)}), bf16[32,20,2048]{2,1,0:T(8,128)(2,1)S(1)}, u32[]{:S(2)}, u32[]{:S(2)}) async-start(bf16[32,20,2048]{2,1,0:T(8,128)(2,1)} %bitcast.5), calls=%async_computation | async-start | bytes 6291456 | tf_op jit(solution)/shard_map/all_to_all | solution.py:63
  31.3 143.0 %all-gather.4.cloned.1.call-start = ((), (), s32[]{:S(2)}) async-start(), calls=%async_computation.4 | async-start | bytes 1671168 | tf_op jit(solution)/shard_map/all_gather | solution.py:45
  32.0 146.0 %all-gather.6.cloned.1.call-start = ((), (), s32[]{:S(2)}) async-start(), calls=%async_computation.5 | async-start | bytes 1671168 | tf_op jit(solution)/shard_map/all_gather | solution.py:46
  32.7 150.3 %all-gather.8.cloned.1.call-start = ((), (), s32[]{:S(2)}) async-start(), calls=%async_computation.6 | async-start | bytes 1671168 | tf_op jit(solution)/shard_map/all_gather | solution.py:48
  348.1 148.1 %all-to-all-start.2 = ((bf16[32,20,2048]{2,1,0:T(8,128)(2,1)}), bf16[32,20,2048]{2,1,0:T(8,128)(2,1)S(1)}, u32[]{:S(2)}, u32[]{:S(2)}) async-start(bf16[32,20,2048]{2,1,0:T(8,128)(2,1)} %bitcast.9), calls=%async_computation.2 | async-start | bytes 6291456 | tf_op jit(solution)/shard_map/all_to_all | solution.py:63
  355.9 9.6 collective-permute-start.2
  570.4 688.3 %all-to-all-start.3 = ((bf16[32,20,2048]{2,1,0:T(8,128)(2,1)}), bf16[32,20,2048]{2,1,0:T(8,128)(2,1)}, u32[]{:S(2)}, u32[]{:S(2)}) async-start(bf16[32,20,2048]{2,1,0:T(8,128)(2,1)} %reshape.106), calls=%async_computation.3 | async-start | bytes 6291456 | tf_op jit(solution)/shard_map/all_to_all | solution.py:74
  580.4 671.8 %all-reduce.2.cloned.1.call-start = ((), (), s32[]{:S(2)}) async-start(), calls=%async_computation.7 | async-start | bytes 524288 | tf_op jit(solution)/shard_map/psum | solution.py:132
  580.7 5.9 collective-permute-start
  587.3 6.4 collective-permute-start.1
  595.2 6.2 collective-permute-start
  602.2 6.3 collective-permute-start.1
  610.1 6.2 collective-permute-start
  617.1 6.3 collective-permute-start.1
  624.9 6.2 collective-permute-start
  631.9 6.3 collective-permute-start.1
  646.3 6.3 collective-permute-start.1
  654.2 6.2 collective-permute-start
  661.2 6.3 collective-permute-start.1
  669.0 6.2 collective-permute-start
  676.0 6.3 collective-permute-start.1
  683.9 6.2 collective-permute-start
  690.9 5.9 collective-permute-start.1
  698.3 6.1 collective-permute-start
  705.1 6.4 collective-permute-start.1
  713.1 6.0 collective-permute-start
  719.9 6.1 collective-permute-start.1
  734.1 5.9 collective-permute-start.1
  748.1 5.9 collective-permute-start.1
  762.1 5.9 collective-permute-start.1
  776.1 5.9 collective-permute-start.1
  790.1 5.9 collective-permute-start.1
  804.1 5.9 collective-permute-start.1
  818.0 5.9 collective-permute-start.1
  832.0 5.9 collective-permute-start.1
  846.0 5.9 collective-permute-start.1
  860.0 5.9 collective-permute-start.1
  874.0 5.9 collective-permute-start.1
  888.0 5.9 collective-permute-start.1
  902.0 5.9 collective-permute-start.1
  916.0 5.9 collective-permute-start.1
  930.0 5.9 collective-permute-start.1
  944.0 5.9 collective-permute-start.1
  957.9 5.9 collective-permute-start.1
  971.9 5.9 collective-permute-start.1
  985.9 5.9 collective-permute-start.1
  1027.9 5.9 collective-permute-start.1
  1037.2 7.2 collective-permute-start.3
  (37 other events, 400.4 us)
Sparse Core Ops, SparseCore 0:
  34.2 42.6 all-gather.3
  79.1 41.9 all-gather.5
  123.1 44.2 all-gather.7
  1045.3 206.9 all-reduce.1
where the time goes:
time: 1270 us
  waiting for transfers between devices  561 us (44%)
  starting transfers between devices  350 us (28%)
  blocking collectives  202 us (16%)
  matrix products  67.7 us (5%)
  loops' own time  44 us (3%)
  local copies, waits for them, and re-layouts  22.1 us (2%)
  between operations  14.1 us (1%)
    ppermute x66, starting transfers between devices, swapped(): return lax.ppermute(value, axis, pairs)  313 us
    all_to_all x2, waiting for transfers between devices, deliver(): lax.all_to_all(copies.reshape(groups, capacity, width), 'expert', split_a...  268 us
    psum x1, waiting for transfers between devices, shards(): right_mean = lax.psum(right_pair, 'dp') / lax.axis_size('dp')  207 us
    all_to_all x1, blocking collectives, collect(): lax.all_to_all(part, 'expert', split_axis=0, concat_axis=0, tiled=True)  151 us
    ppermute x66, waiting for transfers between devices, swapped(): return lax.ppermute(value, axis, pairs)  83.3 us
    psum x1, blocking collectives, shards(): left = lax.psum(left_local, 'dp')  51.4 us
    another operation x1, loops' own time, shards(): lax.fori_loop(0, rank, column_step, jnp.zeros((half_rows_count, rank), jn...  44 us
    all_to_all x2, starting transfers between devices, deliver(): lax.all_to_all(copies.reshape(groups, capacity, width), 'expert', split_a...  26.4 us
  transfers between devices with their start and end apart: 73, of which 69 were waited for; matrix products, arithmetic and copies ran while one was open for 4% of the time, Pallas kernels for 0%

commit v1 on v0

v1 whole, which is shorter than its diff:
```python
import jax
import jax.numpy as jnp
from jax import lax
from jax.experimental import pallas as pl
from jax.experimental.pallas import tpu as pltpu
from jax.sharding import Mesh
from jax.sharding import PartitionSpec as P

HIGHEST = lax.Precision.HIGHEST
PIECES = 2


def dot(left, right, dims, precision=None):
    return lax.dot_general(
        left, right, (dims, ((), ())), precision=precision, preferred_element_type=jnp.float32
    )


def swapped(value, axis, mask):
    pairs = [(source, source ^ mask) for source in range(lax.axis_size(axis))]
    return lax.ppermute(value, axis, pairs)


def summed(value):
    bit = 1
    while bit < lax.axis_size("dp"):
        value = value + swapped(value, "dp", bit)
        bit *= 2
    return value + swapped(value, "half", 1)


def basis_kernel(left_ref, out_ref):
    left = left_ref[...]
    rank = left.shape[0]
    gram = lax.dot_general(
        left, left, (((1,), (1,)), ((), ())), precision=HIGHEST, preferred_element_type=jnp.float32
    )
    row_ids = lax.broadcasted_iota(jnp.int32, (rank, rank), 0)
    inverse = jnp.where(
        row_ids == lax.broadcasted_iota(jnp.int32, (rank, rank), 1), 1.0, 0.0
    ).astype(jnp.float32)
    for k in range(rank):
        scale = 1.0 / jnp.sqrt(gram[k : k + 1, k : k + 1])
        gram_row = gram[k : k + 1, :] * scale
        inverse_row = inverse[k : k + 1, :] * scale
        below = jnp.where(row_ids > k, gram[:, k : k + 1] * scale, 0.0)
        gram = gram - below * gram_row
        inverse = jnp.where(row_ids == k, inverse_row, inverse - below * inverse_row)
    out_ref[...] = lax.dot_general(
        inverse, left, (((1,), (0,)), ((), ())), precision=HIGHEST, preferred_element_type=jnp.float32
    )


def basis_of(left_t):
    return pl.pallas_call(
        basis_kernel,
        out_shape=jax.ShapeDtypeStruct(left_t.shape, jnp.float32),
        in_specs=[pl.BlockSpec(memory_space=pltpu.VMEM)],
        out_specs=pl.BlockSpec(memory_space=pltpu.VMEM),
    )(left_t)


def shards(tokens, target, routes, gates, w_gate, w_up, w_down, error, q_start):
    experts = lax.axis_size("expert")
    half = lax.axis_index("half")
    tok, width = tokens.shape
    top = routes.shape[1]
    hidden_half = w_gate.shape[1]
    capacity = max(2, min(tok, 2 * (5 * tok * top // (8 * experts))))
    piece = width // PIECES
    unit = PIECES * capacity
    slots = experts * capacity
    bf16, f32 = jnp.bfloat16, jnp.float32

    def both_halves(mine, other):
        return jnp.where(half == 0, mine, other), jnp.where(half == 0, other, mine)

    own = jnp.concatenate([w_gate, w_up, w_down.T], axis=1)
    first, second = both_halves(own, swapped(own, "half", 1))
    cut = [slice(i * hidden_half, (i + 1) * hidden_half) for i in range(3)]
    packed = jnp.concatenate([part[:, c] for c in cut for part in (first, second)], axis=1)
    weights = lax.all_gather(packed, "dp", axis=0, tiled=True)
    inner = 2 * hidden_half

    expert_ids = jnp.arange(experts, dtype=jnp.int32)
    hits = (routes[:, :, None] == expert_ids).astype(jnp.int32)
    per_token = jnp.sum(hits, axis=1)
    earlier = jnp.cumsum(per_token, axis=0) - per_token
    position = jnp.sum(hits * earlier[:, None, :], axis=2)
    base = (routes * unit + position).T
    places = jnp.arange(PIECES, dtype=jnp.int32)[:, None, None] * capacity + base
    select = (places[..., None] == jnp.arange(experts * unit, dtype=jnp.int32)).astype(bf16)
    spread = jnp.sum(select, axis=1).reshape(PIECES * tok, experts * unit)
    select = select.reshape(PIECES * top * tok, experts * unit)

    def pieces_of(rows):
        return jnp.concatenate(jnp.split(rows, PIECES, axis=-1), axis=0)

    def exchange(rows):
        sent = rows.reshape(experts, unit, piece)
        return lax.all_to_all(sent, "expert", split_axis=0, concat_axis=0, tiled=True)

    def rows_of(received):
        parts = received.reshape(experts, PIECES, capacity, piece)
        return parts.transpose(0, 2, 1, 3).reshape(slots, width)

    def units_of(rows):
        parts = rows.reshape(experts, capacity, PIECES, piece)
        return parts.transpose(0, 2, 1, 3).reshape(experts * unit, piece)

    inbox = rows_of(exchange(dot(spread, pieces_of(tokens), ((0,), (0,))).astype(bf16)))

    q_t = q_start.T
    q_full = jnp.concatenate(both_halves(q_t, swapped(q_t, "half", 1)), axis=0)
    error_left = dot(q_full, error.astype(f32), ((1,), (1,)), HIGHEST)

    pre = dot(inbox, weights[:, : 2 * inner], ((1,), (0,)))
    pre_gate, pre_up = pre[:, :inner], pre[:, inner:]
    sig = jax.nn.sigmoid(pre_gate)
    act = pre_gate * sig
    hidden = (act * pre_up).astype(bf16)
    down = weights[:, 2 * inner :]
    expert_out = dot(hidden, down, ((1,), (1,))).astype(bf16)
    returned = exchange(units_of(expert_out)).reshape(experts * unit, piece)
    picked = dot(select, returned, ((1,), (0,))).reshape(PIECES, top, tok, piece)
    gate = gates.T[None, :, :, None]
    layer_sum = jnp.sum(gate * picked, axis=1)
    slope = layer_sum - pieces_of(target).reshape(PIECES, tok, piece).astype(f32)
    out_grad = (gate * slope[:, None]).astype(bf16).reshape(PIECES * top * tok, piece)
    grad_in = rows_of(exchange(dot(select, out_grad, ((0,), (0,))).astype(bf16)))

    hidden_parts = (hidden[:, :hidden_half], hidden[:, hidden_half:])
    hidden_mine, hidden_theirs = both_halves(*hidden_parts)
    hidden_other = swapped(hidden_theirs, "half", 1)
    grad_other = swapped(grad_in, "half", 1)

    hidden_grad = dot(grad_in, down, ((1,), (0,)))
    gate_grad = (hidden_grad * pre_up * sig * (1.0 + pre_gate * (1.0 - sig))).astype(bf16)
    up_grad = (hidden_grad * act).astype(bf16)
    both_grads = jnp.concatenate([gate_grad, up_grad], axis=1)
    token_part = dot(both_grads, weights[:, : 2 * inner], ((1,), (1,))).astype(bf16)
    slot_grad = exchange(units_of(token_part)).reshape(experts * unit, piece)
    token_grad = dot(spread, slot_grad, ((1,), (0,))).astype(bf16)
    token_grad = jnp.concatenate(jnp.split(token_grad, PIECES, axis=0), axis=1)

    grad_q = dot(q_full, grad_in.astype(f32), ((1,), (1,)), HIGHEST)
    zeros = jnp.zeros_like(error_left)
    left = dot(grad_q, hidden.astype(f32), ((1,), (0,)), HIGHEST) + jnp.concatenate(
        both_halves(error_left, zeros), axis=1
    )
    basis = basis_of(summed(left))
    basis_mine = jnp.where(half == 0, basis[:, :hidden_half], basis[:, hidden_half:])

    hidden_basis = dot(basis, hidden.astype(f32), ((1,), (1,)), HIGHEST)
    right = dot(hidden_basis, grad_in.astype(f32), ((1,), (0,)), HIGHEST) + dot(
        basis_mine, error.astype(f32), ((1,), (0,)), HIGHEST
    )
    right = summed(right) / lax.axis_size("dp")
    rank_half = right.shape[0] // 2
    q_columns = jnp.where(half == 0, right[:rank_half], right[rank_half:])
    q_rows = width // lax.axis_size("dp")
    q_factor = lax.dynamic_slice_in_dim(q_columns, lax.axis_index("dp") * q_rows, q_rows, 1).T

    merged = (
        dot(hidden_mine, grad_in, ((0,), (0,)))
        + dot(hidden_other, grad_other, ((0,), (0,)))
        + error.astype(f32)
    )
    new_error = (merged - dot(basis_mine, right, ((0,), (0,)), HIGHEST)).astype(bf16)
    return token_grad, basis_mine.T, q_factor, new_error


def solution(mesh):
    experts = mesh.shape["expert"] // 2
    split = Mesh(
        mesh.devices.reshape(mesh.shape["dp"], experts, 2), ("dp", "expert", "half")
    )
    pair = ("expert", "half")
    rows = P(("dp",) + pair, None)
    in_specs = (rows, rows, rows, rows, P("dp", pair), P("dp", pair), P(pair, "dp"), rows, P(None, pair))
    out_specs = (rows, P(pair, None), P("dp", pair), rows)
    return jax.shard_map(shards, mesh=split, in_specs=in_specs, out_specs=out_specs, check_vma=False)
```

time: 1270 us -> 406 us (0.32)
  waiting for transfers between devices: 561 us -> 159 us
  starting transfers between devices: 350 us -> 84.4 us
  blocking collectives: 202 us -> 74.4 us
  loops' own time: 44 us -> 0 us
  matrix products: 67.7 us -> 35.5 us
    ppermute x66 -> x14, starting transfers between devices: 313 us -> 49.2 us  [swapped(): return lax.ppermute(value, axis, pairs)]
    psum x1 -> x0, waiting for transfers between devices: 207 us -> none  [shards(): right_mean = lax.psum(right_pair, 'dp') / lax.axis_size('dp')]
    all_to_all x3, waiting for transfers between devices: 268 us -> 104 us  [exchange(): lax.all_to_all(sent, 'expert', split_axis=0, concat_axis=0, tiled=True)]
    all_to_all x1, blocking collectives: 151 us -> 74.4 us  [exchange(): lax.all_to_all(sent, 'expert', split_axis=0, concat_axis=0, tiled=True)]
    psum x1 -> x0, blocking collectives: 51.4 us -> none  [shards(): left = lax.psum(left_local, 'dp')]
    another operation x1 -> x0, loops' own time: 44 us -> none  [shards(): lax.fori_loop(0, rank, column_step, jnp.zeros((half_rows_count, rank), jn...]
    dot_general x78 -> x17, matrix products: 67.7 us -> 35.5 us  [dot(): lax.dot_general(left, right, (dims, ((), ())), precision=precision, prefe...]
    ppermute x66 -> x14, waiting for transfers between devices: 83.3 us -> 51.8 us  [swapped(): return lax.ppermute(value, axis, pairs)]
  transfers between devices with their start and end apart: 73 -> 18, of which waited for: 69 -> 14; matrix products, arithmetic and copies ran while one was open for 4% -> 6% of each run, Pallas kernels for 0% -> 1%
where the time goes in v1:
time: 406 us; the launch traced here: 405 us
  waiting for transfers between devices  159 us (39%)
  starting transfers between devices  84.4 us (21%)
  blocking collectives  74.4 us (18%)
  matrix products  35.5 us (9%)
  local copies, waits for them, and re-layouts  23.8 us (6%)
  between operations  14.7 us (4%)
  other arithmetic  8.47 us (2%)
  Pallas kernels  5.06 us (1%)
    all_to_all x3, waiting for transfers between devices, exchange(): lax.all_to_all(sent, 'expert', split_axis=0, concat_axis=0, tiled=True)  104 us
    all_to_all x1, blocking collectives, exchange(): lax.all_to_all(sent, 'expert', split_axis=0, concat_axis=0, tiled=True)  74.4 us
    ppermute x14, waiting for transfers between devices, swapped(): return lax.ppermute(value, axis, pairs)  51.8 us
    ppermute x14, starting transfers between devices, swapped(): return lax.ppermute(value, axis, pairs)  49.2 us
    dot_general x17, matrix products, dot(): lax.dot_general(left, right, (dims, ((), ())), precision=precision, prefe...  35.5 us
    all_to_all x3, starting transfers between devices, exchange(): lax.all_to_all(sent, 'expert', split_axis=0, concat_axis=0, tiled=True)  35.1 us
  transfers between devices with their start and end apart: 18, of which 14 were waited for; matrix products, arithmetic and copies ran while one was open for 6% of the time, Pallas kernels for 1%

profile of v1, /device:TPU:1, one launch (start us, length us, event | category | flops | bytes accessed | tf_op | source)
XLA Modules:
  0.0 404.8 jit_solution(11131029050536282216)
XLA Ops:
  10.2 5.7 %collective-permute-start = (bf16[128,1152]{0,1:T(8,128)(2,1)S(1)}, bf16[128,1152]{0,1:T(8,128)(2,1)S(1)}, u32[]{:S(2)}, u32[]{:S(2)}) collective-permute-start(bf16[128,1152]{0,1:T(8,128)(2,1)S(1)} %pad_maximum_fusion.2), channel_id=1, source_target_pairs={{0,1},{1,0},{2,3},{3,2},{4,5},{5,4},{6,7},{7,6},{8,9},{9,8},{10,11... | collective-permute-start | bytes 884744 | tf_op jit(solution)/shard_map/ppermute | solution.py:21
  15.8 4.1 %collective-permute-done = bf16[128,1152]{0,1:T(8,128)(2,1)S(1)} collective-permute-done((bf16[128,1152]{0,1:T(8,128)(2,1)S(1)}, bf16[128,1152]{0,1:T(8,128)(2,1)S(1)}, u32[]{:S(2)}, u32[]{:S(2)}) %collective-permute-start) | collective-permute-done | bytes 294944 | tf_op jit(solution)/shard_map/ppermute | solution.py:21
  23.5 74.4 %all_to_all.20 = bf16[16,40,1024]{2,1,0:T(8,128)(2,1)S(1)} all-to-all(bf16[16,40,1024]{2,1,0:T(8,128)(2,1)S(1)} %bitcast.74), channel_id=1, replica_groups=mesh['dp'=16,'expert'=16,'half'=2] {'expert'}, dimensions={0} | all-to-all | bytes 2621440 | tf_op jit(solution)/shard_map/all_to_all | solution.py:101
  98.6 1.3 copy.64
  100.3 3.2 all-gather.2.cloned.1.call-done
  103.6 5.0 %fusion.2 = f32[320,1536]{1,0:T(8,128)S(1)} fusion(bf16[320,2048]{1,0:T(8,128)(2,1)S(1)} %bitcast.86, bf16[2048,2304]{0,1:T(8,128)(2,1)} %all-gather.2.cloned.1.call-done), kind=kOutput, calls=%fused_computation.2 | convolution fusion | flops 2013265920 | bytes 9568256 | tf_op jit(solution)/shard_map/dot_general | solution.py:14
  109.8 3.1 fusion.11
  114.6 1.8 copy.68
  116.4 11.3 %all-to-all-start.1 = ((bf16[16,40,1024]{2,1,0:T(8,128)(2,1)}), bf16[16,40,1024]{2,1,0:T(8,128)(2,1)S(1)}, u32[]{:S(2)}, u32[]{:S(2)}) async-start(bf16[16,40,1024]{2,1,0:T(8,128)(2,1)} %copy.68), calls=%async_computation.1 | async-start | bytes 2621440 | tf_op jit(solution)/shard_map/all_to_all | solution.py:101
  127.9 57.5 %all-to-all-done.1 = bf16[16,40,1024]{2,1,0:T(8,128)(2,1)S(1)} async-done(((bf16[16,40,1024]{2,1,0:T(8,128)(2,1)}), bf16[16,40,1024]{2,1,0:T(8,128)(2,1)S(1)}, u32[]{:S(2)}, u32[]{:S(2)}) %all-to-all-start.1) | async-done | bytes 1310752 | tf_op jit(solution)/shard_map/all_to_all | solution.py:101
  186.6 2.0 bitcast_convert_fusion
  188.6 11.8 %all-to-all-start.2 = ((bf16[16,40,1024]{2,1,0:T(8,128)(2,1)}), bf16[16,40,1024]{2,1,0:T(8,128)(2,1)S(1)}, u32[]{:S(2)}, u32[]{:S(2)}) async-start(bf16[16,40,1024]{2,1,0:T(8,128)(2,1)} %bitcast.84), calls=%async_computation.2 | async-start | bytes 2621440 | tf_op jit(solution)/shard_map/all_to_all | solution.py:101
  200.4 4.1 %collective-permute-start.1 = (f32[16,2048]{1,0:T(8,128)S(1)}, f32[16,2048]{1,0:T(8,128)S(1)}, u32[]{:S(2)}, u32[]{:S(2)}) collective-permute-start(f32[16,2048]{1,0:T(8,128)S(1)} %bitcast.89), channel_id=1, source_target_pairs={{0,1},{1,0},{2,3},{3,2},{4,5},{5,4},{6,7},{7,6},{8,9},{9,8},{10,11... | collective-permute-start | bytes 393224 | tf_op jit(solution)/shard_map/ppermute | solution.py:21
  204.5 3.6 collective-permute-done.1
  209.7 2.1 broadcast_select_fusion.6
  211.7 46.1 %all-to-all-done.2 = bf16[16,40,1024]{2,1,0:T(8,128)(2,1)S(1)} async-done(((bf16[16,40,1024]{2,1,0:T(8,128)(2,1)}), bf16[16,40,1024]{2,1,0:T(8,128)(2,1)S(1)}, u32[]{:S(2)}, u32[]{:S(2)}) %all-to-all-start.2) | async-done | bytes 1310752 | tf_op jit(solution)/shard_map/all_to_all | solution.py:101
  261.4 3.5 multiply_convert_fusion.3
  265.9 3.3 fusion.8
  269.1 4.4 %reshape.107 = bf16[16,20,2,1024]{3,2,1,0:T(2,128)(2,1)} reshape(bf16[320,2048]{1,0:T(8,128)(2,1)} %fusion.8) | data formatting | bytes 2621440 | tf_op jit(solution)/shard_map/reshape | solution.py:108
  273.5 2.0 copy.71
  275.6 1.8 copy.72
  277.3 11.9 %all-to-all-start.3 = ((bf16[16,40,1024]{2,1,0:T(8,128)(2,1)}), bf16[16,40,1024]{2,1,0:T(8,128)(2,1)}, u32[]{:S(2)}, u32[]{:S(2)}) async-start(bf16[16,40,1024]{2,1,0:T(8,128)(2,1)} %copy.72), calls=%async_computation.3 | async-start | bytes 2621440 | tf_op jit(solution)/shard_map/all_to_all | solution.py:101
  289.3 2.1 fusion.35
  291.8 2.7 collective-permute-start.2
  295.4 2.3 collective-permute-start.3
  297.7 3.7 collective-permute-done.3
  301.5 4.0 collective-permute-start.4
  305.5 3.2 collective-permute-done.4
  308.7 2.2 collective-permute-start.5
  311.0 3.5 collective-permute-done.5
  314.5 4.1 %collective-permute-start.6 = (f32[32,768]{1,0:T(8,128)S(1)}, f32[32,768]{1,0:T(8,128)S(1)}, u32[]{:S(2)}, u32[]{:S(2)}) collective-permute-start(f32[32,768]{1,0:T(8,128)S(1)} %add.81), channel_id=1, source_target_pairs={{0,1},{1,0},{2,3},{3,2},{4,5},{5,4},{6,7},{7,6},{8,9},{9,8},{10,11... | collective-permute-start | bytes 294920 | tf_op jit(solution)/shard_map/ppermute | solution.py:21
  318.6 3.2 collective-permute-done.6
  322.4 5.1 %shard_map.120 = f32[32,768]{1,0:T(8,128)} custom-call(f32[32,768]{1,0:T(8,128)} %add.82.left_ref), custom_call_target="tpu_custom_call" | custom-call | tf_op jit(solution)/shard_map/pallas_call | solution.py:55
  327.5 1.5 fusion.45
  330.6 5.2 %collective-permute-start.7 = (f32[32,2048]{1,0:T(8,128)S(1)}, f32[32,2048]{1,0:T(8,128)S(1)}, u32[]{:S(2)}, u32[]{:S(2)}) collective-permute-start(f32[32,2048]{1,0:T(8,128)S(1)} %convolution_add_fusion), channel_id=1, source_target_pairs={{0,32},{32,0},{64,96},{96,64},{128,160},{160,128},{192,224},{224,1... | collective-permute-start | bytes 786440 | tf_op jit(solution)/shard_map/ppermute | solution.py:21
  335.9 4.1 %collective-permute-start.13 = (bf16[320,2048]{1,0:T(8,128)(2,1)S(1)}, bf16[320,2048]{1,0:T(8,128)(2,1)}, u32[]{:S(2)}, u32[]{:S(2)}) collective-permute-start(bf16[320,2048]{1,0:T(8,128)(2,1)S(1)} %bitcast.72), channel_id=1, source_target_pairs={{0,1},{1,0},{2,3},{3,2},{4,5},{5,4},{6,7},{7,6},{8,9},{9,8},{10,11... | collective-permute-start | bytes 3932168 | tf_op jit(solution)/shard_map/ppermute | solution.py:21
  340.0 2.6 collective-permute-start.8
  342.6 7.0 %collective-permute-done.8 = f32[32,2048]{1,0:T(8,128)S(1)} collective-permute-done((f32[32,2048]{1,0:T(8,128)S(1)}, f32[32,2048]{1,0:T(8,128)S(1)}, u32[]{:S(2)}, u32[]{:S(2)}) %collective-permute-start.8) | collective-permute-done | bytes 262176 | tf_op jit(solution)/shard_map/ppermute | solution.py:21
  350.3 4.0 collective-permute-start.9
  354.4 2.7 collective-permute-start.12
  357.1 3.7 collective-permute-done.9
  361.9 2.0 collective-permute-start.10
  365.5 14.3 %collective-permute-done.10 = f32[32,2048]{1,0:T(8,128)S(1)} collective-permute-done((f32[32,2048]{1,0:T(8,128)S(1)}, f32[32,2048]{1,0:T(8,128)S(1)}, u32[]{:S(2)}, u32[]{:S(2)}) %collective-permute-start.10) | collective-permute-done | bytes 262176 | tf_op jit(solution)/shard_map/ppermute | solution.py:21
  379.9 3.5 collective-permute-start.11
  383.4 2.3 fusion.47
  385.8 4.5 %collective-permute-done.11 = f32[32,2048]{1,0:T(8,128)S(1)} collective-permute-done((f32[32,2048]{1,0:T(8,128)S(1)}, f32[32,2048]{1,0:T(8,128)S(1)}, u32[]{:S(2)}, u32[]{:S(2)}) %collective-permute-start.11) | collective-permute-done | bytes 262176 | tf_op jit(solution)/shard_map/ppermute | solution.py:21
  391.0 4.2 %subtract_convert_fusion = bf16[384,2048]{1,0:T(8,128)(2,1)} fusion(bf16[384,2048]{1,0:T(8,128)(2,1)S(1)} %copy-done, f32[384,2048]{1,0:T(8,128)S(1)} %fusion.29, f32[384,2048]{1,0:T(8,128)S(1)} %fusion.47, f32[32,2048]{1,0:T(8,128)S(1)} %add_multiply_fusion, f32[32,768]{1,0:T(8,128)S(1)} %copy-done.5, pred[]{:T(512)S(6)} %eq.71), kind=kOutput, calls=%fused_computation.4 | convolution fusion | flops 305934336 | bytes 9797633 | tf_op jit(solution)/shard_map/dot_general | solution.py:14
  395.2 1.9 convolution_convert_fusion.1
  (98 shorter events, 26.5 us)
Async XLA Ops:
  7.2 96.4 %all-gather.2.cloned.1.call-start = ((), (), s32[]{:S(2)}) async-start(), calls=%async_computation.4 | async-start | bytes 10027008 | tf_op jit(solution)/shard_map/all_gather | solution.py:82
  10.2 11.8 %copy-start.12 = (s32[128,2]{0,1:T(2,128)S(1)}, s32[128,2]{0,1:T(2,128)}, u32[]{:S(2)}) copy-start(s32[128,2]{0,1:T(2,128)} %param.11) | copy-start | bytes 3076
  10.2 9.8 %collective-permute-start = (bf16[128,1152]{0,1:T(8,128)(2,1)S(1)}, bf16[128,1152]{0,1:T(8,128)(2,1)S(1)}, u32[]{:S(2)}, u32[]{:S(2)}) collective-permute-start(bf16[128,1152]{0,1:T(8,128)(2,1)S(1)} %pad_maximum_fusion.2), channel_id=1, source_target_pairs={{0,1},{1,0},{2,3},{3,2},{4,5},{5,4},{6,7},{7,6},{8,9},{9,8},{10,11... | collective-permute-start | bytes 884744 | tf_op jit(solution)/shard_map/ppermute | solution.py:21
  21.0 1.8 copy-start.8
  21.1 0.8 copy-start.7
  22.8 0.7 copy-start.1
  108.6 1.3 copy-start.3
  116.4 11.4 %copy-start.9 = (bf16[128,2048]{1,0:T(8,128)(2,1)S(1)}, bf16[128,2048]{1,0:T(8,128)(2,1)}, u32[]{:S(2)}) copy-start(bf16[128,2048]{1,0:T(8,128)(2,1)} %param.10) | copy-start | bytes 1572868
  116.4 69.0 %all-to-all-start.1 = ((bf16[16,40,1024]{2,1,0:T(8,128)(2,1)}), bf16[16,40,1024]{2,1,0:T(8,128)(2,1)S(1)}, u32[]{:S(2)}, u32[]{:S(2)}) async-start(bf16[16,40,1024]{2,1,0:T(8,128)(2,1)} %copy.68), calls=%async_computation.1 | async-start | bytes 2621440 | tf_op jit(solution)/shard_map/all_to_all | solution.py:101
  127.8 57.6 %copy-start.13 = (f32[128,2]{0,1:T(2,128)S(1)}, f32[128,2]{0,1:T(2,128)}, u32[]{:S(2)}) copy-start(f32[128,2]{0,1:T(2,128)} %param.12) | copy-start | bytes 3076
  188.6 11.8 %copy-start.11 = (f32[2048,16]{0,1:T(8,128)S(1)}, f32[2048,16]{0,1:T(8,128)}, u32[]{:S(2)}) copy-start(f32[2048,16]{0,1:T(8,128)} %param.17) | copy-start | bytes 393220
  188.6 21.1 %copy-start = (bf16[384,2048]{1,0:T(8,128)(2,1)S(1)}, bf16[384,2048]{1,0:T(8,128)(2,1)}, u32[]{:S(2)}) copy-start(bf16[384,2048]{1,0:T(8,128)(2,1)} %param.16) | copy-start | bytes 4718596
  188.6 69.2 %all-to-all-start.2 = ((bf16[16,40,1024]{2,1,0:T(8,128)(2,1)}), bf16[16,40,1024]{2,1,0:T(8,128)(2,1)S(1)}, u32[]{:S(2)}, u32[]{:S(2)}) async-start(bf16[16,40,1024]{2,1,0:T(8,128)(2,1)} %bitcast.84), calls=%async_computation.2 | async-start | bytes 2621440 | tf_op jit(solution)/shard_map/all_to_all | solution.py:101
  200.4 7.7 %collective-permute-start.1 = (f32[16,2048]{1,0:T(8,128)S(1)}, f32[16,2048]{1,0:T(8,128)S(1)}, u32[]{:S(2)}, u32[]{:S(2)}) collective-permute-start(f32[16,2048]{1,0:T(8,128)S(1)} %bitcast.89), channel_id=1, source_target_pairs={{0,1},{1,0},{2,3},{3,2},{4,5},{5,4},{6,7},{7,6},{8,9},{9,8},{10,11... | collective-permute-start | bytes 393224 | tf_op jit(solution)/shard_map/ppermute | solution.py:21
  209.0 0.7 copy-start.6
  259.9 1.5 copy-start.4
  259.9 5.1 %slice-start = ((s8[9437184]{0:T(1024)(128)(4,1)}), s8[1048576]{0:T(1024)(128)(4,1)S(1)}, s32[]{:S(2)}) async-start(s8[9437184]{0:T(1024)(128)(4,1)} %bitcast.90), calls=%async_computation.5 | async-start | bytes 2097152
  261.4 3.5 slice-start.1
  261.4 4.4 %slice-start.2 = ((s8[9437184]{0:T(1024)(128)(4,1)}), s8[4194304]{0:T(1024)(128)(4,1)S(1)}, s32[]{:S(2)}) async-start(s8[9437184]{0:T(1024)(128)(4,1)} %bitcast.90), calls=%async_computation.7 | async-start | bytes 8388608
  277.3 117.9 %all-to-all-start.3 = ((bf16[16,40,1024]{2,1,0:T(8,128)(2,1)}), bf16[16,40,1024]{2,1,0:T(8,128)(2,1)}, u32[]{:S(2)}, u32[]{:S(2)}) async-start(bf16[16,40,1024]{2,1,0:T(8,128)(2,1)} %copy.72), calls=%async_computation.3 | async-start | bytes 2621440 | tf_op jit(solution)/shard_map/all_to_all | solution.py:101
  289.3 2.1 copy-start.10
  291.8 3.6 collective-permute-start.2
  295.4 6.0 %collective-permute-start.3 = (f32[32,768]{1,0:T(8,128)S(1)}, f32[32,768]{1,0:T(8,128)S(1)}, u32[]{:S(2)}, u32[]{:S(2)}) collective-permute-start(f32[32,768]{1,0:T(8,128)S(1)} %add.78), channel_id=1, source_target_pairs={{0,64},{32,96},{64,0},{96,32},{128,192},{160,224},{192,128},{224,1... | collective-permute-start | bytes 294920 | tf_op jit(solution)/shard_map/ppermute | solution.py:21
  301.5 7.3 %collective-permute-start.4 = (f32[32,768]{1,0:T(8,128)S(1)}, f32[32,768]{1,0:T(8,128)S(1)}, u32[]{:S(2)}, u32[]{:S(2)}) collective-permute-start(f32[32,768]{1,0:T(8,128)S(1)} %add.79), channel_id=1, source_target_pairs={{0,128},{32,160},{64,192},{96,224},{128,0},{160,32},{192,64},{224,... | collective-permute-start | bytes 294920 | tf_op jit(solution)/shard_map/ppermute | solution.py:21
  308.7 5.8 %collective-permute-start.5 = (f32[32,768]{1,0:T(8,128)S(1)}, f32[32,768]{1,0:T(8,128)S(1)}, u32[]{:S(2)}, u32[]{:S(2)}) collective-permute-start(f32[32,768]{1,0:T(8,128)S(1)} %add.80), channel_id=1, source_target_pairs={{0,256},{32,288},{64,320},{96,352},{128,384},{160,416},{192,448},{... | collective-permute-start | bytes 294920 | tf_op jit(solution)/shard_map/ppermute | solution.py:21
  314.5 7.3 %collective-permute-start.6 = (f32[32,768]{1,0:T(8,128)S(1)}, f32[32,768]{1,0:T(8,128)S(1)}, u32[]{:S(2)}, u32[]{:S(2)}) collective-permute-start(f32[32,768]{1,0:T(8,128)S(1)} %add.81), channel_id=1, source_target_pairs={{0,1},{1,0},{2,3},{3,2},{4,5},{5,4},{6,7},{7,6},{8,9},{9,8},{10,11... | collective-permute-start | bytes 294920 | tf_op jit(solution)/shard_map/ppermute | solution.py:21
  327.5 2.3 copy-start.5
  330.6 9.3 %collective-permute-start.7 = (f32[32,2048]{1,0:T(8,128)S(1)}, f32[32,2048]{1,0:T(8,128)S(1)}, u32[]{:S(2)}, u32[]{:S(2)}) collective-permute-start(f32[32,2048]{1,0:T(8,128)S(1)} %convolution_add_fusion), channel_id=1, source_target_pairs={{0,32},{32,0},{64,96},{96,64},{128,160},{160,128},{192,224},{224,1... | collective-permute-start | bytes 786440 | tf_op jit(solution)/shard_map/ppermute | solution.py:21
  335.9 47.6 %collective-permute-start.13 = (bf16[320,2048]{1,0:T(8,128)(2,1)S(1)}, bf16[320,2048]{1,0:T(8,128)(2,1)}, u32[]{:S(2)}, u32[]{:S(2)}) collective-permute-start(bf16[320,2048]{1,0:T(8,128)(2,1)S(1)} %bitcast.72), channel_id=1, source_target_pairs={{0,1},{1,0},{2,3},{3,2},{4,5},{5,4},{6,7},{7,6},{8,9},{9,8},{10,11... | collective-permute-start | bytes 3932168 | tf_op jit(solution)/shard_map/ppermute | solution.py:21
  340.0 9.6 %collective-permute-start.8 = (f32[32,2048]{1,0:T(8,128)S(1)}, f32[32,2048]{1,0:T(8,128)S(1)}, u32[]{:S(2)}, u32[]{:S(2)}) collective-permute-start(f32[32,2048]{1,0:T(8,128)S(1)} %add.84), channel_id=1, source_target_pairs={{0,64},{32,96},{64,0},{96,32},{128,192},{160,224},{192,128},{224,1... | collective-permute-start | bytes 786440 | tf_op jit(solution)/shard_map/ppermute | solution.py:21
  350.3 10.5 %collective-permute-start.9 = (f32[32,2048]{1,0:T(8,128)}, f32[32,2048]{1,0:T(8,128)}, u32[]{:S(2)}, u32[]{:S(2)}) collective-permute-start(f32[32,2048]{1,0:T(8,128)} %add.85), channel_id=1, source_target_pairs={{0,128},{32,160},{64,192},{96,224},{128,0},{160,32},{192,64},{224,... | collective-permute-start | bytes 786440 | tf_op jit(solution)/shard_map/ppermute | solution.py:21
  354.4 29.0 %collective-permute-start.12 = (bf16[320,384]{1,0:T(8,128)(2,1)S(1)}, bf16[320,384]{1,0:T(8,128)(2,1)S(1)}, u32[]{:S(2)}, u32[]{:S(2)}) collective-permute-start(bf16[320,384]{1,0:T(8,128)(2,1)S(1)} %broadcast_select_fusion.2), channel_id=1, source_target_pairs={{0,1},{1,0},{2,3},{3,2},{4,5},{5,4},{6,7},{7,6},{8,9},{9,8},{10,11... | collective-permute-start | bytes 737288 | tf_op jit(solution)/shard_map/ppermute | solution.py:21
  361.9 18.0 %collective-permute-start.10 = (f32[32,2048]{1,0:T(8,128)S(1)}, f32[32,2048]{1,0:T(8,128)S(1)}, u32[]{:S(2)}, u32[]{:S(2)}) collective-permute-start(f32[32,2048]{1,0:T(8,128)S(1)} %add.86), channel_id=1, source_target_pairs={{0,256},{32,288},{64,320},{96,352},{128,384},{160,416},{192,448},{... | collective-permute-start | bytes 786440 | tf_op jit(solution)/shard_map/ppermute | solution.py:21
  379.9 10.4 %collective-permute-start.11 = (f32[32,2048]{1,0:T(8,128)S(1)}, f32[32,2048]{1,0:T(8,128)S(1)}, u32[]{:S(2)}, u32[]{:S(2)}) collective-permute-start(f32[32,2048]{1,0:T(8,128)S(1)} %add.87), channel_id=1, source_target_pairs={{0,1},{1,0},{2,3},{3,2},{4,5},{5,4},{6,7},{7,6},{8,9},{9,8},{10,11... | collective-permute-start | bytes 786440 | tf_op jit(solution)/shard_map/ppermute | solution.py:21
  391.0 4.2 %copy-start.2 = (bf16[2,128,640]{2,1,0:T(8,128)(2,1)S(1)}, bf16[2,128,640]{2,1,0:T(8,128)(2,1)}, u32[]{:S(2)}) copy-start(bf16[2,128,640]{2,1,0:T(8,128)(2,1)} %copy-done.1) | copy-start | bytes 983044
Sparse Core Ops, SparseCore 0:
  22.0 81.4 all-gather.1

commit v2 on v1

v2 whole, which is shorter than its diff:
```python
import jax
import jax.numpy as jnp
from jax import lax
from jax.experimental import pallas as pl
from jax.experimental.pallas import tpu as pltpu
from jax.sharding import Mesh
from jax.sharding import PartitionSpec as P

HIGHEST = lax.Precision.HIGHEST
BF16, F32 = jnp.bfloat16, jnp.float32
PIECES = 2
BLOCK = 4
NN = ((1,), (0,))
NT = ((1,), (1,))
TN = ((0,), (0,))
DP = ("group", "core")
PLANE = ("group", "half")


def dot(left, right, dims, precision=None):
    return lax.dot_general(
        left, right, (dims, ((), ())), precision=precision, preferred_element_type=F32
    )


def thirds(value):
    high = value.astype(BF16)
    rest = value - high.astype(F32)
    middle = rest.astype(BF16)
    low = (rest - middle.astype(F32)).astype(BF16)
    return jnp.concatenate([high, middle, low], axis=0)


def folded(value):
    rows = value.shape[0] // 3
    return value[:rows] + value[rows : 2 * rows] + value[2 * rows :]


def local_call(kernel, outs, scratch, *operands, hbm=(), out_hbm=(), memory=16, smem=()):
    def specs(count, there, scalars=()):
        spaces = [pltpu.HBM if i in there else pltpu.VMEM for i in range(count)]
        spaces = [pltpu.SMEM if i in scalars else space for i, space in enumerate(spaces)]
        return [pl.BlockSpec(memory_space=space) for space in spaces]

    return pl.pallas_call(
        kernel,
        out_shape=[jax.ShapeDtypeStruct(shape, dtype) for shape, dtype in outs],
        in_specs=specs(len(operands), hbm, smem),
        out_specs=specs(len(outs), out_hbm),
        scratch_shapes=scratch,
        compiler_params=pltpu.CompilerParams(vmem_limit_bytes=memory * 2**20),
    )(*operands)


def sides_of(array, width):
    return [array.at[:, pl.ds(side * width, width)] for side in range(2)]


def blocks_of(array, rows):
    return [array.at[pl.ds(i * rows, rows), :] for i in range(array.shape[0] // rows)]


def copies_of(sources, targets, sems, first):
    return [
        pltpu.make_async_copy(source, target, sems.at[first + i])
        for i, (source, target) in enumerate(zip(sources, targets))
    ]


def started(copies):
    for copy in copies:
        copy.start()


def finished(copies):
    for copy in copies:
        copy.wait()


def weight_copies(w_ref, proj_ref, down_ref, sems, half):
    proj, down = [], []
    for side in range(2):
        start = side * 3 * half
        proj.append(w_ref.at[:, pl.ds(start, 2 * half)])
        down.append(w_ref.at[:, pl.ds(start + 2 * half, half)])
    return (
        copies_of(proj, [proj_ref.at[side] for side in range(2)], sems, 0),
        copies_of(down, [down_ref.at[side] for side in range(2)], sems, 2),
    )


def to_rows(units_ref, gather_ref, rows_ref, arrivals):
    count, piece = gather_ref.shape[0], units_ref.shape[1]
    part = count // PIECES
    for i, copy in enumerate(arrivals):
        copy.wait()
        block = dot(gather_ref[...], units_ref[i * count : (i + 1) * count, :], NN).astype(BF16)
        for j in range(PIECES):
            rows_ref[i * part : (i + 1) * part, j * piece : (j + 1) * piece] = block[
                j * part : (j + 1) * part
            ]


def to_units(rows_ref, scatter_ref, units_ref, departures):
    count, piece = scatter_ref.shape[0], units_ref.shape[1]
    part = count // PIECES
    for i, copy in enumerate(departures):
        block = jnp.concatenate(
            [
                rows_ref[i * part : (i + 1) * part, j * piece : (j + 1) * piece]
                for j in range(PIECES)
            ],
            axis=0,
        )
        units_ref[i * count : (i + 1) * count, :] = dot(scatter_ref[...], block, NN).astype(BF16)
        copy.start()


def forward_kernel(
    got_hbm, gather_ref, scatter_ref, w_hbm, units_hbm, hidden_ref, act_hbm, slope_hbm,
    proj_ref, down_ref, got_ref, rows_ref, outs_ref, units_ref, act_ref, slope_ref, sems,
):
    half = hidden_ref.shape[1] // 2
    piece = got_ref.shape[1]
    count = gather_ref.shape[0]
    blocks = got_ref.shape[0] // count
    arrivals = copies_of(blocks_of(got_hbm, count), blocks_of(got_ref, count), sems, 8)
    departures = copies_of(
        blocks_of(units_ref, count), blocks_of(units_hbm, count), sems, 8 + blocks
    )
    proj, down = weight_copies(w_hbm, proj_ref, down_ref, sems, half)
    kept = copies_of(sides_of(act_ref, half), sides_of(act_hbm, half), sems, 4)
    kept += copies_of(sides_of(slope_ref, half), sides_of(slope_hbm, half), sems, 6)
    started(arrivals + proj + down)
    to_rows(got_ref, gather_ref, rows_ref, arrivals)
    rows = rows_ref[...]
    for side in range(2):
        proj[side].wait()
        pre = dot(rows, proj_ref[side], NN)
        pre_gate, pre_up = pre[:, :half], pre[:, half:]
        sig = jax.nn.sigmoid(pre_gate)
        act = pre_gate * sig
        columns = slice(side * half, (side + 1) * half)
        hidden_ref[:, columns] = (act * pre_up).astype(BF16)
        act_ref[:, columns] = act
        slope_ref[:, columns] = pre_up * sig * (1.0 + pre_gate * (1.0 - sig))
        kept[side].start()
        kept[2 + side].start()
    finished(down)
    for j in range(PIECES):
        cols = slice(j * piece, (j + 1) * piece)
        out = dot(hidden_ref[:, :half], down_ref[0, cols, :], NT)
        out = out + dot(hidden_ref[:, half:], down_ref[1, cols, :], NT)
        outs_ref[:, cols] = out.astype(BF16)
    to_units(outs_ref, scatter_ref, units_ref, departures)
    finished(kept + departures)


def backward_kernel(
    got_hbm, act_hbm, slope_hbm, hidden_ref, q_ref, error_left_ref, gather_ref, scatter_ref, w_hbm,
    units_hbm, rows_hbm, left_ref,
    proj_ref, down_ref, got_ref, rows_ref, outs_ref, units_ref, act_ref, slope_ref, sems, grads_ref,
):
    half = act_ref.shape[1] // 2
    piece = units_ref.shape[1]
    count = gather_ref.shape[0]
    blocks = got_ref.shape[0] // count
    arrivals = copies_of(blocks_of(got_hbm, count), blocks_of(got_ref, count), sems, 8)
    departures = copies_of(
        blocks_of(units_ref, count), blocks_of(units_hbm, count), sems, 8 + blocks
    )
    proj, down = weight_copies(w_hbm, proj_ref, down_ref, sems, half)
    kept = copies_of(sides_of(act_hbm, half), sides_of(act_ref, half), sems, 4)
    kept += copies_of(sides_of(slope_hbm, half), sides_of(slope_ref, half), sems, 6)
    out_rows = copies_of([rows_ref], [rows_hbm], sems, 8 + 2 * blocks)
    started(arrivals + down + kept + proj)
    to_rows(got_ref, gather_ref, rows_ref, arrivals)
    started(out_rows)
    rows = rows_ref[...]
    grad_q = folded(dot(thirds(q_ref[...]), rows, NT))
    left = folded(dot(thirds(grad_q), hidden_ref[...], NN))
    left_ref[:, :half] = left[:, :half] + error_left_ref[...]
    left_ref[:, half:] = left[:, half:]
    for side in range(2):
        columns = slice(side * half, (side + 1) * half)
        down[side].wait()
        hidden_grad = dot(rows, down_ref[side], NN)
        kept[side].wait()
        kept[2 + side].wait()
        grads_ref[side, :, :half] = (hidden_grad * slope_ref[:, columns]).astype(BF16)
        grads_ref[side, :, half:] = (hidden_grad * act_ref[:, columns]).astype(BF16)
    finished(proj)
    for j in range(PIECES):
        cols = slice(j * piece, (j + 1) * piece)
        out = dot(grads_ref[0], proj_ref[0, cols, :], NT)
        out = out + dot(grads_ref[1], proj_ref[1, cols, :], NT)
        outs_ref[:, cols] = out.astype(BF16)
    to_units(outs_ref, scatter_ref, units_ref, departures)
    finished(departures + out_rows)


def basis_kernel(
    core_ref, left_ref, hidden_ref, rows_hbm, error_hbm, basis_ref, terms_ref, right_ref, away_ref,
    rows_ref, error_ref, sems,
):
    copies = copies_of([rows_hbm, error_hbm], [rows_ref, error_ref], sems, 0)
    started(copies)
    left = left_ref[...]
    rank = left.shape[0]
    half = left.shape[1] // 2
    gram = dot(left, left, NT, HIGHEST)
    row_ids = lax.broadcasted_iota(jnp.int32, (rank, rank), 0)
    inverse = jnp.where(
        row_ids == lax.broadcasted_iota(jnp.int32, (rank, rank), 1), 1.0, 0.0
    ).astype(F32)
    for k in range(rank):
        scale = 1.0 / jnp.sqrt(gram[k : k + 1, k : k + 1])
        gram_row = gram[k : k + 1, :] * scale
        inverse_row = inverse[k : k + 1, :] * scale
        below = jnp.where(row_ids > k, gram[:, k : k + 1] * scale, 0.0)
        gram = gram - below * gram_row
        inverse = jnp.where(row_ids == k, inverse_row, inverse - below * inverse_row)
    basis = dot(inverse, left, NN, HIGHEST)
    mine = basis[:, :half]
    basis_ref[...] = mine
    terms = thirds(mine)
    terms_ref[...] = jnp.concatenate(
        [terms[:rank], terms[:rank], terms[rank : 2 * rank], terms[rank : 2 * rank]], axis=0
    )
    finished(copies)
    hidden_basis = folded(dot(thirds(basis), hidden_ref[...], NT))
    right = folded(dot(terms, error_ref[...], NN))
    right = right + folded(dot(thirds(hidden_basis), rows_ref[...], NN))
    span = right_ref.shape[1]
    first = core_ref[0] == 0
    right_ref[...] = jnp.where(first, right[:, :span], right[:, span:])
    away_ref[...] = jnp.where(first, right[:, span:], right[:, :span])


def error_kernel(merged_ref, terms_ref, right_ref, fresh_ref):
    right = right_ref[...]
    rank = right.shape[0]
    parts = thirds(right)
    high, middle = parts[:rank], parts[rank : 2 * rank]
    approx = dot(terms_ref[...], jnp.concatenate([high, middle, high, middle], axis=0), TN)
    fresh_ref[...] = (merged_ref[...] - approx).astype(BF16)


def moved(value, mask):
    count = lax.axis_size("group") * lax.axis_size("half")
    return lax.ppermute(value, PLANE, [(source, source ^ mask) for source in range(count)])


def plane_sum(value, flip):
    near, far, both = moved(value, 2), moved(value, 4), moved(value, 6)
    value = (value + near) + (far + both)
    near, far, both = moved(value, 8), moved(value, 1), moved(value, 9)
    return (value + near) + flip(far + both)


def shards(tokens, target, routes, gates, w_gate, w_up, w_down, error, q_start):
    experts = lax.axis_size("expert")
    half = lax.axis_index("half")
    tok, width = tokens.shape
    top = routes.shape[1]
    hidden_half = w_gate.shape[1]
    inner = 2 * hidden_half
    capacity = max(2, min(tok, 2 * (5 * tok * top // (8 * experts))))
    piece = width // PIECES
    unit = PIECES * capacity
    slots = experts * capacity
    rank = 2 * q_start.shape[1]

    own = jnp.concatenate([w_gate, w_up, w_down.T], axis=1)
    packed = jnp.concatenate([own, moved(own, 1)], axis=1)

    expert_ids = jnp.arange(experts, dtype=jnp.int32)
    hits = (routes[:, :, None] == expert_ids).astype(jnp.int32)
    per_token = jnp.sum(hits, axis=1)
    earlier = jnp.cumsum(per_token, axis=0) - per_token
    position = jnp.sum(hits * earlier[:, None, :], axis=2)
    base = (routes * unit + position).T
    lanes = jnp.arange(experts * unit, dtype=jnp.int32)
    places = jnp.arange(PIECES, dtype=jnp.int32)[:, None, None] * capacity + base
    select = (places[..., None] == lanes).astype(BF16)
    spread = jnp.sum(select, axis=1).reshape(PIECES * tok, experts * unit)
    select = select.reshape(PIECES * top * tok, experts * unit)

    block = min(BLOCK, experts)
    order = (
        jnp.arange(PIECES, dtype=jnp.int32)[:, None, None] * capacity
        + jnp.arange(block, dtype=jnp.int32)[None, :, None] * unit
        + jnp.arange(capacity, dtype=jnp.int32)[None, None, :]
    ).reshape(block * unit)
    block_lanes = jnp.arange(block * unit, dtype=jnp.int32)
    gather = (order[:, None] == block_lanes).astype(BF16)
    scatter = (block_lanes[:, None] == order).astype(BF16)

    def pieces_of(rows):
        return jnp.concatenate(jnp.split(rows, PIECES, axis=-1), axis=0)

    def exchange(rows):
        sent = rows.reshape(experts, unit, piece)
        back = lax.all_to_all(sent, "expert", split_axis=0, concat_axis=0, tiled=True)
        return back.reshape(experts * unit, piece)

    send = dot(spread, pieces_of(tokens), TN).astype(BF16)
    packed, send = lax.optimization_barrier((packed, send))
    weights = lax.all_gather(packed, DP, axis=0, tiled=True)
    inbox = exchange(send)

    q_mine = q_start.T
    q_other = moved(q_mine, 1)
    q_full = jnp.concatenate(
        [jnp.where(half == 0, q_mine, q_other), jnp.where(half == 0, q_other, q_mine)], axis=0
    )
    error_left = dot(q_full, error.astype(F32), NT, HIGHEST)
    inbox, q_full, error_left = lax.optimization_barrier((inbox, q_full, error_left))

    unit_shape, row_shape = (experts * unit, piece), (slots, width)
    blocks = experts // block
    scratch = [
        pltpu.VMEM((2, width, inner), BF16),
        pltpu.VMEM((2, width, hidden_half), BF16),
        pltpu.VMEM(unit_shape, BF16),
        pltpu.VMEM(row_shape, BF16),
        pltpu.VMEM(row_shape, BF16),
        pltpu.VMEM(unit_shape, BF16),
        pltpu.VMEM((slots, inner), F32),
        pltpu.VMEM((slots, inner), F32),
        pltpu.SemaphoreType.DMA((9 + 2 * blocks,)),
    ]
    returned, hidden, act, act_slope = local_call(
        forward_kernel,
        [(unit_shape, BF16), ((slots, inner), BF16), ((slots, inner), F32), ((slots, inner), F32)],
        scratch,
        inbox, gather, scatter, weights, hbm=(0, 3), out_hbm=(0, 2, 3), memory=58,
    )
    returned = exchange(returned)
    picked = dot(select, returned, NN).reshape(PIECES, top, tok, piece)
    gate = gates.T[None, :, :, None]
    layer_sum = jnp.sum(gate * picked, axis=1)
    slope = layer_sum - pieces_of(target).reshape(PIECES, tok, piece).astype(F32)
    out_grad = (gate * slope[:, None]).astype(BF16).reshape(PIECES * top * tok, piece)
    grad_got = exchange(dot(select, out_grad, TN).astype(BF16))
    hidden_other = moved(hidden[:, hidden_half:], 1)
    grad_got, hidden_other = lax.optimization_barrier((grad_got, hidden_other))

    token_part, rows, left = local_call(
        backward_kernel,
        [(unit_shape, BF16), (row_shape, BF16), ((rank, inner), F32)],
        scratch + [pltpu.VMEM((2, slots, inner), BF16)],
        grad_got, act, act_slope, hidden, q_full, error_left, gather, scatter, weights,
        hbm=(0, 1, 2, 8), out_hbm=(0, 1), memory=58,
    )
    slot_grad = exchange(token_part)
    token_grad = dot(spread, slot_grad, NN).astype(BF16)
    token_grad = jnp.concatenate(jnp.split(token_grad, PIECES, axis=0), axis=1)

    def flip(value):
        return jnp.concatenate([value[:, hidden_half:], value[:, :hidden_half]], axis=1)

    left = jnp.sum(lax.all_gather(left, "core"), axis=0)
    left, sent_rows = lax.optimization_barrier((left, rows))
    rows_other = moved(sent_rows, 1)
    left, rows_other = lax.optimization_barrier((plane_sum(left, flip), rows_other))
    core = lax.axis_index("core")
    span = width // lax.axis_size("core")
    basis, terms, right, right_away = local_call(
        basis_kernel,
        [
            ((rank, hidden_half), F32),
            ((4 * rank, hidden_half), BF16),
            ((rank, span), F32),
            ((rank, span), F32),
        ],
        [
            pltpu.VMEM(row_shape, BF16),
            pltpu.VMEM((hidden_half, width), BF16),
            pltpu.SemaphoreType.DMA((2,)),
        ],
        core.reshape(1), left, hidden, rows, error, hbm=(3, 4), smem=(0,),
    )
    merged = (
        dot(hidden[:, :hidden_half], rows, TN)
        + dot(hidden_other, rows_other, TN)
        + error.astype(F32)
    )
    right = right + lax.ppermute(right_away, "core", [(0, 1), (1, 0)])
    right = plane_sum(right, lambda value: value) / (lax.axis_size("group") * lax.axis_size("core"))
    right = lax.all_gather(right, "core", axis=1, tiled=True)
    (new_error,) = local_call(
        error_kernel, [((hidden_half, width), BF16)], [], merged, terms, right
    )
    q_columns = jnp.where(half == 0, right[: rank // 2], right[rank // 2 :])
    replicas = lax.axis_size("group") * lax.axis_size("core")
    replica = lax.axis_index("group") * lax.axis_size("core") + lax.axis_index("core")
    q_rows = width // replicas
    q_factor = lax.dynamic_slice_in_dim(q_columns, replica * q_rows, q_rows, 1).T
    return token_grad, basis.T, q_factor, new_error


def solution(mesh):
    replicas, places = mesh.shape["dp"], mesh.shape["expert"]
    split = Mesh(
        mesh.devices.reshape(replicas // 2, 2, places // 2, 2),
        ("group", "core", "expert", "half"),
    )
    pair = ("expert", "half")
    rows = P(DP + pair, None)
    in_specs = (rows, rows, rows, rows, P(DP, pair), P(DP, pair), P(pair, DP), rows, P(None, pair))
    out_specs = (rows, P(pair, None), P(DP, pair), rows)
    return jax.shard_map(shards, mesh=split, in_specs=in_specs, out_specs=out_specs, check_vma=False)
```

time: 406 us -> 373 us (0.919)
  blocking collectives: 74.4 us -> 8.08 us
  starting transfers between devices: 84.4 us -> 113 us
  matrix products: 35.5 us -> 12.1 us
  Pallas kernels: 5.06 us -> 27.5 us
  waiting for transfers between devices: 159 us -> 180 us
  local copies, waits for them, and re-layouts: 23.8 us -> 4.48 us
    all_to_all x1 -> x0, blocking collectives: 74.4 us -> none  [exchange(): lax.all_to_all(sent, 'expert', split_axis=0, concat_axis=0, tiled=True)]
    all_to_all x3 -> x4, waiting for transfers between devices: 104 us -> 152 us  [exchange(): lax.all_to_all(sent, 'expert', split_axis=0, concat_axis=0, tiled=True)]
    dot_general x17 -> x7, matrix products: 35.5 us -> 12.1 us  [dot(): lax.dot_general(left, right, (dims, ((), ())), precision=precision, prefe...]
    ppermute x14 -> x17, waiting for transfers between devices: 51.8 us -> 28.6 us  [the longest x16 27.3 us: moved(): lax.ppermute(value, PLANE, [(source, source ^ mask) for source in range(c...]
    pallas_call x1 -> x4, Pallas kernels: 5.06 us -> 27.5 us  [local_call(): pl.pallas_call(kernel, out_shape=[jax.ShapeDtypeStruct(shape, dtype) for...]
    all_to_all x3 -> x4, starting transfers between devices: 35.1 us -> 53.3 us  [exchange(): lax.all_to_all(sent, 'expert', split_axis=0, concat_axis=0, tiled=True)]
    ppermute x14 -> x17, starting transfers between devices: 49.2 us -> 60.2 us  [the longest x16 57.8 us: moved(): lax.ppermute(value, PLANE, [(source, source ^ mask) for source in range(c...]
    reshape x4 -> x0, local copies, waits for them, and re-layouts: 8.12 us -> none  [units_of(): parts = rows.reshape(experts, capacity, PIECES, piece)]
  transfers between devices with their start and end apart: 18 -> 22, of which waited for: 14 -> 13; matrix products, arithmetic and copies ran while one was open for 6% -> 4% of each run, Pallas kernels for 1% -> 2%
where the time goes in v2:
time: 373 us; the launch traced here: 372 us
  waiting for transfers between devices  180 us (48%)
  starting transfers between devices  113 us (30%)
  Pallas kernels  27.5 us (7%)
  between operations  14.6 us (4%)
  matrix products  12.1 us (3%)
  other arithmetic  11.4 us (3%)
  blocking collectives  8.08 us (2%)
  local copies, waits for them, and re-layouts  4.48 us (1%)
    all_to_all x4, waiting for transfers between devices, exchange(): lax.all_to_all(sent, 'expert', split_axis=0, concat_axis=0, tiled=True)  152 us
    ppermute x16, starting transfers between devices, moved(): lax.ppermute(value, PLANE, [(source, source ^ mask) for source in range(c...  57.8 us
    all_to_all x4, starting transfers between devices, exchange(): lax.all_to_all(sent, 'expert', split_axis=0, concat_axis=0, tiled=True)  53.3 us
    pallas_call x4, Pallas kernels, local_call(): pl.pallas_call(kernel, out_shape=[jax.ShapeDtypeStruct(shape, dtype) for...  27.5 us
    ppermute x16, waiting for transfers between devices, moved(): lax.ppermute(value, PLANE, [(source, source ^ mask) for source in range(c...  27.3 us
    dot_general x7, matrix products, dot(): lax.dot_general(left, right, (dims, ((), ())), precision=precision, prefe...  12.1 us
  transfers between devices with their start and end apart: 22, of which 13 were waited for; matrix products, arithmetic and copies ran while one was open for 4% of the time, Pallas kernels for 2%

profile of v2, /device:TPU:1, one launch (start us, length us, event | category | flops | bytes accessed | tf_op | source)
XLA Modules:
  0.0 371.9 jit_solution(2926510319019023992)
XLA Ops:
  7.2 1.1 copy.26
  9.3 5.7 %collective-permute-start = (bf16[128,1152]{1,0:T(8,128)(2,1)S(1)}, bf16[128,1152]{1,0:T(8,128)(2,1)S(1)}, u32[]{:S(2)}, u32[]{:S(2)}) collective-permute-start(bf16[128,1152]{1,0:T(8,128)(2,1)S(1)} %pad_maximum_fusion.3), channel_id=1, source_target_pairs={{0,1},{1,0},{64,65},{65,64},{128,129},{129,128},{192,193},{193,192... | collective-permute-start | bytes 884744 | tf_op jit(solution)/shard_map/ppermute | solution.py:251
  17.9 1.6 convolution_convert_fusion
  20.4 17.0 %all-to-all-start = ((bf16[16,40,1024]{2,1,0:T(8,128)(2,1)}), bf16[16,40,1024]{2,1,0:T(8,128)(2,1)S(1)}, u32[]{:S(2)}, u32[]{:S(2)}) async-start(bf16[16,40,1024]{2,1,0:T(8,128)(2,1)} %bitcast.5), calls=%async_computation | async-start | bytes 2621440 | tf_op jit(solution)/shard_map/all_to_all | solution.py:304
  37.4 4.8 %collective-permute-start.1 = (f32[16,2048]{1,0:T(8,128)S(1)}, f32[16,2048]{1,0:T(8,128)S(1)}, u32[]{:S(2)}, u32[]{:S(2)}) collective-permute-start(f32[16,2048]{1,0:T(8,128)S(1)} %bitcast.54), channel_id=1, source_target_pairs={{0,1},{1,0},{64,65},{65,64},{128,129},{129,128},{192,193},{193,192... | collective-permute-start | bytes 393224 | tf_op jit(solution)/shard_map/ppermute | solution.py:251
  43.2 1.4 collective-permute-done.1
  45.3 2.1 fusion.17.error_left_ref
  47.4 47.2 %all-to-all-done = bf16[16,40,1024]{2,1,0:T(8,128)(2,1)S(1)} async-done(((bf16[16,40,1024]{2,1,0:T(8,128)(2,1)}), bf16[16,40,1024]{2,1,0:T(8,128)(2,1)S(1)}, u32[]{:S(2)}, u32[]{:S(2)}) %all-to-all-start) | async-done | bytes 1310752 | tf_op jit(solution)/shard_map/all_to_all | solution.py:304
  94.6 1.1 copy-done.6
  95.7 9.9 %shard_map.120 = (bf16[640,1024]{1,0:T(8,128)(2,1)}, bf16[320,768]{1,0:T(8,128)(2,1)}, f32[320,768]{1,0:T(8,128)}, f32[320,768]{1,0:T(8,128)}) custom-call(bf16[640,1024]{1,0:T(8,128)(2,1)} %bitcast.42, bf16[160,160]{1,0:T(8,128)(2,1)} %get-tuple-element.61.gather_ref, bf16[160,160]{1,0:T(8,128)(2,1)} %get-tuple-element.60.scatter_ref, ...), custom_call_target="tpu_custom_call" | custom-call | tf_op jit(solution)/shard_map/pallas_call | solution.py:45
  105.6 12.2 %all-to-all-start.1 = ((bf16[16,40,1024]{2,1,0:T(8,128)(2,1)}), bf16[16,40,1024]{2,1,0:T(8,128)(2,1)S(1)}, u32[]{:S(2)}, u32[]{:S(2)}) async-start(bf16[16,40,1024]{2,1,0:T(8,128)(2,1)} %bitcast.48), calls=%async_computation.1 | async-start | bytes 2621440 | tf_op jit(solution)/shard_map/all_to_all | solution.py:304
  117.9 57.2 %all-to-all-done.1 = bf16[16,40,1024]{2,1,0:T(8,128)(2,1)S(1)} async-done(((bf16[16,40,1024]{2,1,0:T(8,128)(2,1)}), bf16[16,40,1024]{2,1,0:T(8,128)(2,1)S(1)}, u32[]{:S(2)}, u32[]{:S(2)}) %all-to-all-start.1) | async-done | bytes 1310752 | tf_op jit(solution)/shard_map/all_to_all | solution.py:304
  175.1 1.0 multiply_reduce_fusion
  176.3 2.0 bitcast_convert_fusion
  178.3 12.0 %all-to-all-start.2 = ((bf16[16,40,1024]{2,1,0:T(8,128)(2,1)}), bf16[16,40,1024]{2,1,0:T(8,128)(2,1)S(1)}, u32[]{:S(2)}, u32[]{:S(2)}) async-start(bf16[16,40,1024]{2,1,0:T(8,128)(2,1)} %bitcast.50), calls=%async_computation.2 | async-start | bytes 2621440 | tf_op jit(solution)/shard_map/all_to_all | solution.py:304
  190.4 5.0 %collective-permute-start.2 = (bf16[320,384]{1,0:T(8,128)(2,1)S(1)}, bf16[320,384]{1,0:T(8,128)(2,1)}, u32[]{:S(2)}, u32[]{:S(2)}) collective-permute-start(bf16[320,384]{1,0:T(8,128)(2,1)S(1)} %slice.18), channel_id=1, source_target_pairs={{0,1},{1,0},{64,65},{65,64},{128,129},{129,128},{192,193},{193,192... | collective-permute-start | bytes 737288 | tf_op jit(solution)/shard_map/ppermute | solution.py:251
  195.4 5.2 %collective-permute-done.2 = bf16[320,384]{1,0:T(8,128)(2,1)} collective-permute-done((bf16[320,384]{1,0:T(8,128)(2,1)S(1)}, bf16[320,384]{1,0:T(8,128)(2,1)}, u32[]{:S(2)}, u32[]{:S(2)}) %collective-permute-start.2) | collective-permute-done | bytes 245792 | tf_op jit(solution)/shard_map/ppermute | solution.py:251
  200.6 47.1 %all-to-all-done.2 = bf16[16,40,1024]{2,1,0:T(8,128)(2,1)S(1)} async-done(((bf16[16,40,1024]{2,1,0:T(8,128)(2,1)}), bf16[16,40,1024]{2,1,0:T(8,128)(2,1)S(1)}, u32[]{:S(2)}, u32[]{:S(2)}) %all-to-all-start.2) | async-done | bytes 1310752 | tf_op jit(solution)/shard_map/all_to_all | solution.py:304
  247.7 1.1 copy-done.7
  248.8 10.6 %shard_map.121 = (bf16[640,1024]{1,0:T(8,128)(2,1)}, bf16[320,2048]{1,0:T(8,128)(2,1)}, f32[32,768]{1,0:T(8,128)}) custom-call(bf16[640,1024]{1,0:T(8,128)(2,1)} %bitcast.43, f32[320,768]{1,0:T(8,128)} %get-tuple-element.32.act_hbm, f32[320,768]{1,0:T(8,128)} %get-tuple-element.33.slope_hbm, bf16[320,768]{1,0:T(8,128)(2,1)} %get-tuple-element.30.hidden_ref, ...), custom_call_target="tpu_custom_call" | custom-call | tf_op jit(solution)/shard_map/pallas_call | solution.py:45
  259.5 12.1 %all-to-all-start.3 = ((bf16[16,40,1024]{2,1,0:T(8,128)(2,1)}), bf16[16,40,1024]{2,1,0:T(8,128)(2,1)}, u32[]{:S(2)}, u32[]{:S(2)}) async-start(bf16[16,40,1024]{2,1,0:T(8,128)(2,1)} %bitcast.47), calls=%async_computation.3 | async-start | bytes 2621440 | tf_op jit(solution)/shard_map/all_to_all | solution.py:304
  271.6 2.6 all-gather
  275.2 4.8 %collective-permute-start.9 = (bf16[320,2048]{1,0:T(8,128)(2,1)S(1)}, bf16[320,2048]{1,0:T(8,128)(2,1)}, u32[]{:S(2)}, u32[]{:S(2)}) collective-permute-start(bf16[320,2048]{1,0:T(8,128)(2,1)S(1)} %copy-done.1), channel_id=1, source_target_pairs={{0,1},{1,0},{64,65},{65,64},{128,129},{129,128},{192,193},{193,192... | collective-permute-start | bytes 3932168 | tf_op jit(solution)/shard_map/ppermute | solution.py:251
  280.1 3.1 collective-permute-start.3
  283.2 4.4 %collective-permute-start.4 = (f32[32,768]{1,0:T(8,128)S(1)}, f32[32,768]{1,0:T(8,128)S(1)}, u32[]{:S(2)}, u32[]{:S(2)}) collective-permute-start(f32[32,768]{1,0:T(8,128)S(1)} %reduce_sum.52), channel_id=1, source_target_pairs={{0,128},{1,129},{64,192},{65,193},{128,0},{129,1},{192,64},{193,65... | collective-permute-start | bytes 294920 | tf_op jit(solution)/shard_map/ppermute | solution.py:251
  287.5 2.1 collective-permute-start.5
  290.5 4.1 %collective-permute-done.5 = f32[32,768]{1,0:T(8,128)S(1)} collective-permute-done((f32[32,768]{1,0:T(8,128)S(1)}, f32[32,768]{1,0:T(8,128)S(1)}, u32[]{:S(2)}, u32[]{:S(2)}) %collective-permute-start.5) | collective-permute-done | bytes 98336 | tf_op jit(solution)/shard_map/ppermute | solution.py:251
  295.4 2.0 collective-permute-start.7
  297.4 4.7 %collective-permute-start.8 = (f32[32,768]{1,0:T(8,128)S(1)}, f32[32,768]{1,0:T(8,128)}, u32[]{:S(2)}, u32[]{:S(2)}) collective-permute-start(f32[32,768]{1,0:T(8,128)S(1)} %add_add_fusion.1), channel_id=1, source_target_pairs={{0,257},{1,256},{64,321},{65,320},{128,385},{129,384},{192,449},{1... | collective-permute-start | bytes 294920 | tf_op jit(solution)/shard_map/ppermute | solution.py:251
  302.1 1.9 collective-permute-start.6
  304.0 6.9 %collective-permute-done.7 = f32[32,768]{1,0:T(8,128)} collective-permute-done((f32[32,768]{1,0:T(8,128)S(1)}, f32[32,768]{1,0:T(8,128)}, u32[]{:S(2)}, u32[]{:S(2)}) %collective-permute-start.7) | collective-permute-done | bytes 98336 | tf_op jit(solution)/shard_map/ppermute | solution.py:251
  310.9 2.8 collective-permute-done.8
  314.7 5.2 %shard_map.122 = (f32[32,384]{1,0:T(8,128)}, bf16[128,384]{1,0:T(8,128)(2,1)S(1)}, f32[32,1024]{1,0:T(8,128)S(1)}, f32[32,1024]{1,0:T(8,128)}) custom-call(s32[1]{0:T(128)} %bitcast.19.core_ref, f32[32,768]{1,0:T(8,128)S(1)} %maximum_add_fusion.left_ref, bf16[320,768]{1,0:T(8,128)(2,1)S(1)} %copy-done.3, bf16[320,2048]{1,0:T(8,128)(2,1)S(1)} %copy-done.1, ...), custom_call_target="tpu_custom_call" | custom-call | tf_op jit(solution)/shard_map/pallas_call | solution.py:45
  320.5 2.4 collective-permute-start.10
  322.9 1.3 collective-permute-done.10
  325.1 3.1 collective-permute-start.11
  328.3 4.4 %collective-permute-start.12 = (f32[32,1024]{1,0:T(8,128)S(1)}, f32[32,1024]{1,0:T(8,128)S(1)}, u32[]{:S(2)}, u32[]{:S(2)}) collective-permute-start(f32[32,1024]{1,0:T(8,128)S(1)} %add.172), channel_id=1, source_target_pairs={{0,128},{1,129},{64,192},{65,193},{128,0},{129,1},{192,64},{193,65... | collective-permute-start | bytes 393224 | tf_op jit(solution)/shard_map/ppermute | solution.py:251
  332.6 2.1 collective-permute-start.13
  335.8 1.0 collective-permute-done.12
  336.8 2.7 collective-permute-done.13
  339.6 3.4 collective-permute-start.14
  343.0 4.5 %collective-permute-start.15 = (f32[32,1024]{1,0:T(8,128)S(1)}, f32[32,1024]{1,0:T(8,128)S(1)}, u32[]{:S(2)}, u32[]{:S(2)}) collective-permute-start(f32[32,1024]{1,0:T(8,128)S(1)} %add_add_fusion), channel_id=1, source_target_pairs={{0,1},{1,0},{64,65},{65,64},{128,129},{129,128},{192,193},{193,192... | collective-permute-start | bytes 393224 | tf_op jit(solution)/shard_map/ppermute | solution.py:251
  347.5 1.9 collective-permute-start.16
  349.4 2.5 convert_add_fusion.merged_ref
  352.0 2.4 collective-permute-done.16
  354.4 5.4 %all_gather.15.right_ref = f32[32,2048]{1,0:T(8,128)S(1)} all-gather(f32[32,1024]{1,0:T(8,128)S(1)} %add_multiply_fusion), channel_id=1, replica_groups=mesh['group'=8,'core'=2,'expert'=16,'half'=2] {'core'}, dimensions={1}, use_global_device_ids=true | all-gather | bytes 393216 | tf_op jit(solution)/shard_map/all_gather | solution.py:391
  359.9 1.7 shard_map.123
  362.3 1.9 convolution_convert_fusion.1
  (84 shorter events, 14.6 us)
Async XLA Ops:
  7.2 10.2 %copy-start.10 = (bf16[128,2048]{1,0:T(8,128)(2,1)S(1)}, bf16[128,2048]{1,0:T(8,128)(2,1)}, u32[]{:S(2)}) copy-start(bf16[128,2048]{1,0:T(8,128)(2,1)} %param.9) | copy-start | bytes 1572868
  7.2 87.4 %all-gather.3.cloned.1.call-start = ((), (), s32[]{:S(2)}) async-start(), calls=%async_computation.4 | async-start | bytes 10027008 | tf_op jit(solution)/shard_map/all_gather | solution.py:309
  9.3 10.2 %collective-permute-start = (bf16[128,1152]{1,0:T(8,128)(2,1)S(1)}, bf16[128,1152]{1,0:T(8,128)(2,1)S(1)}, u32[]{:S(2)}, u32[]{:S(2)}) collective-permute-start(bf16[128,1152]{1,0:T(8,128)(2,1)S(1)} %pad_maximum_fusion.3), channel_id=1, source_target_pairs={{0,1},{1,0},{64,65},{65,64},{128,129},{129,128},{192,193},{193,192... | collective-permute-start | bytes 884744 | tf_op jit(solution)/shard_map/ppermute | solution.py:251
  17.6 1.8 copy-start.12
  17.6 1.8 copy-start.13
  17.9 2.5 copy-start.8
  20.4 17.0 %copy-start.15 = (f32[2048,16]{0,1:T(8,128)S(1)}, f32[2048,16]{0,1:T(8,128)}, u32[]{:S(2)}) copy-start(f32[2048,16]{0,1:T(8,128)} %param.17) | copy-start | bytes 393220
  20.4 25.0 %copy-start = (bf16[384,2048]{1,0:T(8,128)(2,1)S(1)}, bf16[384,2048]{1,0:T(8,128)(2,1)}, u32[]{:S(2)}) copy-start(bf16[384,2048]{1,0:T(8,128)(2,1)} %error_hbm.1) | copy-start | bytes 4718596
  20.4 74.2 %all-to-all-start = ((bf16[16,40,1024]{2,1,0:T(8,128)(2,1)}), bf16[16,40,1024]{2,1,0:T(8,128)(2,1)S(1)}, u32[]{:S(2)}, u32[]{:S(2)}) async-start(bf16[16,40,1024]{2,1,0:T(8,128)(2,1)} %bitcast.5), calls=%async_computation | async-start | bytes 2621440 | tf_op jit(solution)/shard_map/all_to_all | solution.py:304
  37.4 7.2 %collective-permute-start.1 = (f32[16,2048]{1,0:T(8,128)S(1)}, f32[16,2048]{1,0:T(8,128)S(1)}, u32[]{:S(2)}, u32[]{:S(2)}) collective-permute-start(f32[16,2048]{1,0:T(8,128)S(1)} %bitcast.54), channel_id=1, source_target_pairs={{0,1},{1,0},{64,65},{65,64},{128,129},{129,128},{192,193},{193,192... | collective-permute-start | bytes 393224 | tf_op jit(solution)/shard_map/ppermute | solution.py:251
  94.6 1.1 copy-start.6
  105.6 12.2 %copy-start.11 = (bf16[128,2048]{1,0:T(8,128)(2,1)S(1)}, bf16[128,2048]{1,0:T(8,128)(2,1)}, u32[]{:S(2)}) copy-start(bf16[128,2048]{1,0:T(8,128)(2,1)} %param.10) | copy-start | bytes 1572868
  105.6 69.5 %all-to-all-start.1 = ((bf16[16,40,1024]{2,1,0:T(8,128)(2,1)}), bf16[16,40,1024]{2,1,0:T(8,128)(2,1)S(1)}, u32[]{:S(2)}, u32[]{:S(2)}) async-start(bf16[16,40,1024]{2,1,0:T(8,128)(2,1)} %bitcast.48), calls=%async_computation.1 | async-start | bytes 2621440 | tf_op jit(solution)/shard_map/all_to_all | solution.py:304
  117.8 57.4 %copy-start.17 = (f32[128,2]{0,1:T(2,128)S(1)}, f32[128,2]{0,1:T(2,128)}, u32[]{:S(2)}) copy-start(f32[128,2]{0,1:T(2,128)} %param.12) | copy-start | bytes 3076
  178.3 12.1 %copy-start.2 = (bf16[320,768]{1,0:T(8,128)(2,1)S(1)}, bf16[320,768]{1,0:T(8,128)(2,1)}, u32[]{:S(2)}) copy-start(bf16[320,768]{1,0:T(8,128)(2,1)} %get-tuple-element.30.hidden_ref) | copy-start | bytes 1474564
  178.3 69.4 %all-to-all-start.2 = ((bf16[16,40,1024]{2,1,0:T(8,128)(2,1)}), bf16[16,40,1024]{2,1,0:T(8,128)(2,1)S(1)}, u32[]{:S(2)}, u32[]{:S(2)}) async-start(bf16[16,40,1024]{2,1,0:T(8,128)(2,1)} %bitcast.50), calls=%async_computation.2 | async-start | bytes 2621440 | tf_op jit(solution)/shard_map/all_to_all | solution.py:304
  190.4 10.2 %collective-permute-start.2 = (bf16[320,384]{1,0:T(8,128)(2,1)S(1)}, bf16[320,384]{1,0:T(8,128)(2,1)}, u32[]{:S(2)}, u32[]{:S(2)}) collective-permute-start(bf16[320,384]{1,0:T(8,128)(2,1)S(1)} %slice.18), channel_id=1, source_target_pairs={{0,1},{1,0},{64,65},{65,64},{128,129},{129,128},{192,193},{193,192... | collective-permute-start | bytes 737288 | tf_op jit(solution)/shard_map/ppermute | solution.py:251
  247.7 1.1 copy-start.7
  259.5 12.2 %copy-start.16 = (f32[32,768]{1,0:T(8,128)S(1)}, f32[32,768]{1,0:T(8,128)}, u32[]{:S(2)}) copy-start(f32[32,768]{1,0:T(8,128)} %get-tuple-element.37) | copy-start | bytes 294916
  259.5 15.8 %copy-start.1 = (bf16[320,2048]{1,0:T(8,128)(2,1)S(1)}, bf16[320,2048]{1,0:T(8,128)(2,1)}, u32[]{:S(2)}) copy-start(bf16[320,2048]{1,0:T(8,128)(2,1)} %get-tuple-element.40.rows_hbm) | copy-start | bytes 3932164
  259.5 102.8 %all-to-all-start.3 = ((bf16[16,40,1024]{2,1,0:T(8,128)(2,1)}), bf16[16,40,1024]{2,1,0:T(8,128)(2,1)}, u32[]{:S(2)}, u32[]{:S(2)}) async-start(bf16[16,40,1024]{2,1,0:T(8,128)(2,1)} %bitcast.47), calls=%async_computation.3 | async-start | bytes 2621440 | tf_op jit(solution)/shard_map/all_to_all | solution.py:304
  271.6 43.1 %copy-start.3 = (bf16[320,768]{1,0:T(8,128)(2,1)S(1)}, bf16[320,768]{1,0:T(8,128)(2,1)}, u32[]{:S(2)}) copy-start(bf16[320,768]{1,0:T(8,128)(2,1)} %get-tuple-element.30.hidden_ref) | copy-start | bytes 1474564
  275.2 15.2 %copy-start.14 = (f32[32,768]{1,0:T(8,128)}, f32[32,768]{1,0:T(8,128)S(1)}, u32[]{:S(2)}) copy-start(f32[32,768]{1,0:T(8,128)S(1)} %reduce_sum.52) | copy-start | bytes 294916
  275.2 39.4 %collective-permute-start.9 = (bf16[320,2048]{1,0:T(8,128)(2,1)S(1)}, bf16[320,2048]{1,0:T(8,128)(2,1)}, u32[]{:S(2)}, u32[]{:S(2)}) collective-permute-start(bf16[320,2048]{1,0:T(8,128)(2,1)S(1)} %copy-done.1), channel_id=1, source_target_pairs={{0,1},{1,0},{64,65},{65,64},{128,129},{129,128},{192,193},{193,192... | collective-permute-start | bytes 3932168 | tf_op jit(solution)/shard_map/ppermute | solution.py:251
  280.1 9.6 %collective-permute-start.3 = (f32[32,768]{1,0:T(8,128)S(1)}, f32[32,768]{1,0:T(8,128)S(1)}, u32[]{:S(2)}, u32[]{:S(2)}) collective-permute-start(f32[32,768]{1,0:T(8,128)S(1)} %reduce_sum.52), channel_id=1, source_target_pairs={{0,64},{1,65},{64,0},{65,1},{128,192},{129,193},{192,128},{193,129... | collective-permute-start | bytes 294920 | tf_op jit(solution)/shard_map/ppermute | solution.py:251
  283.2 7.3 %collective-permute-start.4 = (f32[32,768]{1,0:T(8,128)S(1)}, f32[32,768]{1,0:T(8,128)S(1)}, u32[]{:S(2)}, u32[]{:S(2)}) collective-permute-start(f32[32,768]{1,0:T(8,128)S(1)} %reduce_sum.52), channel_id=1, source_target_pairs={{0,128},{1,129},{64,192},{65,193},{128,0},{129,1},{192,64},{193,65... | collective-permute-start | bytes 294920 | tf_op jit(solution)/shard_map/ppermute | solution.py:251
  287.5 7.0 %collective-permute-start.5 = (f32[32,768]{1,0:T(8,128)S(1)}, f32[32,768]{1,0:T(8,128)S(1)}, u32[]{:S(2)}, u32[]{:S(2)}) collective-permute-start(f32[32,768]{1,0:T(8,128)S(1)} %reduce_sum.52), channel_id=1, source_target_pairs={{0,192},{1,193},{64,128},{65,129},{128,64},{129,65},{192,0},{193,1... | collective-permute-start | bytes 294920 | tf_op jit(solution)/shard_map/ppermute | solution.py:251
  295.4 15.4 %collective-permute-start.7 = (f32[32,768]{1,0:T(8,128)S(1)}, f32[32,768]{1,0:T(8,128)}, u32[]{:S(2)}, u32[]{:S(2)}) collective-permute-start(f32[32,768]{1,0:T(8,128)S(1)} %add_add_fusion.1), channel_id=1, source_target_pairs={{0,1},{1,0},{64,65},{65,64},{128,129},{129,128},{192,193},{193,192... | collective-permute-start | bytes 294920 | tf_op jit(solution)/shard_map/ppermute | solution.py:251
  297.4 16.2 %collective-permute-start.8 = (f32[32,768]{1,0:T(8,128)S(1)}, f32[32,768]{1,0:T(8,128)}, u32[]{:S(2)}, u32[]{:S(2)}) collective-permute-start(f32[32,768]{1,0:T(8,128)S(1)} %add_add_fusion.1), channel_id=1, source_target_pairs={{0,257},{1,256},{64,321},{65,320},{128,385},{129,384},{192,449},{1... | collective-permute-start | bytes 294920 | tf_op jit(solution)/shard_map/ppermute | solution.py:251
  302.1 12.5 %collective-permute-start.6 = (f32[32,768]{1,0:T(8,128)S(1)}, f32[32,768]{1,0:T(8,128)S(1)}, u32[]{:S(2)}, u32[]{:S(2)}) collective-permute-start(f32[32,768]{1,0:T(8,128)S(1)} %add_add_fusion.1), channel_id=1, source_target_pairs={{0,256},{1,257},{64,320},{65,321},{128,384},{129,385},{192,448},{1... | collective-permute-start | bytes 294920 | tf_op jit(solution)/shard_map/ppermute | solution.py:251
  319.9 0.6 copy-start.4
  320.5 3.7 collective-permute-start.10
  325.1 10.6 %collective-permute-start.11 = (f32[32,1024]{1,0:T(8,128)S(1)}, f32[32,1024]{1,0:T(8,128)S(1)}, u32[]{:S(2)}, u32[]{:S(2)}) collective-permute-start(f32[32,1024]{1,0:T(8,128)S(1)} %add.172), channel_id=1, source_target_pairs={{0,64},{1,65},{64,0},{65,1},{128,192},{129,193},{192,128},{193,129... | collective-permute-start | bytes 393224 | tf_op jit(solution)/shard_map/ppermute | solution.py:251
  328.3 8.6 %collective-permute-start.12 = (f32[32,1024]{1,0:T(8,128)S(1)}, f32[32,1024]{1,0:T(8,128)S(1)}, u32[]{:S(2)}, u32[]{:S(2)}) collective-permute-start(f32[32,1024]{1,0:T(8,128)S(1)} %add.172), channel_id=1, source_target_pairs={{0,128},{1,129},{64,192},{65,193},{128,0},{129,1},{192,64},{193,65... | collective-permute-start | bytes 393224 | tf_op jit(solution)/shard_map/ppermute | solution.py:251
  332.6 6.9 %collective-permute-start.13 = (f32[32,1024]{1,0:T(8,128)S(1)}, f32[32,1024]{1,0:T(8,128)S(1)}, u32[]{:S(2)}, u32[]{:S(2)}) collective-permute-start(f32[32,1024]{1,0:T(8,128)S(1)} %add.172), channel_id=1, source_target_pairs={{0,192},{1,193},{64,128},{65,129},{128,64},{129,65},{192,0},{193,1... | collective-permute-start | bytes 393224 | tf_op jit(solution)/shard_map/ppermute | solution.py:251
  339.6 20.3 %copy-start.5 = (bf16[128,384]{1,0:T(8,128)(2,1)S(1)}, bf16[128,384]{1,0:T(8,128)(2,1)}, u32[]{:S(2)}) copy-start(bf16[128,384]{1,0:T(8,128)(2,1)} %copy-done.4) | copy-start | bytes 294916
  339.6 12.4 %collective-permute-start.14 = (f32[32,1024]{1,0:T(8,128)S(1)}, f32[32,1024]{1,0:T(8,128)S(1)}, u32[]{:S(2)}, u32[]{:S(2)}) collective-permute-start(f32[32,1024]{1,0:T(8,128)S(1)} %add_add_fusion), channel_id=1, source_target_pairs={{0,256},{1,257},{64,320},{65,321},{128,384},{129,385},{192,448},{1... | collective-permute-start | bytes 393224 | tf_op jit(solution)/shard_map/ppermute | solution.py:251
  343.0 9.0 %collective-permute-start.15 = (f32[32,1024]{1,0:T(8,128)S(1)}, f32[32,1024]{1,0:T(8,128)S(1)}, u32[]{:S(2)}, u32[]{:S(2)}) collective-permute-start(f32[32,1024]{1,0:T(8,128)S(1)} %add_add_fusion), channel_id=1, source_target_pairs={{0,1},{1,0},{64,65},{65,64},{128,129},{129,128},{192,193},{193,192... | collective-permute-start | bytes 393224 | tf_op jit(solution)/shard_map/ppermute | solution.py:251
  347.5 6.9 %collective-permute-start.16 = (f32[32,1024]{1,0:T(8,128)S(1)}, f32[32,1024]{1,0:T(8,128)S(1)}, u32[]{:S(2)}, u32[]{:S(2)}) collective-permute-start(f32[32,1024]{1,0:T(8,128)S(1)} %add_add_fusion), channel_id=1, source_target_pairs={{0,257},{1,256},{64,321},{65,320},{128,385},{129,384},{192,449},{1... | collective-permute-start | bytes 393224 | tf_op jit(solution)/shard_map/ppermute | solution.py:251
  359.9 2.4 copy-start.9
Sparse Core Ops, SparseCore 0:
  20.5 73.0 all-gather.2

commit v3 on v2

--- a/solution.py
+++ b/solution.py
@@ -1,3 +1,5 @@
+import functools
+
 import jax
 import jax.numpy as jnp
 from jax import lax
@@ -13,8 +15,8 @@
 NN = ((1,), (0,))
 NT = ((1,), (1,))
 TN = ((0,), (0,))
-DP = ("group", "core")
-PLANE = ("group", "half")
+DP = ("along", "across", "core")
+PLANE = ("along", "across", "half")
 
 
 def dot(left, right, dims, precision=None):
@@ -89,21 +91,37 @@
     )
 
 
-def to_rows(units_ref, gather_ref, rows_ref, arrivals):
-    count, piece = gather_ref.shape[0], units_ref.shape[1]
+def reorder(count, capacity, dim):
+    rows = lax.broadcasted_iota(jnp.int32, (count, count), dim)
     part = count // PIECES
+    pieces = sum((rows >= part * j).astype(jnp.int32) for j in range(1, PIECES))
+    inside = rows - part * pieces
+    experts = sum(
+        (inside >= capacity * i).astype(jnp.int32) for i in range(1, part // capacity)
+    )
+    place = inside - capacity * experts + capacity * pieces + PIECES * capacity * experts
+    return (place == lax.broadcasted_iota(jnp.int32, (count, count), 1 - dim)).astype(BF16)
+
+
+def to_rows(units_ref, rows_ref, arrivals, capacity):
+    piece = units_ref.shape[1]
+    count = units_ref.shape[0] // len(arrivals)
+    part = count // PIECES
+    order = reorder(count, capacity, 0)
     for i, copy in enumerate(arrivals):
         copy.wait()
-        block = dot(gather_ref[...], units_ref[i * count : (i + 1) * count, :], NN).astype(BF16)
+        block = dot(order, units_ref[i * count : (i + 1) * count, :], NN).astype(BF16)
         for j in range(PIECES):
             rows_ref[i * part : (i + 1) * part, j * piece : (j + 1) * piece] = block[
                 j * part : (j + 1) * part
             ]
 
 
-def to_units(rows_ref, scatter_ref, units_ref, departures):
-    count, piece = scatter_ref.shape[0], units_ref.shape[1]
+def to_units(rows_ref, units_ref, departures, capacity):
+    piece = units_ref.shape[1]
+    count = units_ref.shape[0] // len(departures)
     part = count // PIECES
+    order = reorder(count, capacity, 1)
     for i, copy in enumerate(departures):
         block = jnp.concatenate(
             [
@@ -112,27 +130,27 @@
             ],
             axis=0,
         )
-        units_ref[i * count : (i + 1) * count, :] = dot(scatter_ref[...], block, NN).astype(BF16)
+        units_ref[i * count : (i + 1) * count, :] = dot(order, block, NN).astype(BF16)
         copy.start()
 
 
 def forward_kernel(
-    got_hbm, gather_ref, scatter_ref, w_hbm, units_hbm, hidden_ref, act_hbm, slope_hbm,
-    proj_ref, down_ref, got_ref, rows_ref, outs_ref, units_ref, act_ref, slope_ref, sems,
+    blocks, capacity, got_hbm, w_hbm, units_hbm, hidden_hbm, act_hbm, slope_hbm,
+    proj_ref, down_ref, got_ref, rows_ref, outs_ref, units_ref, act_ref, slope_ref, hidden_ref, sems,
 ):
     half = hidden_ref.shape[1] // 2
     piece = got_ref.shape[1]
-    count = gather_ref.shape[0]
-    blocks = got_ref.shape[0] // count
-    arrivals = copies_of(blocks_of(got_hbm, count), blocks_of(got_ref, count), sems, 8)
+    count = got_ref.shape[0] // blocks
+    arrivals = copies_of(blocks_of(got_hbm, count), blocks_of(got_ref, count), sems, 12)
     departures = copies_of(
-        blocks_of(units_ref, count), blocks_of(units_hbm, count), sems, 8 + blocks
+        blocks_of(units_ref, count), blocks_of(units_hbm, count), sems, 12 + blocks
     )
     proj, down = weight_copies(w_hbm, proj_ref, down_ref, sems, half)
     kept = copies_of(sides_of(act_ref, half), sides_of(act_hbm, half), sems, 4)
     kept += copies_of(sides_of(slope_ref, half), sides_of(slope_hbm, half), sems, 6)
+    kept += copies_of(sides_of(hidden_ref, half), sides_of(hidden_hbm, half), sems, 8)
     started(arrivals + proj + down)
-    to_rows(got_ref, gather_ref, rows_ref, arrivals)
+    to_rows(got_ref, rows_ref, arrivals, capacity)
     rows = rows_ref[...]
     for side in range(2):
         proj[side].wait()
@@ -144,43 +162,47 @@
         hidden_ref[:, columns] = (act * pre_up).astype(BF16)
         act_ref[:, columns] = act
         slope_ref[:, columns] = pre_up * sig * (1.0 + pre_gate * (1.0 - sig))
-        kept[side].start()
-        kept[2 + side].start()
+        started(kept[side::2])
     finished(down)
     for j in range(PIECES):
         cols = slice(j * piece, (j + 1) * piece)
         out = dot(hidden_ref[:, :half], down_ref[0, cols, :], NT)
         out = out + dot(hidden_ref[:, half:], down_ref[1, cols, :], NT)
         outs_ref[:, cols] = out.astype(BF16)
-    to_units(outs_ref, scatter_ref, units_ref, departures)
+    to_units(outs_ref, units_ref, departures, capacity)
     finished(kept + departures)
 
 
 def backward_kernel(
-    got_hbm, act_hbm, slope_hbm, hidden_ref, q_ref, error_left_ref, gather_ref, scatter_ref, w_hbm,
-    units_hbm, rows_hbm, left_ref,
-    proj_ref, down_ref, got_ref, rows_ref, outs_ref, units_ref, act_ref, slope_ref, sems, grads_ref,
+    blocks, capacity, got_hbm, act_hbm, slope_hbm, hidden_hbm, q_hbm, error_left_hbm, w_hbm,
+    units_hbm, rows_hbm, left_hbm,
+    proj_ref, down_ref, got_ref, rows_ref, outs_ref, units_ref, act_ref, slope_ref, hidden_ref, sems,
+    grads_ref, q_ref, error_left_ref, left_ref,
 ):
     half = act_ref.shape[1] // 2
     piece = units_ref.shape[1]
-    count = gather_ref.shape[0]
-    blocks = got_ref.shape[0] // count
-    arrivals = copies_of(blocks_of(got_hbm, count), blocks_of(got_ref, count), sems, 8)
+    count = got_ref.shape[0] // blocks
+    arrivals = copies_of(blocks_of(got_hbm, count), blocks_of(got_ref, count), sems, 12)
     departures = copies_of(
-        blocks_of(units_ref, count), blocks_of(units_hbm, count), sems, 8 + blocks
+        blocks_of(units_ref, count), blocks_of(units_hbm, count), sems, 12 + blocks
     )
     proj, down = weight_copies(w_hbm, proj_ref, down_ref, sems, half)
     kept = copies_of(sides_of(act_hbm, half), sides_of(act_ref, half), sems, 4)
     kept += copies_of(sides_of(slope_hbm, half), sides_of(slope_ref, half), sems, 6)
-    out_rows = copies_of([rows_ref], [rows_hbm], sems, 8 + 2 * blocks)
-    started(arrivals + down + kept + proj)
-    to_rows(got_ref, gather_ref, rows_ref, arrivals)
+    small = copies_of([q_hbm, hidden_hbm], [q_ref, hidden_ref], sems, 8)
+    small += copies_of([error_left_hbm], [error_left_ref], sems, 10)
+    out_rows = copies_of([rows_ref], [rows_hbm], sems, 12 + 2 * blocks)
+    out_left = copies_of([left_ref], [left_hbm], sems, 11)
+    started(arrivals + small + down + kept + proj)
+    to_rows(got_ref, rows_ref, arrivals, capacity)
     started(out_rows)
     rows = rows_ref[...]
+    finished(small)
     grad_q = folded(dot(thirds(q_ref[...]), rows, NT))
     left = folded(dot(thirds(grad_q), hidden_ref[...], NN))
     left_ref[:, :half] = left[:, :half] + error_left_ref[...]
     left_ref[:, half:] = left[:, half:]
+    started(out_left)
     for side in range(2):
         columns = slice(side * half, (side + 1) * half)
         down[side].wait()
@@ -195,12 +217,12 @@
         out = dot(grads_ref[0], proj_ref[0, cols, :], NT)
         out = out + dot(grads_ref[1], proj_ref[1, cols, :], NT)
         outs_ref[:, cols] = out.astype(BF16)
-    to_units(outs_ref, scatter_ref, units_ref, departures)
-    finished(departures + out_rows)
+    to_units(outs_ref, units_ref, departures, capacity)
+    finished(departures + out_rows + out_left)
 
 
 def basis_kernel(
-    core_ref, left_ref, hidden_ref, rows_hbm, error_hbm, basis_ref, terms_ref, right_ref, away_ref,
+    core_ref, left_ref, hidden_ref, rows_hbm, error_hbm, basis_ref, right_ref, away_ref,
     rows_ref, error_ref, sems,
 ):
     copies = copies_of([rows_hbm, error_hbm], [rows_ref, error_ref], sems, 0)
@@ -224,9 +246,6 @@
     mine = basis[:, :half]
     basis_ref[...] = mine
     terms = thirds(mine)
-    terms_ref[...] = jnp.concatenate(
-        [terms[:rank], terms[:rank], terms[rank : 2 * rank], terms[rank : 2 * rank]], axis=0
-    )
     finished(copies)
     hidden_basis = folded(dot(thirds(basis), hidden_ref[...], NT))
     right = folded(dot(terms, error_ref[...], NN))
@@ -237,25 +256,25 @@
     away_ref[...] = jnp.where(first, right[:, span:], right[:, :span])
 
 
-def error_kernel(merged_ref, terms_ref, right_ref, fresh_ref):
-    right = right_ref[...]
-    rank = right.shape[0]
-    parts = thirds(right)
-    high, middle = parts[:rank], parts[rank : 2 * rank]
-    approx = dot(terms_ref[...], jnp.concatenate([high, middle, high, middle], axis=0), TN)
+def error_kernel(merged_ref, basis_ref, right_ref, fresh_ref):
+    rank = right_ref.shape[0]
+    basis, right = thirds(basis_ref[...]), thirds(right_ref[...])
+    high, middle = right[:rank], right[rank : 2 * rank]
+    left = jnp.concatenate([basis[:rank], basis[:rank], basis[rank : 2 * rank]], axis=0)
+    approx = dot(left, jnp.concatenate([high, middle, high], axis=0), TN)
     fresh_ref[...] = (merged_ref[...] - approx).astype(BF16)
 
 
 def moved(value, mask):
-    count = lax.axis_size("group") * lax.axis_size("half")
+    count = lax.axis_size("along") * lax.axis_size("across") * lax.axis_size("half")
     return lax.ppermute(value, PLANE, [(source, source ^ mask) for source in range(count)])
 
 
-def plane_sum(value, flip):
-    near, far, both = moved(value, 2), moved(value, 4), moved(value, 6)
-    value = (value + near) + (far + both)
-    near, far, both = moved(value, 8), moved(value, 1), moved(value, 9)
-    return (value + near) + flip(far + both)
+def pairs_sum(values):
+    while values.shape[0] > 1:
+        half = values.shape[0] // 2
+        values = values[:half] + values[half:]
+    return values[0]
 
 
 def shards(tokens, target, routes, gates, w_gate, w_up, w_down, error, q_start):
@@ -286,16 +305,6 @@
     spread = jnp.sum(select, axis=1).reshape(PIECES * tok, experts * unit)
     select = select.reshape(PIECES * top * tok, experts * unit)
 
-    block = min(BLOCK, experts)
-    order = (
-        jnp.arange(PIECES, dtype=jnp.int32)[:, None, None] * capacity
-        + jnp.arange(block, dtype=jnp.int32)[None, :, None] * unit
-        + jnp.arange(capacity, dtype=jnp.int32)[None, None, :]
-    ).reshape(block * unit)
-    block_lanes = jnp.arange(block * unit, dtype=jnp.int32)
-    gather = (order[:, None] == block_lanes).astype(BF16)
-    scatter = (block_lanes[:, None] == order).astype(BF16)
-
     def pieces_of(rows):
         return jnp.concatenate(jnp.split(rows, PIECES, axis=-1), axis=0)
 
@@ -318,7 +327,7 @@
     inbox, q_full, error_left = lax.optimization_barrier((inbox, q_full, error_left))
 
     unit_shape, row_shape = (experts * unit, piece), (slots, width)
-    blocks = experts // block
+    blocks = experts // min(BLOCK, experts)
     scratch = [
         pltpu.VMEM((2, width, inner), BF16),
         pltpu.VMEM((2, width, hidden_half), BF16),
@@ -328,13 +337,14 @@
         pltpu.VMEM(unit_shape, BF16),
         pltpu.VMEM((slots, inner), F32),
         pltpu.VMEM((slots, inner), F32),
-        pltpu.SemaphoreType.DMA((9 + 2 * blocks,)),
+        pltpu.VMEM((slots, inner), BF16),
+        pltpu.SemaphoreType.DMA((13 + 2 * blocks,)),
     ]
     returned, hidden, act, act_slope = local_call(
-        forward_kernel,
+        functools.partial(forward_kernel, blocks, capacity),
         [(unit_shape, BF16), ((slots, inner), BF16), ((slots, inner), F32), ((slots, inner), F32)],
         scratch,
-        inbox, gather, scatter, weights, hbm=(0, 3), out_hbm=(0, 2, 3), memory=58,
+        inbox, weights, hbm=(0, 1), out_hbm=(0, 1, 2, 3), memory=58,
     )
     returned = exchange(returned)
     picked = dot(select, returned, NN).reshape(PIECES, top, tok, piece)
@@ -347,30 +357,43 @@
     grad_got, hidden_other = lax.optimization_barrier((grad_got, hidden_other))
 
     token_part, rows, left = local_call(
-        backward_kernel,
+        functools.partial(backward_kernel, blocks, capacity),
         [(unit_shape, BF16), (row_shape, BF16), ((rank, inner), F32)],
-        scratch + [pltpu.VMEM((2, slots, inner), BF16)],
-        grad_got, act, act_slope, hidden, q_full, error_left, gather, scatter, weights,
-        hbm=(0, 1, 2, 8), out_hbm=(0, 1), memory=58,
+        scratch
+        + [
+            pltpu.VMEM((2, slots, inner), BF16),
+            pltpu.VMEM((rank, width), F32),
+            pltpu.VMEM((rank, hidden_half), F32),
+            pltpu.VMEM((rank, inner), F32),
+        ],
+        grad_got, act, act_slope, hidden, q_full, error_left, weights,
+        hbm=range(7), out_hbm=range(3), memory=58,
     )
     slot_grad = exchange(token_part)
     token_grad = dot(spread, slot_grad, NN).astype(BF16)
     token_grad = jnp.concatenate(jnp.split(token_grad, PIECES, axis=0), axis=1)
 
-    def flip(value):
-        return jnp.concatenate([value[:, hidden_half:], value[:, :hidden_half]], axis=1)
-
-    left = jnp.sum(lax.all_gather(left, "core"), axis=0)
-    left, sent_rows = lax.optimization_barrier((left, rows))
-    rows_other = moved(sent_rows, 1)
-    left, rows_other = lax.optimization_barrier((plane_sum(left, flip), rows_other))
+    rows_all = lax.all_gather(rows, "half", axis=0, tiled=True)
+    hidden_mine = hidden[:, :hidden_half]
+    hidden_all = jnp.concatenate(
+        [
+            jnp.where(half == 0, hidden_mine, hidden_other),
+            jnp.where(half == 0, hidden_other, hidden_mine),
+        ],
+        axis=0,
+    )
+
+    left = pairs_sum(lax.all_gather(left, ("across", "core")))
+    near, far, both = moved(left, 8), moved(left, 1), moved(left, 9)
+    left = left + near
+    away = far + both
+    left = left + jnp.concatenate([away[:, hidden_half:], away[:, :hidden_half]], axis=1)
     core = lax.axis_index("core")
     span = width // lax.axis_size("core")
-    basis, terms, right, right_away = local_call(
+    basis, right, right_away = local_call(
         basis_kernel,
         [
             ((rank, hidden_half), F32),
-            ((4 * rank, hidden_half), BF16),
             ((rank, span), F32),
             ((rank, span), F32),
         ],
@@ -381,20 +404,21 @@
         ],
         core.reshape(1), left, hidden, rows, error, hbm=(3, 4), smem=(0,),
     )
-    merged = (
-        dot(hidden[:, :hidden_half], rows, TN)
-        + dot(hidden_other, rows_other, TN)
-        + error.astype(F32)
-    )
-    right = right + lax.ppermute(right_away, "core", [(0, 1), (1, 0)])
-    right = plane_sum(right, lambda value: value) / (lax.axis_size("group") * lax.axis_size("core"))
-    right = lax.all_gather(right, "core", axis=1, tiled=True)
+    right = (right + lax.ppermute(right_away, "core", [(0, 1), (1, 0)])).astype(BF16)
+    right = lax.all_gather(right, ("across", "core"))
+    right = pairs_sum(right.reshape(-1, 2, rank, span).astype(F32))
+    right = right.transpose(1, 0, 2).reshape(rank, width)
+    near, far, both = moved(right, 8), moved(right, 1), moved(right, 9)
+    merged = dot(hidden_all, rows_all, TN) + error.astype(F32)
+    replicas = lax.axis_size("along") * lax.axis_size("across") * lax.axis_size("core")
+    right, token_grad = lax.optimization_barrier((right + near, token_grad))
+    right = (right + (far + both)) / replicas
     (new_error,) = local_call(
-        error_kernel, [((hidden_half, width), BF16)], [], merged, terms, right
+        error_kernel, [((hidden_half, width), BF16)], [], merged, basis, right
     )
     q_columns = jnp.where(half == 0, right[: rank // 2], right[rank // 2 :])
-    replicas = lax.axis_size("group") * lax.axis_size("core")
-    replica = lax.axis_index("group") * lax.axis_size("core") + lax.axis_index("core")
+    replica = lax.axis_index("along") * lax.axis_size("across") + lax.axis_index("across")
+    replica = replica * lax.axis_size("core") + core
     q_rows = width // replicas
     q_factor = lax.dynamic_slice_in_dim(q_columns, replica * q_rows, q_rows, 1).T
     return token_grad, basis.T, q_factor, new_error
@@ -403,8 +427,8 @@
 def solution(mesh):
     replicas, places = mesh.shape["dp"], mesh.shape["expert"]
     split = Mesh(
-        mesh.devices.reshape(replicas // 2, 2, places // 2, 2),
-        ("group", "core", "expert", "half"),
+        mesh.devices.reshape(2, replicas // 4, 2, places // 2, 2),
+        ("along", "across", "core", "expert", "half"),
     )
     pair = ("expert", "half")
     rows = P(DP + pair, None)

time: 373 us -> 357 us (0.957)
  starting transfers between devices: 113 us -> 90.3 us
  blocking collectives: 8.08 us -> 27.6 us
  waiting for transfers between devices: 180 us -> 170 us
  Pallas kernels: 27.5 us -> 23.7 us
    ppermute x16 -> x9, starting transfers between devices: 57.8 us -> 33.9 us  [moved(): lax.ppermute(value, PLANE, [(source, source ^ mask) for source in range(c...]
    all_gather x2, blocking collectives: 8.08 us -> 27.6 us  [the longest x1 14.3 us: shards(): left = pairs_sum(lax.all_gather(left, ('across', 'core')))]
    ppermute x16 -> x9, waiting for transfers between devices: 27.3 us -> 16.5 us  [moved(): lax.ppermute(value, PLANE, [(source, source ^ mask) for source in range(c...]
    pallas_call x4, Pallas kernels: 27.5 us -> 23.7 us  [local_call(): pl.pallas_call(kernel, out_shape=[jax.ShapeDtypeStruct(shape, dtype) for...]
    dot_general x7 -> x6, matrix products: 12.1 us -> 13.4 us  [dot(): lax.dot_general(left, right, (dims, ((), ())), precision=precision, prefe...]
  transfers between devices with their start and end apart: 22 -> 16, of which waited for: 13 -> 8; matrix products, arithmetic and copies ran while one was open for 4% -> 5% of each run, Pallas kernels for 2% -> 1%
where the time goes in v3:
time: 357 us; the launch traced here: 355 us
  waiting for transfers between devices  170 us (48%)
  starting transfers between devices  90.3 us (25%)
  blocking collectives  27.6 us (8%)
  Pallas kernels  23.7 us (7%)
  between operations  14.6 us (4%)
  matrix products  13.4 us (4%)
  other arithmetic  11 us (3%)
  local copies, waits for them, and re-layouts  4.85 us (1%)
    all_to_all x4, waiting for transfers between devices, exchange(): lax.all_to_all(sent, 'expert', split_axis=0, concat_axis=0, tiled=True)  152 us
    all_to_all x4, starting transfers between devices, exchange(): lax.all_to_all(sent, 'expert', split_axis=0, concat_axis=0, tiled=True)  53.1 us
    ppermute x9, starting transfers between devices, moved(): lax.ppermute(value, PLANE, [(source, source ^ mask) for source in range(c...  33.9 us
    pallas_call x4, Pallas kernels, local_call(): pl.pallas_call(kernel, out_shape=[jax.ShapeDtypeStruct(shape, dtype) for...  23.7 us
    ppermute x9, waiting for transfers between devices, moved(): lax.ppermute(value, PLANE, [(source, source ^ mask) for source in range(c...  16.5 us
    all_gather x1, blocking collectives, shards(): left = pairs_sum(lax.all_gather(left, ('across', 'core')))  14.3 us
    dot_general x6, matrix products, dot(): lax.dot_general(left, right, (dims, ((), ())), precision=precision, prefe...  13.4 us
    all_gather x1, blocking collectives, shards(): right = lax.all_gather(right, ('across', 'core'))  13.3 us
  transfers between devices with their start and end apart: 16, of which 8 were waited for; matrix products, arithmetic and copies ran while one was open for 5% of the time, Pallas kernels for 1%

profile of v3, /device:TPU:1, one launch (start us, length us, event | category | flops | bytes accessed | tf_op | source)
XLA Modules:
  0.0 355.3 jit_solution(4386848460385426654)
XLA Ops:
  7.2 1.1 copy.29
  8.3 1.0 pad_maximum_fusion.3
  9.3 5.7 %collective-permute-start = (bf16[128,1152]{1,0:T(8,128)(2,1)S(1)}, bf16[128,1152]{1,0:T(8,128)(2,1)S(1)}, u32[]{:S(2)}, u32[]{:S(2)}) collective-permute-start(bf16[128,1152]{1,0:T(8,128)(2,1)S(1)} %pad_maximum_fusion.3), channel_id=1, source_target_pairs={{0,1},{1,0},{64,65},{65,64},{128,129},{129,128},{192,193},{193,192... | collective-permute-start | bytes 884744 | tf_op jit(solution)/shard_map/ppermute | solution.py:270
  14.9 0.7 convert_reduce_fusion
  16.0 0.7 select_reduce_fusion
  17.9 1.6 convolution_convert_fusion
  19.5 0.9 pad_maximum_fusion
  20.4 17.0 %all-to-all-start = ((bf16[16,40,1024]{2,1,0:T(8,128)(2,1)}), bf16[16,40,1024]{2,1,0:T(8,128)(2,1)S(1)}, u32[]{:S(2)}, u32[]{:S(2)}) async-start(bf16[16,40,1024]{2,1,0:T(8,128)(2,1)} %bitcast.6), calls=%async_computation | async-start | bytes 2621440 | tf_op jit(solution)/shard_map/all_to_all | solution.py:313
  37.3 4.8 %collective-permute-start.1 = (f32[16,2048]{1,0:T(8,128)S(1)}, f32[16,2048]{1,0:T(8,128)S(1)}, u32[]{:S(2)}, u32[]{:S(2)}) collective-permute-start(f32[16,2048]{1,0:T(8,128)S(1)} %bitcast.61), channel_id=1, source_target_pairs={{0,1},{1,0},{64,65},{65,64},{128,129},{129,128},{192,193},{193,192... | collective-permute-start | bytes 393224 | tf_op jit(solution)/shard_map/ppermute | solution.py:270
  42.2 2.4 collective-permute-done.1
  44.6 0.7 pad_maximum_fusion.4.q_hbm
  45.3 2.1 fusion.17.error_left_hbm
  47.4 47.2 %all-to-all-done = bf16[16,40,1024]{2,1,0:T(8,128)(2,1)S(1)} async-done(((bf16[16,40,1024]{2,1,0:T(8,128)(2,1)}), bf16[16,40,1024]{2,1,0:T(8,128)(2,1)S(1)}, u32[]{:S(2)}, u32[]{:S(2)}) %all-to-all-start) | async-done | bytes 1310752 | tf_op jit(solution)/shard_map/all_to_all | solution.py:313
  94.6 1.1 copy-done.7
  95.7 8.3 %shard_map.120 = (bf16[640,1024]{1,0:T(8,128)(2,1)}, bf16[320,768]{1,0:T(8,128)(2,1)}, f32[320,768]{1,0:T(8,128)}, f32[320,768]{1,0:T(8,128)}) custom-call(bf16[640,1024]{1,0:T(8,128)(2,1)} %bitcast.45, bf16[2048,2304]{1,0:T(8,128)(2,1)} %all-gather.5.cloned.1.call-done.w_hbm), custom_call_target="tpu_custom_call" | custom-call | tf_op jit(solution)/shard_map/pallas_call | solution.py:47
  103.9 12.2 %all-to-all-start.1 = ((bf16[16,40,1024]{2,1,0:T(8,128)(2,1)}), bf16[16,40,1024]{2,1,0:T(8,128)(2,1)S(1)}, u32[]{:S(2)}, u32[]{:S(2)}) async-start(bf16[16,40,1024]{2,1,0:T(8,128)(2,1)} %bitcast.50), calls=%async_computation.1 | async-start | bytes 2621440 | tf_op jit(solution)/shard_map/all_to_all | solution.py:313
  116.2 57.3 %all-to-all-done.1 = bf16[16,40,1024]{2,1,0:T(8,128)(2,1)S(1)} async-done(((bf16[16,40,1024]{2,1,0:T(8,128)(2,1)}), bf16[16,40,1024]{2,1,0:T(8,128)(2,1)S(1)}, u32[]{:S(2)}, u32[]{:S(2)}) %all-to-all-start.1) | async-done | bytes 1310752 | tf_op jit(solution)/shard_map/all_to_all | solution.py:313
  173.5 1.0 multiply_reduce_fusion
  174.7 2.0 bitcast_convert_fusion
  176.7 12.0 %all-to-all-start.2 = ((bf16[16,40,1024]{2,1,0:T(8,128)(2,1)}), bf16[16,40,1024]{2,1,0:T(8,128)(2,1)S(1)}, u32[]{:S(2)}, u32[]{:S(2)}) async-start(bf16[16,40,1024]{2,1,0:T(8,128)(2,1)} %bitcast.52), calls=%async_computation.2 | async-start | bytes 2621440 | tf_op jit(solution)/shard_map/all_to_all | solution.py:313
  188.8 5.0 %collective-permute-start.2 = (bf16[320,384]{1,0:T(8,128)(2,1)S(1)}, bf16[320,384]{1,0:T(8,128)(2,1)}, u32[]{:S(2)}, u32[]{:S(2)}) collective-permute-start(bf16[320,384]{1,0:T(8,128)(2,1)S(1)} %slice.52), channel_id=1, source_target_pairs={{0,1},{1,0},{64,65},{65,64},{128,129},{129,128},{192,193},{193,192... | collective-permute-start | bytes 737288 | tf_op jit(solution)/shard_map/ppermute | solution.py:270
  193.8 5.2 %collective-permute-done.2 = bf16[320,384]{1,0:T(8,128)(2,1)} collective-permute-done((bf16[320,384]{1,0:T(8,128)(2,1)S(1)}, bf16[320,384]{1,0:T(8,128)(2,1)}, u32[]{:S(2)}, u32[]{:S(2)}) %collective-permute-start.2) | collective-permute-done | bytes 245792 | tf_op jit(solution)/shard_map/ppermute | solution.py:270
  199.0 47.1 %all-to-all-done.2 = bf16[16,40,1024]{2,1,0:T(8,128)(2,1)S(1)} async-done(((bf16[16,40,1024]{2,1,0:T(8,128)(2,1)}), bf16[16,40,1024]{2,1,0:T(8,128)(2,1)S(1)}, u32[]{:S(2)}, u32[]{:S(2)}) %all-to-all-start.2) | async-done | bytes 1310752 | tf_op jit(solution)/shard_map/all_to_all | solution.py:313
  246.1 1.1 copy-done.6
  247.1 9.2 %shard_map.121 = (bf16[640,1024]{1,0:T(8,128)(2,1)}, bf16[320,2048]{1,0:T(8,128)(2,1)}, f32[32,768]{1,0:T(8,128)}) custom-call(bf16[640,1024]{1,0:T(8,128)(2,1)} %bitcast.44, f32[320,768]{1,0:T(8,128)} %get-tuple-element.29.act_hbm, f32[320,768]{1,0:T(8,128)} %get-tuple-element.30.slope_hbm, bf16[320,768]{1,0:T(8,128)(2,1)} %get-tuple-element.27.hidden_hbm.hidden_ref, ...), custom_call_target="tpu_custom_call" | custom-call | tf_op jit(solution)/shard_map/pallas_call | solution.py:47
  256.3 12.0 %all-to-all-start.3 = ((bf16[16,40,1024]{2,1,0:T(8,128)(2,1)}), bf16[16,40,1024]{2,1,0:T(8,128)(2,1)}, u32[]{:S(2)}, u32[]{:S(2)}) async-start(bf16[16,40,1024]{2,1,0:T(8,128)(2,1)} %bitcast.49), calls=%async_computation.3 | async-start | bytes 2621440 | tf_op jit(solution)/shard_map/all_to_all | solution.py:313
  268.3 0.7 all-gather.7.cloned.1.call-update
  269.2 14.3 %all-gather = f32[256,768]{1,0:T(8,128)S(1)} all-gather(f32[32,768]{1,0:T(8,128)S(1)} %copy-done.16), channel_id=2, replica_groups=mesh['along'=2,'across'=4,'core'=2,'expert'=16,'half'=2] {'across','core'}, dimensions={0}, use_global_device_ids=true | all-gather | bytes 884736 | tf_op jit(solution)/shard_map/all_gather | solution.py:386
  284.3 4.8 %collective-permute-start.4 = (f32[32,768]{1,0:T(8,128)S(1)}, f32[32,768]{1,0:T(8,128)}, u32[]{:S(2)}, u32[]{:S(2)}) collective-permute-start(f32[32,768]{1,0:T(8,128)S(1)} %slice_add_fusion.4), channel_id=1, source_target_pairs={{0,1},{1,0},{64,65},{65,64},{128,129},{129,128},{192,193},{193,192... | collective-permute-start | bytes 294920 | tf_op jit(solution)/shard_map/ppermute | solution.py:270
  289.1 2.7 collective-permute-start.5
  291.8 1.9 collective-permute-start.3
  293.7 7.1 %collective-permute-done.5 = f32[32,768]{1,0:T(8,128)} collective-permute-done((f32[32,768]{1,0:T(8,128)S(1)}, f32[32,768]{1,0:T(8,128)}, u32[]{:S(2)}, u32[]{:S(2)}) %collective-permute-start.5) | collective-permute-done | bytes 98336 | tf_op jit(solution)/shard_map/ppermute | solution.py:270
  300.9 1.0 add.78
  301.9 1.0 maximum_add_fusion.left_ref
  302.9 4.5 %shard_map.122 = (f32[32,384]{1,0:T(8,128)}, f32[32,1024]{1,0:T(8,128)S(1)}, f32[32,1024]{1,0:T(8,128)S(1)}) custom-call(s32[1]{0:T(128)} %bitcast.core_ref, f32[32,768]{1,0:T(8,128)S(1)} %maximum_add_fusion.left_ref, bf16[320,768]{1,0:T(8,128)(2,1)S(1)} %copy-done.4, bf16[320,2048]{1,0:T(8,128)(2,1)S(1)} %copy-done.2, bf16[384,2048]{1,0:T(8,128)(2,1)S(1)} %copy-done), custom_call_target="tpu_custom_call" | custom-call | tf_op jit(solution)/shard_map/pallas_call | solution.py:47
  307.4 3.2 collective-permute-start.6
  310.7 1.0 collective-permute-done.6
  311.7 13.3 %all-gather.1 = bf16[256,1024]{1,0:T(8,128)(2,1)S(1)} all-gather(bf16[32,1024]{1,0:T(8,128)(2,1)S(1)} %add_convert_fusion), channel_id=3, replica_groups=mesh['along'=2,'across'=4,'core'=2,'expert'=16,'half'=2] {'across','core'}, dimensions={0}, use_global_device_ids=true | all-gather | bytes 589824 | tf_op jit(solution)/shard_map/all_gather | solution.py:408
  325.5 1.9 collective-permute-start.7
  327.4 1.0 broadcast_select_fusion.1
  328.4 3.0 collective-permute-start.9
  331.4 4.1 %collective-permute-start.8 = (f32[32,2048]{1,0:T(8,128)S(1)}, f32[32,2048]{1,0:T(8,128)}, u32[]{:S(2)}, u32[]{:S(2)}) collective-permute-start(f32[32,2048]{1,0:T(8,128)S(1)} %bitcast.55), channel_id=1, source_target_pairs={{0,1},{1,0},{64,65},{65,64},{128,129},{129,128},{192,193},{193,192... | collective-permute-start | bytes 786440 | tf_op jit(solution)/shard_map/ppermute | solution.py:270
  335.6 4.8 %convert_add_fusion.merged_ref = f32[384,2048]{1,0:T(8,128)} fusion(bf16[384,2048]{1,0:T(8,128)(2,1)S(1)} %copy-done, bf16[640,2048]{1,0:T(8,128)(2,1)} %all-gather.7.cloned.1.call-done, bf16[320,384]{1,0:T(8,128)(2,1)S(1)} %get-tuple-element.43, bf16[320,384]{1,0:T(8,128)(2,1)S(1)} %get-tuple-element.42), kind=kOutput, calls=%fused_computation | convolution fusion | flops 1009188864 | bytes 7831552 | tf_op jit(solution)/shard_map/dot_general | solution.py:23
  340.4 1.9 convolution_convert_fusion.1
  342.4 0.8 pad_maximum_fusion.2
  343.2 1.8 collective-permute-done.9
  345.0 1.1 add_multiply_fusion.right_ref
  346.1 1.7 shard_map.123
  (74 shorter events, 4.0 us)
Async XLA Ops:
  7.2 10.2 %copy-start.11 = (bf16[128,2048]{1,0:T(8,128)(2,1)S(1)}, bf16[128,2048]{1,0:T(8,128)(2,1)}, u32[]{:S(2)}) copy-start(bf16[128,2048]{1,0:T(8,128)(2,1)} %param.9) | copy-start | bytes 1572868
  7.2 87.4 %all-gather.5.cloned.1.call-start = ((), (), s32[]{:S(2)}) async-start(), calls=%async_computation.4 | async-start | bytes 10027008 | tf_op jit(solution)/shard_map/all_gather | solution.py:318
  9.3 10.2 %collective-permute-start = (bf16[128,1152]{1,0:T(8,128)(2,1)S(1)}, bf16[128,1152]{1,0:T(8,128)(2,1)S(1)}, u32[]{:S(2)}, u32[]{:S(2)}) collective-permute-start(bf16[128,1152]{1,0:T(8,128)(2,1)S(1)} %pad_maximum_fusion.3), channel_id=1, source_target_pairs={{0,1},{1,0},{64,65},{65,64},{128,129},{129,128},{192,193},{193,192... | collective-permute-start | bytes 884744 | tf_op jit(solution)/shard_map/ppermute | solution.py:270
  17.6 1.8 copy-start.13
  17.6 1.8 copy-start.14
  17.9 2.5 copy-start.8
  20.3 17.0 %copy-start.15 = (f32[2048,16]{0,1:T(8,128)S(1)}, f32[2048,16]{0,1:T(8,128)}, u32[]{:S(2)}) copy-start(f32[2048,16]{0,1:T(8,128)} %param.17) | copy-start | bytes 393220
  20.4 25.0 %copy-start = (bf16[384,2048]{1,0:T(8,128)(2,1)S(1)}, bf16[384,2048]{1,0:T(8,128)(2,1)}, u32[]{:S(2)}) copy-start(bf16[384,2048]{1,0:T(8,128)(2,1)} %error_hbm.1) | copy-start | bytes 4718596
  20.4 74.2 %all-to-all-start = ((bf16[16,40,1024]{2,1,0:T(8,128)(2,1)}), bf16[16,40,1024]{2,1,0:T(8,128)(2,1)S(1)}, u32[]{:S(2)}, u32[]{:S(2)}) async-start(bf16[16,40,1024]{2,1,0:T(8,128)(2,1)} %bitcast.6), calls=%async_computation | async-start | bytes 2621440 | tf_op jit(solution)/shard_map/all_to_all | solution.py:313
  37.3 7.2 %collective-permute-start.1 = (f32[16,2048]{1,0:T(8,128)S(1)}, f32[16,2048]{1,0:T(8,128)S(1)}, u32[]{:S(2)}, u32[]{:S(2)}) collective-permute-start(f32[16,2048]{1,0:T(8,128)S(1)} %bitcast.61), channel_id=1, source_target_pairs={{0,1},{1,0},{64,65},{65,64},{128,129},{129,128},{192,193},{193,192... | collective-permute-start | bytes 393224 | tf_op jit(solution)/shard_map/ppermute | solution.py:270
  94.6 1.1 copy-start.7
  103.9 12.2 %copy-start.12 = (bf16[128,2048]{1,0:T(8,128)(2,1)S(1)}, bf16[128,2048]{1,0:T(8,128)(2,1)}, u32[]{:S(2)}) copy-start(bf16[128,2048]{1,0:T(8,128)(2,1)} %param.10) | copy-start | bytes 1572868
  103.9 69.6 %all-to-all-start.1 = ((bf16[16,40,1024]{2,1,0:T(8,128)(2,1)}), bf16[16,40,1024]{2,1,0:T(8,128)(2,1)S(1)}, u32[]{:S(2)}, u32[]{:S(2)}) async-start(bf16[16,40,1024]{2,1,0:T(8,128)(2,1)} %bitcast.50), calls=%async_computation.1 | async-start | bytes 2621440 | tf_op jit(solution)/shard_map/all_to_all | solution.py:313
  116.1 57.4 %copy-start.17 = (f32[128,2]{0,1:T(2,128)S(1)}, f32[128,2]{0,1:T(2,128)}, u32[]{:S(2)}) copy-start(f32[128,2]{0,1:T(2,128)} %param.12) | copy-start | bytes 3076
  176.7 12.0 %copy-start.3 = (bf16[320,768]{1,0:T(8,128)(2,1)S(1)}, bf16[320,768]{1,0:T(8,128)(2,1)}, u32[]{:S(2)}) copy-start(bf16[320,768]{1,0:T(8,128)(2,1)} %get-tuple-element.27.hidden_hbm.hidden_ref) | copy-start | bytes 1474564
  176.7 69.4 %all-to-all-start.2 = ((bf16[16,40,1024]{2,1,0:T(8,128)(2,1)}), bf16[16,40,1024]{2,1,0:T(8,128)(2,1)S(1)}, u32[]{:S(2)}, u32[]{:S(2)}) async-start(bf16[16,40,1024]{2,1,0:T(8,128)(2,1)} %bitcast.52), calls=%async_computation.2 | async-start | bytes 2621440 | tf_op jit(solution)/shard_map/all_to_all | solution.py:313
  188.8 10.2 %collective-permute-start.2 = (bf16[320,384]{1,0:T(8,128)(2,1)S(1)}, bf16[320,384]{1,0:T(8,128)(2,1)}, u32[]{:S(2)}, u32[]{:S(2)}) collective-permute-start(bf16[320,384]{1,0:T(8,128)(2,1)S(1)} %slice.52), channel_id=1, source_target_pairs={{0,1},{1,0},{64,65},{65,64},{128,129},{129,128},{192,193},{193,192... | collective-permute-start | bytes 737288 | tf_op jit(solution)/shard_map/ppermute | solution.py:270
  246.1 1.1 copy-start.6
  256.3 84.1 %all-to-all-start.3 = ((bf16[16,40,1024]{2,1,0:T(8,128)(2,1)}), bf16[16,40,1024]{2,1,0:T(8,128)(2,1)}, u32[]{:S(2)}, u32[]{:S(2)}) async-start(bf16[16,40,1024]{2,1,0:T(8,128)(2,1)} %bitcast.49), calls=%async_computation.3 | async-start | bytes 2621440 | tf_op jit(solution)/shard_map/all_to_all | solution.py:313
  268.3 0.9 copy-start.16
  268.3 67.3 %all-gather.7.cloned.1.call-start = ((), (), s32[]{:S(2)}) async-start(), calls=%async_computation.5 | async-start | bytes 3932160 | tf_op jit(solution)/shard_map/all_gather | solution.py:376
  283.5 19.4 %copy-start.2 = (bf16[320,2048]{1,0:T(8,128)(2,1)S(1)}, bf16[320,2048]{1,0:T(8,128)(2,1)}, u32[]{:S(2)}) copy-start(bf16[320,2048]{1,0:T(8,128)(2,1)} %get-tuple-element.34.rows_hbm) | copy-start | bytes 3932164
  283.5 19.4 %copy-start.4 = (bf16[320,768]{1,0:T(8,128)(2,1)S(1)}, bf16[320,768]{1,0:T(8,128)(2,1)}, u32[]{:S(2)}) copy-start(bf16[320,768]{1,0:T(8,128)(2,1)} %get-tuple-element.27.hidden_hbm.hidden_ref) | copy-start | bytes 1474564
  283.6 0.7 copy-start.10
  284.3 9.5 %collective-permute-start.4 = (f32[32,768]{1,0:T(8,128)S(1)}, f32[32,768]{1,0:T(8,128)}, u32[]{:S(2)}, u32[]{:S(2)}) collective-permute-start(f32[32,768]{1,0:T(8,128)S(1)} %slice_add_fusion.4), channel_id=1, source_target_pairs={{0,1},{1,0},{64,65},{65,64},{128,129},{129,128},{192,193},{193,192... | collective-permute-start | bytes 294920 | tf_op jit(solution)/shard_map/ppermute | solution.py:270
  289.1 11.8 %collective-permute-start.5 = (f32[32,768]{1,0:T(8,128)S(1)}, f32[32,768]{1,0:T(8,128)}, u32[]{:S(2)}, u32[]{:S(2)}) collective-permute-start(f32[32,768]{1,0:T(8,128)S(1)} %slice_add_fusion.4), channel_id=1, source_target_pairs={{0,257},{1,256},{64,321},{65,320},{128,385},{129,384},{192,449},{1... | collective-permute-start | bytes 294920 | tf_op jit(solution)/shard_map/ppermute | solution.py:270
  291.8 10.1 %collective-permute-start.3 = (f32[32,768]{1,0:T(8,128)S(1)}, f32[32,768]{1,0:T(8,128)S(1)}, u32[]{:S(2)}, u32[]{:S(2)}) collective-permute-start(f32[32,768]{1,0:T(8,128)S(1)} %slice_add_fusion.4), channel_id=1, source_target_pairs={{0,256},{1,257},{64,320},{65,321},{128,384},{129,385},{192,448},{1... | collective-permute-start | bytes 294920 | tf_op jit(solution)/shard_map/ppermute | solution.py:270
  307.4 4.2 %collective-permute-start.6 = (f32[32,1024]{1,0:T(8,128)S(1)}, f32[32,1024]{1,0:T(8,128)S(1)}, u32[]{:S(2)}, u32[]{:S(2)}) collective-permute-start(f32[32,1024]{1,0:T(8,128)S(1)} %get-tuple-element.36), channel_id=1, source_target_pairs={{0,32},{32,0},{1,33},{33,1},{2,34},{34,2},{3,35},{35,3},{4,36},{36... | collective-permute-start | bytes 393224 | tf_op jit(solution)/shard_map/ppermute | solution.py:407
  325.5 10.0 %collective-permute-start.7 = (f32[32,2048]{1,0:T(8,128)S(1)}, f32[32,2048]{1,0:T(8,128)S(1)}, u32[]{:S(2)}, u32[]{:S(2)}) collective-permute-start(f32[32,2048]{1,0:T(8,128)S(1)} %bitcast.53), channel_id=1, source_target_pairs={{0,256},{1,257},{64,320},{65,321},{128,384},{129,385},{192,448},{1... | collective-permute-start | bytes 786440 | tf_op jit(solution)/shard_map/ppermute | solution.py:270
  328.4 16.6 %collective-permute-start.9 = (f32[32,2048]{1,0:T(8,128)S(1)}, f32[32,2048]{1,0:T(8,128)}, u32[]{:S(2)}, u32[]{:S(2)}) collective-permute-start(f32[32,2048]{1,0:T(8,128)S(1)} %bitcast.54), channel_id=1, source_target_pairs={{0,257},{1,256},{64,321},{65,320},{128,385},{129,384},{192,449},{1... | collective-permute-start | bytes 786440 | tf_op jit(solution)/shard_map/ppermute | solution.py:270
  331.4 13.6 %collective-permute-start.8 = (f32[32,2048]{1,0:T(8,128)S(1)}, f32[32,2048]{1,0:T(8,128)}, u32[]{:S(2)}, u32[]{:S(2)}) collective-permute-start(f32[32,2048]{1,0:T(8,128)S(1)} %bitcast.55), channel_id=1, source_target_pairs={{0,1},{1,0},{64,65},{65,64},{128,129},{129,128},{192,193},{193,192... | collective-permute-start | bytes 786440 | tf_op jit(solution)/shard_map/ppermute | solution.py:270
  335.6 4.9 %copy-start.9 = (bf16[2,128,640]{2,1,0:T(8,128)(2,1)S(1)}, bf16[2,128,640]{2,1,0:T(8,128)(2,1)}, u32[]{:S(2)}) copy-start(bf16[2,128,640]{2,1,0:T(8,128)(2,1)} %copy-done.8) | copy-start | bytes 983044
  342.3 3.8 %copy-start.1 = (f32[384,2048]{1,0:T(8,128)S(1)}, f32[384,2048]{1,0:T(8,128)}, u32[]{:S(2)}) copy-start(f32[384,2048]{1,0:T(8,128)} %convert_add_fusion.merged_ref) | copy-start | bytes 9437188
  342.4 3.7 %copy-start.5 = (f32[32,384]{1,0:T(8,128)S(1)}, f32[32,384]{1,0:T(8,128)}, u32[]{:S(2)}) copy-start(f32[32,384]{1,0:T(8,128)} %get-tuple-element.39.basis_ref) | copy-start | bytes 147460
Sparse Core Ops, SparseCore 0:
  20.5 73.0 all-gather.4
  271.2 54.2 all-gather.6

commit v4 on v3

--- a/solution.py
+++ b/solution.py
@@ -12,6 +12,7 @@
 BF16, F32 = jnp.bfloat16, jnp.float32
 PIECES = 2
 BLOCK = 4
+BLOCKS = 3
 NN = ((1,), (0,))
 NT = ((1,), (1,))
 TN = ((0,), (0,))
@@ -256,13 +257,36 @@
     away_ref[...] = jnp.where(first, right[:, span:], right[:, :span])
 
 
-def error_kernel(merged_ref, basis_ref, right_ref, fresh_ref):
-    rank = right_ref.shape[0]
-    basis, right = thirds(basis_ref[...]), thirds(right_ref[...])
+def error_kernel(
+    replicas, place_ref, merged_ref, basis_ref, right_ref, near_ref, far_ref, both_ref, error_hbm,
+    fresh_hbm, factor_ref, error_ref, total_ref, fresh_ref, sems,
+):
+    rank, width = right_ref.shape
+    count = merged_ref.shape[0] // BLOCKS
+    arrivals = copies_of(blocks_of(error_hbm, count), blocks_of(error_ref, count), sems, 0)
+    results = copies_of(blocks_of(fresh_ref, count), blocks_of(fresh_hbm, count), sems, BLOCKS)
+    started(arrivals)
+    right, near, far, both = (
+        ref[...].astype(F32) for ref in (right_ref, near_ref, far_ref, both_ref)
+    )
+    total = ((right + near) + (far + both)) / replicas
+    total_ref[...] = total
+    span = width // replicas
+    start = pl.multiple_of(place_ref[1] * span, span)
+    columns = total_ref[:, pl.ds(start, span)]
+    factor_ref[...] = jnp.where(place_ref[0] == 0, columns[: rank // 2], columns[rank // 2 :])
+    basis, right = thirds(basis_ref[...]), thirds(total)
     high, middle = right[:rank], right[rank : 2 * rank]
     left = jnp.concatenate([basis[:rank], basis[:rank], basis[rank : 2 * rank]], axis=0)
-    approx = dot(left, jnp.concatenate([high, middle, high], axis=0), TN)
-    fresh_ref[...] = (merged_ref[...] - approx).astype(BF16)
+    terms = jnp.concatenate([high, middle, high], axis=0)
+    for i in range(BLOCKS):
+        part = slice(i * count, (i + 1) * count)
+        approx = dot(left[:, part], terms, TN)
+        arrivals[i].wait()
+        merged = merged_ref[part, :] + error_ref[part, :].astype(F32)
+        fresh_ref[part, :] = (merged - approx).astype(BF16)
+        results[i].start()
+    finished(results)
 
 
 def moved(value, mask):
@@ -344,7 +368,7 @@
         functools.partial(forward_kernel, blocks, capacity),
         [(unit_shape, BF16), ((slots, inner), BF16), ((slots, inner), F32), ((slots, inner), F32)],
         scratch,
-        inbox, weights, hbm=(0, 1), out_hbm=(0, 1, 2, 3), memory=58,
+        inbox, weights, hbm=(0, 1), out_hbm=(0, 1, 2, 3), memory=54,
     )
     returned = exchange(returned)
     picked = dot(select, returned, NN).reshape(PIECES, top, tok, piece)
@@ -354,7 +378,15 @@
     out_grad = (gate * slope[:, None]).astype(BF16).reshape(PIECES * top * tok, piece)
     grad_got = exchange(dot(select, out_grad, TN).astype(BF16))
     hidden_other = moved(hidden[:, hidden_half:], 1)
-    grad_got, hidden_other = lax.optimization_barrier((grad_got, hidden_other))
+    hidden_mine = hidden[:, :hidden_half]
+    hidden_all = jnp.concatenate(
+        [
+            jnp.where(half == 0, hidden_mine, hidden_other),
+            jnp.where(half == 0, hidden_other, hidden_mine),
+        ],
+        axis=0,
+    )
+    grad_got, hidden_all = lax.optimization_barrier((grad_got, hidden_all))
 
     token_part, rows, left = local_call(
         functools.partial(backward_kernel, blocks, capacity),
@@ -367,27 +399,18 @@
             pltpu.VMEM((rank, inner), F32),
         ],
         grad_got, act, act_slope, hidden, q_full, error_left, weights,
-        hbm=range(7), out_hbm=range(3), memory=58,
+        hbm=range(7), out_hbm=range(3), memory=52,
     )
     slot_grad = exchange(token_part)
     token_grad = dot(spread, slot_grad, NN).astype(BF16)
     token_grad = jnp.concatenate(jnp.split(token_grad, PIECES, axis=0), axis=1)
 
     rows_all = lax.all_gather(rows, "half", axis=0, tiled=True)
-    hidden_mine = hidden[:, :hidden_half]
-    hidden_all = jnp.concatenate(
-        [
-            jnp.where(half == 0, hidden_mine, hidden_other),
-            jnp.where(half == 0, hidden_other, hidden_mine),
-        ],
-        axis=0,
-    )
-
+
+    near, far, both = moved(left, 8), moved(left, 1), moved(left, 9)
+    away = far + both
+    left = (left + near) + jnp.concatenate([away[:, hidden_half:], away[:, :hidden_half]], axis=1)
     left = pairs_sum(lax.all_gather(left, ("across", "core")))
-    near, far, both = moved(left, 8), moved(left, 1), moved(left, 9)
-    left = left + near
-    away = far + both
-    left = left + jnp.concatenate([away[:, hidden_half:], away[:, :hidden_half]], axis=1)
     core = lax.axis_index("core")
     span = width // lax.axis_size("core")
     basis, right, right_away = local_call(
@@ -406,22 +429,27 @@
     )
     right = (right + lax.ppermute(right_away, "core", [(0, 1), (1, 0)])).astype(BF16)
     right = lax.all_gather(right, ("across", "core"))
-    right = pairs_sum(right.reshape(-1, 2, rank, span).astype(F32))
-    right = right.transpose(1, 0, 2).reshape(rank, width)
+    right = right.reshape(-1, 2, rank, span).astype(F32).sum(axis=0)
+    right = jnp.concatenate([right[0], right[1]], axis=1).astype(BF16)
     near, far, both = moved(right, 8), moved(right, 1), moved(right, 9)
-    merged = dot(hidden_all, rows_all, TN) + error.astype(F32)
+    merged = dot(hidden_all, rows_all, TN)
     replicas = lax.axis_size("along") * lax.axis_size("across") * lax.axis_size("core")
-    right, token_grad = lax.optimization_barrier((right + near, token_grad))
-    right = (right + (far + both)) / replicas
-    (new_error,) = local_call(
-        error_kernel, [((hidden_half, width), BF16)], [], merged, basis, right
-    )
-    q_columns = jnp.where(half == 0, right[: rank // 2], right[rank // 2 :])
+    near, token_grad = lax.optimization_barrier((near, token_grad))
     replica = lax.axis_index("along") * lax.axis_size("across") + lax.axis_index("across")
     replica = replica * lax.axis_size("core") + core
-    q_rows = width // replicas
-    q_factor = lax.dynamic_slice_in_dim(q_columns, replica * q_rows, q_rows, 1).T
-    return token_grad, basis.T, q_factor, new_error
+    new_error, q_factor = local_call(
+        functools.partial(error_kernel, replicas),
+        [((hidden_half, width), BF16), ((rank // 2, width // replicas), F32)],
+        [
+            pltpu.VMEM((hidden_half, width), BF16),
+            pltpu.VMEM((rank, width), F32),
+            pltpu.VMEM((hidden_half, width), BF16),
+            pltpu.SemaphoreType.DMA((2 * BLOCKS,)),
+        ],
+        jnp.stack([half, replica]), merged, basis, right, near, far, both, error,
+        smem=(0,), hbm=(7,), out_hbm=(0,),
+    )
+    return token_grad, basis.T, q_factor.T, new_error
 
 
 def solution(mesh):

time: 357 us -> 347 us (0.972)
  waiting for transfers between devices: 170 us -> 165 us
  other arithmetic: 11 us -> 6.58 us
    ppermute x9, waiting for transfers between devices: 16.5 us -> 11.1 us  [moved(): lax.ppermute(value, PLANE, [(source, source ^ mask) for source in range(c...]
  transfers between devices with their start and end apart: 16 -> 16, of which waited for: 8 -> 8; matrix products, arithmetic and copies ran while one was open for 5% -> 4% of each run, Pallas kernels for 1% -> 2%
where the time goes in v4:
time: 347 us; the launch traced here: 346 us
  waiting for transfers between devices  165 us (48%)
  starting transfers between devices  89.3 us (26%)
  blocking collectives  28.9 us (8%)
  Pallas kernels  25.8 us (7%)
  between operations  14.6 us (4%)
  matrix products  14.4 us (4%)
  other arithmetic  6.58 us (2%)
    all_to_all x4, waiting for transfers between devices, exchange(): lax.all_to_all(sent, 'expert', split_axis=0, concat_axis=0, tiled=True)  152 us
    all_to_all x4, starting transfers between devices, exchange(): lax.all_to_all(sent, 'expert', split_axis=0, concat_axis=0, tiled=True)  53.3 us
    ppermute x9, starting transfers between devices, moved(): lax.ppermute(value, PLANE, [(source, source ^ mask) for source in range(c...  33.8 us
    pallas_call x4, Pallas kernels, local_call(): pl.pallas_call(kernel, out_shape=[jax.ShapeDtypeStruct(shape, dtype) for...  25.8 us
    all_gather x1, blocking collectives, shards(): left = pairs_sum(lax.all_gather(left, ('across', 'core')))  15.8 us
    dot_general x6, matrix products, dot(): lax.dot_general(left, right, (dims, ((), ())), precision=precision, prefe...  14.4 us
    all_gather x1, blocking collectives, shards(): right = lax.all_gather(right, ('across', 'core'))  13.1 us
    ppermute x9, waiting for transfers between devices, moved(): lax.ppermute(value, PLANE, [(source, source ^ mask) for source in range(c...  11.1 us
  transfers between devices with their start and end apart: 16, of which 8 were waited for; matrix products, arithmetic and copies ran while one was open for 4% of the time, Pallas kernels for 2%

profile of v4, /device:TPU:1, one launch (start us, length us, event | category | flops | bytes accessed | tf_op | source)
XLA Modules:
  0.0 345.8 jit_solution(11032385723766131087)
XLA Ops:
  7.2 1.1 copy.25
  8.3 1.0 pad_maximum_fusion.4
  9.3 5.7 %collective-permute-start = (bf16[128,1152]{1,0:T(8,128)(2,1)S(1)}, bf16[128,1152]{1,0:T(8,128)(2,1)S(1)}, u32[]{:S(2)}, u32[]{:S(2)}) collective-permute-start(bf16[128,1152]{1,0:T(8,128)(2,1)S(1)} %pad_maximum_fusion.4), channel_id=1, source_target_pairs={{0,1},{1,0},{64,65},{65,64},{128,129},{129,128},{192,193},{193,192... | collective-permute-start | bytes 884744 | tf_op jit(solution)/shard_map/ppermute | solution.py:294
  14.9 0.7 convert_reduce_fusion
  15.6 0.1 copy.22
  15.7 0.2 reduce_window_sum.11
  16.0 0.7 select_reduce_fusion
  16.7 0.7 add_bitcast_fusion
  17.5 0.2 fusion.5
  17.6 0.2 copy.26
  17.9 1.6 convolution_convert_fusion
  19.5 0.9 pad_maximum_fusion
  20.4 17.0 %all-to-all-start = ((bf16[16,40,1024]{2,1,0:T(8,128)(2,1)}), bf16[16,40,1024]{2,1,0:T(8,128)(2,1)}, u32[]{:S(2)}, u32[]{:S(2)}) async-start(bf16[16,40,1024]{2,1,0:T(8,128)(2,1)} %bitcast.6), calls=%async_computation | async-start | bytes 2621440 | tf_op jit(solution)/shard_map/all_to_all | solution.py:337
  37.4 4.8 %collective-permute-start.1 = (f32[16,2048]{1,0:T(8,128)S(1)}, f32[16,2048]{1,0:T(8,128)S(1)}, u32[]{:S(2)}, u32[]{:S(2)}) collective-permute-start(f32[16,2048]{1,0:T(8,128)S(1)} %bitcast.56), channel_id=1, source_target_pairs={{0,1},{1,0},{64,65},{65,64},{128,129},{129,128},{192,193},{193,192... | collective-permute-start | bytes 393224 | tf_op jit(solution)/shard_map/ppermute | solution.py:294
  42.2 2.4 collective-permute-done.1
  44.7 1.4 fusion.12.error_left_hbm
  46.1 48.6 %all-to-all-done = bf16[16,40,1024]{2,1,0:T(8,128)(2,1)} async-done(((bf16[16,40,1024]{2,1,0:T(8,128)(2,1)}), bf16[16,40,1024]{2,1,0:T(8,128)(2,1)}, u32[]{:S(2)}, u32[]{:S(2)}) %all-to-all-start) | async-done | bytes 1310752 | tf_op jit(solution)/shard_map/all_to_all | solution.py:337
  94.7 8.3 %shard_map.120 = (bf16[640,1024]{1,0:T(8,128)(2,1)}, bf16[320,768]{1,0:T(8,128)(2,1)}, f32[320,768]{1,0:T(8,128)}, f32[320,768]{1,0:T(8,128)}) custom-call(bf16[640,1024]{1,0:T(8,128)(2,1)} %bitcast.7.got_hbm, bf16[2048,2304]{1,0:T(8,128)(2,1)} %all-gather.5.cloned.1.call-done.w_hbm), custom_call_target="tpu_custom_call" | custom-call | tf_op jit(solution)/shard_map/pallas_call | solution.py:48
  103.0 12.2 %all-to-all-start.1 = ((bf16[16,40,1024]{2,1,0:T(8,128)(2,1)}), bf16[16,40,1024]{2,1,0:T(8,128)(2,1)}, u32[]{:S(2)}, u32[]{:S(2)}) async-start(bf16[16,40,1024]{2,1,0:T(8,128)(2,1)} %bitcast.53), calls=%async_computation.1 | async-start | bytes 2621440 | tf_op jit(solution)/shard_map/all_to_all | solution.py:337
  115.3 57.3 %all-to-all-done.1 = bf16[16,40,1024]{2,1,0:T(8,128)(2,1)} async-done(((bf16[16,40,1024]{2,1,0:T(8,128)(2,1)}), bf16[16,40,1024]{2,1,0:T(8,128)(2,1)}, u32[]{:S(2)}, u32[]{:S(2)}) %all-to-all-start.1) | async-done | bytes 1310752 | tf_op jit(solution)/shard_map/all_to_all | solution.py:337
  172.6 2.5 multiply_reduce_fusion
  175.1 0.2 convert_subtract_fusion
  175.2 2.0 bitcast_convert_fusion
  177.2 12.1 %all-to-all-start.2 = ((bf16[16,40,1024]{2,1,0:T(8,128)(2,1)}), bf16[16,40,1024]{2,1,0:T(8,128)(2,1)}, u32[]{:S(2)}, u32[]{:S(2)}) async-start(bf16[16,40,1024]{2,1,0:T(8,128)(2,1)} %bitcast.52), calls=%async_computation.2 | async-start | bytes 2621440 | tf_op jit(solution)/shard_map/all_to_all | solution.py:337
  189.4 5.1 %collective-permute-start.2 = (bf16[320,384]{1,0:T(8,128)(2,1)S(1)}, bf16[320,384]{1,0:T(8,128)(2,1)S(1)}, u32[]{:S(2)}, u32[]{:S(2)}) collective-permute-start(bf16[320,384]{1,0:T(8,128)(2,1)S(1)} %slice.39), channel_id=1, source_target_pairs={{0,1},{1,0},{64,65},{65,64},{128,129},{129,128},{192,193},{193,192... | collective-permute-start | bytes 737288 | tf_op jit(solution)/shard_map/ppermute | solution.py:294
  194.5 5.2 %collective-permute-done.2 = bf16[320,384]{1,0:T(8,128)(2,1)S(1)} collective-permute-done((bf16[320,384]{1,0:T(8,128)(2,1)S(1)}, bf16[320,384]{1,0:T(8,128)(2,1)S(1)}, u32[]{:S(2)}, u32[]{:S(2)}) %collective-permute-start.2) | collective-permute-done | bytes 245792 | tf_op jit(solution)/shard_map/ppermute | solution.py:294
  199.8 0.8 pad_maximum_fusion.3
  200.6 46.1 %all-to-all-done.2 = bf16[16,40,1024]{2,1,0:T(8,128)(2,1)} async-done(((bf16[16,40,1024]{2,1,0:T(8,128)(2,1)}), bf16[16,40,1024]{2,1,0:T(8,128)(2,1)}, u32[]{:S(2)}, u32[]{:S(2)}) %all-to-all-start.2) | async-done | bytes 1310752 | tf_op jit(solution)/shard_map/all_to_all | solution.py:337
  246.8 8.7 %shard_map.121 = (bf16[640,1024]{1,0:T(8,128)(2,1)}, bf16[320,2048]{1,0:T(8,128)(2,1)}, f32[32,768]{1,0:T(8,128)S(1)}) custom-call(bf16[640,1024]{1,0:T(8,128)(2,1)} %bitcast.17.got_hbm, f32[320,768]{1,0:T(8,128)S(1)} %copy-done.4, f32[320,768]{1,0:T(8,128)} %get-tuple-element.32.slope_hbm, bf16[320,768]{1,0:T(8,128)(2,1)S(1)} %copy-done.3, ...), custom_call_target="tpu_custom_call" | custom-call | tf_op jit(solution)/shard_map/pallas_call | solution.py:48
  255.4 12.0 %all-to-all-start.3 = ((bf16[16,40,1024]{2,1,0:T(8,128)(2,1)}), bf16[16,40,1024]{2,1,0:T(8,128)(2,1)}, u32[]{:S(2)}, u32[]{:S(2)}) async-start(bf16[16,40,1024]{2,1,0:T(8,128)(2,1)} %bitcast.51), calls=%async_computation.3 | async-start | bytes 2621440 | tf_op jit(solution)/shard_map/all_to_all | solution.py:337
  267.5 4.6 %collective-permute-start.5 = (f32[32,768]{1,0:T(8,128)S(1)}, f32[32,768]{1,0:T(8,128)S(1)}, u32[]{:S(2)}, u32[]{:S(2)}) collective-permute-start(f32[32,768]{1,0:T(8,128)S(1)} %get-tuple-element.35), channel_id=1, source_target_pairs={{0,257},{1,256},{64,321},{65,320},{128,385},{129,384},{192,449},{1... | collective-permute-start | bytes 294920 | tf_op jit(solution)/shard_map/ppermute | solution.py:294
  272.1 2.2 collective-permute-start.4
  274.4 2.2 collective-permute-start.3
  276.6 2.8 collective-permute-done.4
  279.4 0.8 collective-permute-done.3
  280.2 15.8 %all-gather = f32[256,768]{1,0:T(8,128)S(1)} all-gather(f32[32,768]{1,0:T(8,128)S(1)} %maximum_add_fusion), channel_id=2, replica_groups=mesh['along'=2,'across'=4,'core'=2,'expert'=16,'half'=2] {'across','core'}, dimensions={0}, use_global_device_ids=true | all-gather | bytes 884736 | tf_op jit(solution)/shard_map/all_gather | solution.py:413
  296.1 5.2 %shard_map.122 = (f32[32,384]{1,0:T(8,128)}, f32[32,1024]{1,0:T(8,128)S(1)}, f32[32,1024]{1,0:T(8,128)}) custom-call(s32[1]{0:T(128)} %bitcast.core_ref, f32[32,768]{1,0:T(8,128)S(1)} %slice_add_fusion.2.left_ref, bf16[320,768]{1,0:T(8,128)(2,1)S(1)} %copy-done.3, bf16[320,2048]{1,0:T(8,128)(2,1)S(1)} %copy-done.2, bf16[384,2048]{1,0:T(8,128)(2,1)S(1)} %copy-done), custom_call_target="tpu_custom_call" | custom-call | tf_op jit(solution)/shard_map/pallas_call | solution.py:48
  301.3 2.2 collective-permute-start.6
  303.6 1.3 collective-permute-done.6
  304.9 13.1 %all-gather.1 = bf16[256,1024]{1,0:T(8,128)(2,1)S(1)} all-gather(bf16[32,1024]{1,0:T(8,128)(2,1)S(1)} %add_convert_fusion), channel_id=3, replica_groups=mesh['along'=2,'across'=4,'core'=2,'expert'=16,'half'=2] {'across','core'}, dimensions={0}, use_global_device_ids=true | all-gather | bytes 589824 | tf_op jit(solution)/shard_map/all_gather | solution.py:431
  318.1 0.1 reduce.1
  318.2 3.9 %collective-permute-start.9 = (bf16[32,2048]{1,0:T(8,128)(2,1)S(1)}, bf16[32,2048]{1,0:T(8,128)(2,1)S(1)}, u32[]{:S(2)}, u32[]{:S(2)}) collective-permute-start(bf16[32,2048]{1,0:T(8,128)(2,1)S(1)} %pad_maximum_fusion.6.right_ref), channel_id=1, source_target_pairs={{0,257},{1,256},{64,321},{65,320},{128,385},{129,384},{192,449},{1... | collective-permute-start | bytes 393224 | tf_op jit(solution)/shard_map/ppermute | solution.py:294
  322.1 2.6 collective-permute-start.8
  324.8 2.5 collective-permute-start.7
  327.4 4.9 %fusion.17.merged_ref = f32[384,2048]{1,0:T(8,128)} fusion(bf16[640,384]{1,0:T(8,128)(2,1)S(1)} %copy-done.8, bf16[640,2048]{1,0:T(8,128)(2,1)} %all-gather.7.cloned.1.call-done), kind=kOutput, calls=%fused_computation.49 | convolution fusion | flops 1006632960 | bytes 6258688 | tf_op jit(solution)/shard_map/dot_general | solution.py:24
  332.2 2.1 convolution_convert_fusion.1
  334.4 0.8 pad_maximum_fusion.2
  335.2 3.7 %shard_map.123 = (bf16[384,2048]{1,0:T(8,128)(2,1)}, f32[16,128]{1,0:T(8,128)}) custom-call(s32[2]{0:T(128)S(1)} %pad_add_fusion.place_ref, f32[384,2048]{1,0:T(8,128)S(1)} %copy-done.1, f32[32,384]{1,0:T(8,128)S(1)} %copy-done.5, bf16[32,2048]{1,0:T(8,128)(2,1)S(1)} %pad_maximum_fusion.6.right_ref, bf16[32,2048]{1,0:T(8,128)(2,1)S(1)} %collective-permute-done.7.near_ref, ...), custom_call_target="tpu_custom_call" | custom-call | tf_op jit(solution)/shard_map/pallas_call | solution.py:48
  (64 shorter events, 0.9 us)
Async XLA Ops:
  7.2 10.2 %copy-start.9 = (bf16[128,2048]{1,0:T(8,128)(2,1)S(1)}, bf16[128,2048]{1,0:T(8,128)(2,1)}, u32[]{:S(2)}) copy-start(bf16[128,2048]{1,0:T(8,128)(2,1)} %param.9) | copy-start | bytes 1572868
  7.2 87.5 %all-gather.5.cloned.1.call-start = ((), (), s32[]{:S(2)}) async-start(), calls=%async_computation.4 | async-start | bytes 10027008 | tf_op jit(solution)/shard_map/all_gather | solution.py:342
  9.3 10.2 %collective-permute-start = (bf16[128,1152]{1,0:T(8,128)(2,1)S(1)}, bf16[128,1152]{1,0:T(8,128)(2,1)S(1)}, u32[]{:S(2)}, u32[]{:S(2)}) collective-permute-start(bf16[128,1152]{1,0:T(8,128)(2,1)S(1)} %pad_maximum_fusion.4), channel_id=1, source_target_pairs={{0,1},{1,0},{64,65},{65,64},{128,129},{129,128},{192,193},{193,192... | collective-permute-start | bytes 884744 | tf_op jit(solution)/shard_map/ppermute | solution.py:294
  17.6 1.8 copy-start.11
  17.6 1.8 copy-start.12
  17.9 2.5 copy-start.6
  20.4 17.0 %copy-start.13 = (f32[2048,16]{0,1:T(8,128)S(1)}, f32[2048,16]{0,1:T(8,128)}, u32[]{:S(2)}) copy-start(f32[2048,16]{0,1:T(8,128)} %param.17) | copy-start | bytes 393220
  20.4 24.3 %copy-start = (bf16[384,2048]{1,0:T(8,128)(2,1)S(1)}, bf16[384,2048]{1,0:T(8,128)(2,1)}, u32[]{:S(2)}) copy-start(bf16[384,2048]{1,0:T(8,128)(2,1)} %error_hbm.3) | copy-start | bytes 4718596
  20.4 74.3 %all-to-all-start = ((bf16[16,40,1024]{2,1,0:T(8,128)(2,1)}), bf16[16,40,1024]{2,1,0:T(8,128)(2,1)}, u32[]{:S(2)}, u32[]{:S(2)}) async-start(bf16[16,40,1024]{2,1,0:T(8,128)(2,1)} %bitcast.6), calls=%async_computation | async-start | bytes 2621440 | tf_op jit(solution)/shard_map/all_to_all | solution.py:337
  37.4 7.2 %collective-permute-start.1 = (f32[16,2048]{1,0:T(8,128)S(1)}, f32[16,2048]{1,0:T(8,128)S(1)}, u32[]{:S(2)}, u32[]{:S(2)}) collective-permute-start(f32[16,2048]{1,0:T(8,128)S(1)} %bitcast.56), channel_id=1, source_target_pairs={{0,1},{1,0},{64,65},{65,64},{128,129},{129,128},{192,193},{193,192... | collective-permute-start | bytes 393224 | tf_op jit(solution)/shard_map/ppermute | solution.py:294
  103.0 12.2 %copy-start.10 = (bf16[128,2048]{1,0:T(8,128)(2,1)S(1)}, bf16[128,2048]{1,0:T(8,128)(2,1)}, u32[]{:S(2)}) copy-start(bf16[128,2048]{1,0:T(8,128)(2,1)} %param.10) | copy-start | bytes 1572868
  103.0 69.6 %all-to-all-start.1 = ((bf16[16,40,1024]{2,1,0:T(8,128)(2,1)}), bf16[16,40,1024]{2,1,0:T(8,128)(2,1)}, u32[]{:S(2)}, u32[]{:S(2)}) async-start(bf16[16,40,1024]{2,1,0:T(8,128)(2,1)} %bitcast.53), calls=%async_computation.1 | async-start | bytes 2621440 | tf_op jit(solution)/shard_map/all_to_all | solution.py:337
  115.2 57.4 %copy-start.14 = (f32[128,2]{0,1:T(2,128)S(1)}, f32[128,2]{0,1:T(2,128)}, u32[]{:S(2)}) copy-start(f32[128,2]{0,1:T(2,128)} %param.12) | copy-start | bytes 3076
  177.2 12.1 %copy-start.3 = (bf16[320,768]{1,0:T(8,128)(2,1)S(1)}, bf16[320,768]{1,0:T(8,128)(2,1)}, u32[]{:S(2)}) copy-start(bf16[320,768]{1,0:T(8,128)(2,1)} %get-tuple-element.29.hidden_hbm.hidden_ref) | copy-start | bytes 1474564
  177.2 69.5 %all-to-all-start.2 = ((bf16[16,40,1024]{2,1,0:T(8,128)(2,1)}), bf16[16,40,1024]{2,1,0:T(8,128)(2,1)}, u32[]{:S(2)}, u32[]{:S(2)}) async-start(bf16[16,40,1024]{2,1,0:T(8,128)(2,1)} %bitcast.52), calls=%async_computation.2 | async-start | bytes 2621440 | tf_op jit(solution)/shard_map/all_to_all | solution.py:337
  189.3 57.4 %copy-start.4 = (f32[320,768]{1,0:T(8,128)S(1)}, f32[320,768]{1,0:T(8,128)}, u32[]{:S(2)}) copy-start(f32[320,768]{1,0:T(8,128)} %get-tuple-element.31.act_hbm) | copy-start | bytes 2949124
  189.4 10.3 %collective-permute-start.2 = (bf16[320,384]{1,0:T(8,128)(2,1)S(1)}, bf16[320,384]{1,0:T(8,128)(2,1)S(1)}, u32[]{:S(2)}, u32[]{:S(2)}) collective-permute-start(bf16[320,384]{1,0:T(8,128)(2,1)S(1)} %slice.39), channel_id=1, source_target_pairs={{0,1},{1,0},{64,65},{65,64},{128,129},{129,128},{192,193},{193,192... | collective-permute-start | bytes 737288 | tf_op jit(solution)/shard_map/ppermute | solution.py:294
  255.4 76.8 %all-to-all-start.3 = ((bf16[16,40,1024]{2,1,0:T(8,128)(2,1)}), bf16[16,40,1024]{2,1,0:T(8,128)(2,1)}, u32[]{:S(2)}, u32[]{:S(2)}) async-start(bf16[16,40,1024]{2,1,0:T(8,128)(2,1)} %bitcast.51), calls=%async_computation.3 | async-start | bytes 2621440 | tf_op jit(solution)/shard_map/all_to_all | solution.py:337
  267.4 59.9 %all-gather.7.cloned.1.call-start = ((), (), s32[]{:S(2)}) async-start(), calls=%async_computation.5 | async-start | bytes 3932160 | tf_op jit(solution)/shard_map/all_gather | solution.py:408
  267.5 9.1 %collective-permute-start.5 = (f32[32,768]{1,0:T(8,128)S(1)}, f32[32,768]{1,0:T(8,128)S(1)}, u32[]{:S(2)}, u32[]{:S(2)}) collective-permute-start(f32[32,768]{1,0:T(8,128)S(1)} %get-tuple-element.35), channel_id=1, source_target_pairs={{0,257},{1,256},{64,321},{65,320},{128,385},{129,384},{192,449},{1... | collective-permute-start | bytes 294920 | tf_op jit(solution)/shard_map/ppermute | solution.py:294
  272.1 7.3 %collective-permute-start.4 = (f32[32,768]{1,0:T(8,128)S(1)}, f32[32,768]{1,0:T(8,128)S(1)}, u32[]{:S(2)}, u32[]{:S(2)}) collective-permute-start(f32[32,768]{1,0:T(8,128)S(1)} %get-tuple-element.35), channel_id=1, source_target_pairs={{0,1},{1,0},{64,65},{65,64},{128,129},{129,128},{192,193},{193,192... | collective-permute-start | bytes 294920 | tf_op jit(solution)/shard_map/ppermute | solution.py:294
  274.4 5.8 %collective-permute-start.3 = (f32[32,768]{1,0:T(8,128)S(1)}, f32[32,768]{1,0:T(8,128)S(1)}, u32[]{:S(2)}, u32[]{:S(2)}) collective-permute-start(f32[32,768]{1,0:T(8,128)S(1)} %get-tuple-element.35), channel_id=1, source_target_pairs={{0,256},{1,257},{64,320},{65,321},{128,384},{129,385},{192,448},{1... | collective-permute-start | bytes 294920 | tf_op jit(solution)/shard_map/ppermute | solution.py:294
  280.2 15.9 %copy-start.2 = (bf16[320,2048]{1,0:T(8,128)(2,1)S(1)}, bf16[320,2048]{1,0:T(8,128)(2,1)}, u32[]{:S(2)}) copy-start(bf16[320,2048]{1,0:T(8,128)(2,1)} %get-tuple-element.36.rows_hbm) | copy-start | bytes 3932164
  301.3 26.0 %copy-start.8 = (bf16[640,384]{1,0:T(8,128)(2,1)S(1)}, bf16[640,384]{1,0:T(8,128)(2,1)}, u32[]{:S(2)}) copy-start(bf16[640,384]{1,0:T(8,128)(2,1)} %pad_maximum_fusion.3) | copy-start | bytes 1474564
  301.3 3.6 %collective-permute-start.6 = (f32[32,1024]{1,0:T(8,128)}, f32[32,1024]{1,0:T(8,128)S(1)}, u32[]{:S(2)}, u32[]{:S(2)}) collective-permute-start(f32[32,1024]{1,0:T(8,128)} %get-tuple-element.38), channel_id=1, source_target_pairs={{0,32},{32,0},{1,33},{33,1},{2,34},{34,2},{3,35},{35,3},{4,36},{36... | collective-permute-start | bytes 393224 | tf_op jit(solution)/shard_map/ppermute | solution.py:430
  318.2 14.1 %copy-start.7 = (bf16[2,128,640]{2,1,0:T(8,128)(2,1)S(1)}, bf16[2,128,640]{2,1,0:T(8,128)(2,1)}, u32[]{:S(2)}) copy-start(bf16[2,128,640]{2,1,0:T(8,128)(2,1)} %copy-done.6) | copy-start | bytes 983044
  318.2 17.0 %collective-permute-start.9 = (bf16[32,2048]{1,0:T(8,128)(2,1)S(1)}, bf16[32,2048]{1,0:T(8,128)(2,1)S(1)}, u32[]{:S(2)}, u32[]{:S(2)}) collective-permute-start(bf16[32,2048]{1,0:T(8,128)(2,1)S(1)} %pad_maximum_fusion.6.right_ref), channel_id=1, source_target_pairs={{0,257},{1,256},{64,321},{65,320},{128,385},{129,384},{192,449},{1... | collective-permute-start | bytes 393224 | tf_op jit(solution)/shard_map/ppermute | solution.py:294
  322.1 13.1 %collective-permute-start.8 = (bf16[32,2048]{1,0:T(8,128)(2,1)S(1)}, bf16[32,2048]{1,0:T(8,128)(2,1)S(1)}, u32[]{:S(2)}, u32[]{:S(2)}) collective-permute-start(bf16[32,2048]{1,0:T(8,128)(2,1)S(1)} %pad_maximum_fusion.6.right_ref), channel_id=1, source_target_pairs={{0,1},{1,0},{64,65},{65,64},{128,129},{129,128},{192,193},{193,192... | collective-permute-start | bytes 393224 | tf_op jit(solution)/shard_map/ppermute | solution.py:294
  324.8 10.4 %collective-permute-start.7 = (bf16[32,2048]{1,0:T(8,128)(2,1)S(1)}, bf16[32,2048]{1,0:T(8,128)(2,1)S(1)}, u32[]{:S(2)}, u32[]{:S(2)}) collective-permute-start(bf16[32,2048]{1,0:T(8,128)(2,1)S(1)} %pad_maximum_fusion.6.right_ref), channel_id=1, source_target_pairs={{0,256},{1,257},{64,320},{65,321},{128,384},{129,385},{192,448},{1... | collective-permute-start | bytes 393224 | tf_op jit(solution)/shard_map/ppermute | solution.py:294
  332.2 3.0 copy-start.1
  334.3 0.9 copy-start.5
Sparse Core Ops, SparseCore 0:
  20.5 73.1 all-gather.4
  274.5 52.4 all-gather.6

commit v5 on v4

--- a/solution.py
+++ b/solution.py
@@ -232,17 +232,15 @@
     rank = left.shape[0]
     half = left.shape[1] // 2
     gram = dot(left, left, NT, HIGHEST)
-    row_ids = lax.broadcasted_iota(jnp.int32, (rank, rank), 0)
-    inverse = jnp.where(
-        row_ids == lax.broadcasted_iota(jnp.int32, (rank, rank), 1), 1.0, 0.0
-    ).astype(F32)
-    for k in range(rank):
-        scale = 1.0 / jnp.sqrt(gram[k : k + 1, k : k + 1])
-        gram_row = gram[k : k + 1, :] * scale
-        inverse_row = inverse[k : k + 1, :] * scale
-        below = jnp.where(row_ids > k, gram[:, k : k + 1] * scale, 0.0)
-        gram = gram - below * gram_row
-        inverse = jnp.where(row_ids == k, inverse_row, inverse - below * inverse_row)
+    row_ids = lax.broadcasted_iota(jnp.int32, (rank, 2 * rank), 0)
+    column_ids = lax.broadcasted_iota(jnp.int32, (rank, 2 * rank), 1)
+    identity = jnp.where(row_ids + rank == column_ids, 1.0, 0.0).astype(F32)
+    work = jnp.concatenate([gram, identity[:, rank:]], axis=1)
+    for k in range(rank - 1):
+        below = work[:, k : k + 1] / work[k : k + 1, k : k + 1]
+        work = work - jnp.where(row_ids > k, below * work[k : k + 1, :], 0.0)
+    pivots = jnp.sum(jnp.where(row_ids == column_ids, work, 0.0), axis=1, keepdims=True)
+    inverse = work[:, rank:] / jnp.sqrt(pivots)
     basis = dot(inverse, left, NN, HIGHEST)
     mine = basis[:, :half]
     basis_ref[...] = mine
@@ -258,11 +256,11 @@
 
 
 def error_kernel(
-    replicas, place_ref, merged_ref, basis_ref, right_ref, near_ref, far_ref, both_ref, error_hbm,
+    replicas, place_ref, grad_ref, basis_ref, right_ref, near_ref, far_ref, both_ref, error_hbm,
     fresh_hbm, factor_ref, error_ref, total_ref, fresh_ref, sems,
 ):
     rank, width = right_ref.shape
-    count = merged_ref.shape[0] // BLOCKS
+    count = grad_ref.shape[0] // BLOCKS
     arrivals = copies_of(blocks_of(error_hbm, count), blocks_of(error_ref, count), sems, 0)
     results = copies_of(blocks_of(fresh_ref, count), blocks_of(fresh_hbm, count), sems, BLOCKS)
     started(arrivals)
@@ -283,7 +281,7 @@
         part = slice(i * count, (i + 1) * count)
         approx = dot(left[:, part], terms, TN)
         arrivals[i].wait()
-        merged = merged_ref[part, :] + error_ref[part, :].astype(F32)
+        merged = grad_ref[part, :].astype(F32) + error_ref[part, :].astype(F32)
         fresh_ref[part, :] = (merged - approx).astype(BF16)
         results[i].start()
     finished(results)
@@ -432,7 +430,7 @@
     right = right.reshape(-1, 2, rank, span).astype(F32).sum(axis=0)
     right = jnp.concatenate([right[0], right[1]], axis=1).astype(BF16)
     near, far, both = moved(right, 8), moved(right, 1), moved(right, 9)
-    merged = dot(hidden_all, rows_all, TN)
+    weight_grad = dot(hidden_all, rows_all, TN).astype(BF16)
     replicas = lax.axis_size("along") * lax.axis_size("across") * lax.axis_size("core")
     near, token_grad = lax.optimization_barrier((near, token_grad))
     replica = lax.axis_index("along") * lax.axis_size("across") + lax.axis_index("across")
@@ -446,7 +444,7 @@
             pltpu.VMEM((hidden_half, width), BF16),
             pltpu.SemaphoreType.DMA((2 * BLOCKS,)),
         ],
-        jnp.stack([half, replica]), merged, basis, right, near, far, both, error,
+        jnp.stack([half, replica]), weight_grad, basis, right, near, far, both, error,
         smem=(0,), hbm=(7,), out_hbm=(0,),
     )
     return token_grad, basis.T, q_factor.T, new_error

time: 347 us -> 345 us (level)
  transfers between devices with their start and end apart: 16 -> 16, of which waited for: 8 -> 9; matrix products, arithmetic and copies ran while one was open for 4% -> 4% of each run, Pallas kernels for 2% -> 1%
where the time goes in v5:
time: 345 us; the launch traced here: 344 us
  waiting for transfers between devices  165 us (48%)
  starting transfers between devices  89.1 us (26%)
  blocking collectives  28.9 us (8%)
  Pallas kernels  25.8 us (7%)
  between operations  14.5 us (4%)
  matrix products  12.8 us (4%)
  other arithmetic  6.56 us (2%)
    all_to_all x4, waiting for transfers between devices, exchange(): lax.all_to_all(sent, 'expert', split_axis=0, concat_axis=0, tiled=True)  152 us
    all_to_all x4, starting transfers between devices, exchange(): lax.all_to_all(sent, 'expert', split_axis=0, concat_axis=0, tiled=True)  53.3 us
    ppermute x9, starting transfers between devices, moved(): lax.ppermute(value, PLANE, [(source, source ^ mask) for source in range(c...  33.6 us
    pallas_call x4, Pallas kernels, local_call(): pl.pallas_call(kernel, out_shape=[jax.ShapeDtypeStruct(shape, dtype) for...  25.8 us
    all_gather x1, blocking collectives, shards(): left = pairs_sum(lax.all_gather(left, ('across', 'core')))  15.8 us
    all_gather x1, blocking collectives, shards(): right = lax.all_gather(right, ('across', 'core'))  13.1 us
    dot_general x6, matrix products, dot(): lax.dot_general(left, right, (dims, ((), ())), precision=precision, prefe...  12.8 us
    ppermute x9, waiting for transfers between devices, moved(): lax.ppermute(value, PLANE, [(source, source ^ mask) for source in range(c...  11.1 us
  transfers between devices with their start and end apart: 16, of which 9 were waited for; matrix products, arithmetic and copies ran while one was open for 4% of the time, Pallas kernels for 1%

profile of v5, /device:TPU:1, one launch (start us, length us, event | category | flops | bytes accessed | tf_op | source)
XLA Modules:
  0.0 344.1 jit_solution(17962794889218083931)
XLA Ops:
  7.2 1.1 copy.25
  8.3 1.0 pad_maximum_fusion.4
  9.3 5.7 %collective-permute-start = (bf16[128,1152]{1,0:T(8,128)(2,1)S(1)}, bf16[128,1152]{1,0:T(8,128)(2,1)S(1)}, u32[]{:S(2)}, u32[]{:S(2)}) collective-permute-start(bf16[128,1152]{1,0:T(8,128)(2,1)S(1)} %pad_maximum_fusion.4), channel_id=1, source_target_pairs={{0,1},{1,0},{64,65},{65,64},{128,129},{129,128},{192,193},{193,192... | collective-permute-start | bytes 884744 | tf_op jit(solution)/shard_map/ppermute | solution.py:292
  14.9 0.7 convert_reduce_fusion
  15.6 0.1 copy.22
  15.7 0.2 reduce_window_sum.11
  16.0 0.7 select_reduce_fusion
  16.7 0.7 add_bitcast_fusion
  17.5 0.2 fusion.5
  17.6 0.2 copy.26
  17.9 1.6 convolution_convert_fusion.1
  19.5 0.8 pad_maximum_fusion
  20.4 17.0 %all-to-all-start = ((bf16[16,40,1024]{2,1,0:T(8,128)(2,1)}), bf16[16,40,1024]{2,1,0:T(8,128)(2,1)}, u32[]{:S(2)}, u32[]{:S(2)}) async-start(bf16[16,40,1024]{2,1,0:T(8,128)(2,1)} %bitcast.6), calls=%async_computation | async-start | bytes 2621440 | tf_op jit(solution)/shard_map/all_to_all | solution.py:335
  37.4 4.8 %collective-permute-start.1 = (f32[16,2048]{1,0:T(8,128)S(1)}, f32[16,2048]{1,0:T(8,128)S(1)}, u32[]{:S(2)}, u32[]{:S(2)}) collective-permute-start(f32[16,2048]{1,0:T(8,128)S(1)} %bitcast.56), channel_id=1, source_target_pairs={{0,1},{1,0},{64,65},{65,64},{128,129},{129,128},{192,193},{193,192... | collective-permute-start | bytes 393224 | tf_op jit(solution)/shard_map/ppermute | solution.py:292
  42.2 2.4 collective-permute-done.1
  44.7 1.4 fusion.12.error_left_hbm
  46.1 48.6 %all-to-all-done = bf16[16,40,1024]{2,1,0:T(8,128)(2,1)} async-done(((bf16[16,40,1024]{2,1,0:T(8,128)(2,1)}), bf16[16,40,1024]{2,1,0:T(8,128)(2,1)}, u32[]{:S(2)}, u32[]{:S(2)}) %all-to-all-start) | async-done | bytes 1310752 | tf_op jit(solution)/shard_map/all_to_all | solution.py:335
  94.7 8.2 %shard_map.120 = (bf16[640,1024]{1,0:T(8,128)(2,1)}, bf16[320,768]{1,0:T(8,128)(2,1)}, f32[320,768]{1,0:T(8,128)}, f32[320,768]{1,0:T(8,128)}) custom-call(bf16[640,1024]{1,0:T(8,128)(2,1)} %bitcast.7.got_hbm, bf16[2048,2304]{1,0:T(8,128)(2,1)} %all-gather.5.cloned.1.call-done.w_hbm), custom_call_target="tpu_custom_call" | custom-call | tf_op jit(solution)/shard_map/pallas_call | solution.py:48
  102.9 12.2 %all-to-all-start.1 = ((bf16[16,40,1024]{2,1,0:T(8,128)(2,1)}), bf16[16,40,1024]{2,1,0:T(8,128)(2,1)}, u32[]{:S(2)}, u32[]{:S(2)}) async-start(bf16[16,40,1024]{2,1,0:T(8,128)(2,1)} %bitcast.53), calls=%async_computation.1 | async-start | bytes 2621440 | tf_op jit(solution)/shard_map/all_to_all | solution.py:335
  115.3 57.3 %all-to-all-done.1 = bf16[16,40,1024]{2,1,0:T(8,128)(2,1)} async-done(((bf16[16,40,1024]{2,1,0:T(8,128)(2,1)}), bf16[16,40,1024]{2,1,0:T(8,128)(2,1)}, u32[]{:S(2)}, u32[]{:S(2)}) %all-to-all-start.1) | async-done | bytes 1310752 | tf_op jit(solution)/shard_map/all_to_all | solution.py:335
  172.6 2.5 multiply_reduce_fusion
  175.1 0.2 convert_subtract_fusion
  175.2 2.0 bitcast_convert_fusion
  177.2 12.1 %all-to-all-start.2 = ((bf16[16,40,1024]{2,1,0:T(8,128)(2,1)}), bf16[16,40,1024]{2,1,0:T(8,128)(2,1)}, u32[]{:S(2)}, u32[]{:S(2)}) async-start(bf16[16,40,1024]{2,1,0:T(8,128)(2,1)} %bitcast.52), calls=%async_computation.2 | async-start | bytes 2621440 | tf_op jit(solution)/shard_map/all_to_all | solution.py:335
  189.4 5.1 %collective-permute-start.2 = (bf16[320,384]{1,0:T(8,128)(2,1)S(1)}, bf16[320,384]{1,0:T(8,128)(2,1)S(1)}, u32[]{:S(2)}, u32[]{:S(2)}) collective-permute-start(bf16[320,384]{1,0:T(8,128)(2,1)S(1)} %slice.39), channel_id=1, source_target_pairs={{0,1},{1,0},{64,65},{65,64},{128,129},{129,128},{192,193},{193,192... | collective-permute-start | bytes 737288 | tf_op jit(solution)/shard_map/ppermute | solution.py:292
  194.5 5.2 %collective-permute-done.2 = bf16[320,384]{1,0:T(8,128)(2,1)S(1)} collective-permute-done((bf16[320,384]{1,0:T(8,128)(2,1)S(1)}, bf16[320,384]{1,0:T(8,128)(2,1)S(1)}, u32[]{:S(2)}, u32[]{:S(2)}) %collective-permute-start.2) | collective-permute-done | bytes 245792 | tf_op jit(solution)/shard_map/ppermute | solution.py:292
  199.8 0.8 pad_maximum_fusion.3
  200.6 46.1 %all-to-all-done.2 = bf16[16,40,1024]{2,1,0:T(8,128)(2,1)} async-done(((bf16[16,40,1024]{2,1,0:T(8,128)(2,1)}), bf16[16,40,1024]{2,1,0:T(8,128)(2,1)}, u32[]{:S(2)}, u32[]{:S(2)}) %all-to-all-start.2) | async-done | bytes 1310752 | tf_op jit(solution)/shard_map/all_to_all | solution.py:335
  246.7 8.7 %shard_map.121 = (bf16[640,1024]{1,0:T(8,128)(2,1)}, bf16[320,2048]{1,0:T(8,128)(2,1)}, f32[32,768]{1,0:T(8,128)S(1)}) custom-call(bf16[640,1024]{1,0:T(8,128)(2,1)} %bitcast.17.got_hbm, f32[320,768]{1,0:T(8,128)S(1)} %copy-done.3, f32[320,768]{1,0:T(8,128)} %get-tuple-element.32.slope_hbm, bf16[320,768]{1,0:T(8,128)(2,1)S(1)} %copy-done.2, ...), custom_call_target="tpu_custom_call" | custom-call | tf_op jit(solution)/shard_map/pallas_call | solution.py:48
  255.4 12.0 %all-to-all-start.3 = ((bf16[16,40,1024]{2,1,0:T(8,128)(2,1)}), bf16[16,40,1024]{2,1,0:T(8,128)(2,1)}, u32[]{:S(2)}, u32[]{:S(2)}) async-start(bf16[16,40,1024]{2,1,0:T(8,128)(2,1)} %bitcast.51), calls=%async_computation.3 | async-start | bytes 2621440 | tf_op jit(solution)/shard_map/all_to_all | solution.py:335
  267.4 4.6 %collective-permute-start.5 = (f32[32,768]{1,0:T(8,128)S(1)}, f32[32,768]{1,0:T(8,128)S(1)}, u32[]{:S(2)}, u32[]{:S(2)}) collective-permute-start(f32[32,768]{1,0:T(8,128)S(1)} %get-tuple-element.35), channel_id=1, source_target_pairs={{0,257},{1,256},{64,321},{65,320},{128,385},{129,384},{192,449},{1... | collective-permute-start | bytes 294920 | tf_op jit(solution)/shard_map/ppermute | solution.py:292
  272.1 2.3 collective-permute-start.4
  274.4 2.2 collective-permute-start.3
  276.6 2.8 collective-permute-done.4
  279.4 0.8 collective-permute-done.3
  280.2 15.8 %all-gather = f32[256,768]{1,0:T(8,128)S(1)} all-gather(f32[32,768]{1,0:T(8,128)S(1)} %maximum_add_fusion), channel_id=2, replica_groups=mesh['along'=2,'across'=4,'core'=2,'expert'=16,'half'=2] {'across','core'}, dimensions={0}, use_global_device_ids=true | all-gather | bytes 884736 | tf_op jit(solution)/shard_map/all_gather | solution.py:411
  296.1 4.9 %shard_map.122 = (f32[32,384]{1,0:T(8,128)}, f32[32,1024]{1,0:T(8,128)S(1)}, f32[32,1024]{1,0:T(8,128)}) custom-call(s32[1]{0:T(128)} %bitcast.core_ref, f32[32,768]{1,0:T(8,128)S(1)} %slice_add_fusion.2.left_ref, bf16[320,768]{1,0:T(8,128)(2,1)S(1)} %copy-done.2, bf16[320,2048]{1,0:T(8,128)(2,1)S(1)} %copy-done.1, bf16[384,2048]{1,0:T(8,128)(2,1)S(1)} %copy-done), custom_call_target="tpu_custom_call" | custom-call | tf_op jit(solution)/shard_map/pallas_call | solution.py:48
  301.0 2.1 collective-permute-start.6
  303.1 1.3 collective-permute-done.6
  304.4 13.1 %all-gather.1 = bf16[256,1024]{1,0:T(8,128)(2,1)S(1)} all-gather(bf16[32,1024]{1,0:T(8,128)(2,1)S(1)} %add_convert_fusion), channel_id=3, replica_groups=mesh['along'=2,'across'=4,'core'=2,'expert'=16,'half'=2] {'across','core'}, dimensions={0}, use_global_device_ids=true | all-gather | bytes 589824 | tf_op jit(solution)/shard_map/all_gather | solution.py:429
  317.7 3.8 %collective-permute-start.9 = (bf16[32,2048]{1,0:T(8,128)(2,1)S(1)}, bf16[32,2048]{1,0:T(8,128)(2,1)S(1)}, u32[]{:S(2)}, u32[]{:S(2)}) collective-permute-start(bf16[32,2048]{1,0:T(8,128)(2,1)S(1)} %pad_maximum_fusion.6.right_ref), channel_id=1, source_target_pairs={{0,257},{1,256},{64,321},{65,320},{128,385},{129,384},{192,449},{1... | collective-permute-start | bytes 393224 | tf_op jit(solution)/shard_map/ppermute | solution.py:292
  321.5 2.6 collective-permute-start.8
  324.1 2.5 collective-permute-start.7
  326.7 0.3 all-gather.7.cloned.1.call-done
  327.0 3.3 convolution_convert_fusion.grad_ref
  330.3 2.0 convolution_convert_fusion.2
  332.4 0.8 pad_maximum_fusion.2
  333.2 4.0 %shard_map.123 = (bf16[384,2048]{1,0:T(8,128)(2,1)}, f32[16,128]{1,0:T(8,128)}) custom-call(s32[2]{0:T(128)S(1)} %pad_add_fusion.place_ref, bf16[384,2048]{1,0:T(8,128)(2,1)S(1)} %convolution_convert_fusion.grad_ref, f32[32,384]{1,0:T(8,128)S(1)} %copy-done.4, bf16[32,2048]{1,0:T(8,128)(2,1)S(1)} %pad_maximum_fusion.6.right_ref, ...), custom_call_target="tpu_custom_call" | custom-call | tf_op jit(solution)/shard_map/pallas_call | solution.py:48
  (58 shorter events, 0.9 us)
Async XLA Ops:
  7.2 10.2 %copy-start.6 = (bf16[128,2048]{1,0:T(8,128)(2,1)S(1)}, bf16[128,2048]{1,0:T(8,128)(2,1)}, u32[]{:S(2)}) copy-start(bf16[128,2048]{1,0:T(8,128)(2,1)} %param.9) | copy-start | bytes 1572868
  7.2 87.5 %all-gather.5.cloned.1.call-start = ((), (), s32[]{:S(2)}) async-start(), calls=%async_computation.4 | async-start | bytes 10027008 | tf_op jit(solution)/shard_map/all_gather | solution.py:340
  9.3 10.2 %collective-permute-start = (bf16[128,1152]{1,0:T(8,128)(2,1)S(1)}, bf16[128,1152]{1,0:T(8,128)(2,1)S(1)}, u32[]{:S(2)}, u32[]{:S(2)}) collective-permute-start(bf16[128,1152]{1,0:T(8,128)(2,1)S(1)} %pad_maximum_fusion.4), channel_id=1, source_target_pairs={{0,1},{1,0},{64,65},{65,64},{128,129},{129,128},{192,193},{193,192... | collective-permute-start | bytes 884744 | tf_op jit(solution)/shard_map/ppermute | solution.py:292
  17.6 1.8 copy-start.8
  17.6 1.8 copy-start.9
  17.9 2.5 copy-start.5
  20.3 17.0 %copy-start.10 = (f32[2048,16]{0,1:T(8,128)S(1)}, f32[2048,16]{0,1:T(8,128)}, u32[]{:S(2)}) copy-start(f32[2048,16]{0,1:T(8,128)} %param.17) | copy-start | bytes 393220
  20.4 24.3 %copy-start = (bf16[384,2048]{1,0:T(8,128)(2,1)S(1)}, bf16[384,2048]{1,0:T(8,128)(2,1)}, u32[]{:S(2)}) copy-start(bf16[384,2048]{1,0:T(8,128)(2,1)} %error_hbm.3) | copy-start | bytes 4718596
  20.4 74.3 %all-to-all-start = ((bf16[16,40,1024]{2,1,0:T(8,128)(2,1)}), bf16[16,40,1024]{2,1,0:T(8,128)(2,1)}, u32[]{:S(2)}, u32[]{:S(2)}) async-start(bf16[16,40,1024]{2,1,0:T(8,128)(2,1)} %bitcast.6), calls=%async_computation | async-start | bytes 2621440 | tf_op jit(solution)/shard_map/all_to_all | solution.py:335
  37.4 7.2 %collective-permute-start.1 = (f32[16,2048]{1,0:T(8,128)S(1)}, f32[16,2048]{1,0:T(8,128)S(1)}, u32[]{:S(2)}, u32[]{:S(2)}) collective-permute-start(f32[16,2048]{1,0:T(8,128)S(1)} %bitcast.56), channel_id=1, source_target_pairs={{0,1},{1,0},{64,65},{65,64},{128,129},{129,128},{192,193},{193,192... | collective-permute-start | bytes 393224 | tf_op jit(solution)/shard_map/ppermute | solution.py:292
  102.9 12.2 %copy-start.7 = (bf16[128,2048]{1,0:T(8,128)(2,1)S(1)}, bf16[128,2048]{1,0:T(8,128)(2,1)}, u32[]{:S(2)}) copy-start(bf16[128,2048]{1,0:T(8,128)(2,1)} %param.10) | copy-start | bytes 1572868
  102.9 69.6 %all-to-all-start.1 = ((bf16[16,40,1024]{2,1,0:T(8,128)(2,1)}), bf16[16,40,1024]{2,1,0:T(8,128)(2,1)}, u32[]{:S(2)}, u32[]{:S(2)}) async-start(bf16[16,40,1024]{2,1,0:T(8,128)(2,1)} %bitcast.53), calls=%async_computation.1 | async-start | bytes 2621440 | tf_op jit(solution)/shard_map/all_to_all | solution.py:335
  115.2 57.4 %copy-start.11 = (f32[128,2]{0,1:T(2,128)S(1)}, f32[128,2]{0,1:T(2,128)}, u32[]{:S(2)}) copy-start(f32[128,2]{0,1:T(2,128)} %param.12) | copy-start | bytes 3076
  177.2 12.1 %copy-start.2 = (bf16[320,768]{1,0:T(8,128)(2,1)S(1)}, bf16[320,768]{1,0:T(8,128)(2,1)}, u32[]{:S(2)}) copy-start(bf16[320,768]{1,0:T(8,128)(2,1)} %get-tuple-element.29.hidden_hbm.hidden_ref) | copy-start | bytes 1474564
  177.2 69.5 %all-to-all-start.2 = ((bf16[16,40,1024]{2,1,0:T(8,128)(2,1)}), bf16[16,40,1024]{2,1,0:T(8,128)(2,1)}, u32[]{:S(2)}, u32[]{:S(2)}) async-start(bf16[16,40,1024]{2,1,0:T(8,128)(2,1)} %bitcast.52), calls=%async_computation.2 | async-start | bytes 2621440 | tf_op jit(solution)/shard_map/all_to_all | solution.py:335
  189.3 57.4 %copy-start.3 = (f32[320,768]{1,0:T(8,128)S(1)}, f32[320,768]{1,0:T(8,128)}, u32[]{:S(2)}) copy-start(f32[320,768]{1,0:T(8,128)} %get-tuple-element.31.act_hbm) | copy-start | bytes 2949124
  189.4 10.3 %collective-permute-start.2 = (bf16[320,384]{1,0:T(8,128)(2,1)S(1)}, bf16[320,384]{1,0:T(8,128)(2,1)S(1)}, u32[]{:S(2)}, u32[]{:S(2)}) collective-permute-start(bf16[320,384]{1,0:T(8,128)(2,1)S(1)} %slice.39), channel_id=1, source_target_pairs={{0,1},{1,0},{64,65},{65,64},{128,129},{129,128},{192,193},{193,192... | collective-permute-start | bytes 737288 | tf_op jit(solution)/shard_map/ppermute | solution.py:292
  255.4 74.9 %all-to-all-start.3 = ((bf16[16,40,1024]{2,1,0:T(8,128)(2,1)}), bf16[16,40,1024]{2,1,0:T(8,128)(2,1)}, u32[]{:S(2)}, u32[]{:S(2)}) async-start(bf16[16,40,1024]{2,1,0:T(8,128)(2,1)} %bitcast.51), calls=%async_computation.3 | async-start | bytes 2621440 | tf_op jit(solution)/shard_map/all_to_all | solution.py:335
  267.4 59.6 %all-gather.7.cloned.1.call-start = ((), (), s32[]{:S(2)}) async-start(), calls=%async_computation.5 | async-start | bytes 3932160 | tf_op jit(solution)/shard_map/all_gather | solution.py:406
  267.4 9.1 %collective-permute-start.5 = (f32[32,768]{1,0:T(8,128)S(1)}, f32[32,768]{1,0:T(8,128)S(1)}, u32[]{:S(2)}, u32[]{:S(2)}) collective-permute-start(f32[32,768]{1,0:T(8,128)S(1)} %get-tuple-element.35), channel_id=1, source_target_pairs={{0,257},{1,256},{64,321},{65,320},{128,385},{129,384},{192,449},{1... | collective-permute-start | bytes 294920 | tf_op jit(solution)/shard_map/ppermute | solution.py:292
  272.1 7.3 %collective-permute-start.4 = (f32[32,768]{1,0:T(8,128)S(1)}, f32[32,768]{1,0:T(8,128)S(1)}, u32[]{:S(2)}, u32[]{:S(2)}) collective-permute-start(f32[32,768]{1,0:T(8,128)S(1)} %get-tuple-element.35), channel_id=1, source_target_pairs={{0,1},{1,0},{64,65},{65,64},{128,129},{129,128},{192,193},{193,192... | collective-permute-start | bytes 294920 | tf_op jit(solution)/shard_map/ppermute | solution.py:292
  274.4 5.8 %collective-permute-start.3 = (f32[32,768]{1,0:T(8,128)S(1)}, f32[32,768]{1,0:T(8,128)S(1)}, u32[]{:S(2)}, u32[]{:S(2)}) collective-permute-start(f32[32,768]{1,0:T(8,128)S(1)} %get-tuple-element.35), channel_id=1, source_target_pairs={{0,256},{1,257},{64,320},{65,321},{128,384},{129,385},{192,448},{1... | collective-permute-start | bytes 294920 | tf_op jit(solution)/shard_map/ppermute | solution.py:292
  280.2 15.9 %copy-start.1 = (bf16[320,2048]{1,0:T(8,128)(2,1)S(1)}, bf16[320,2048]{1,0:T(8,128)(2,1)}, u32[]{:S(2)}) copy-start(bf16[320,2048]{1,0:T(8,128)(2,1)} %get-tuple-element.36.rows_hbm) | copy-start | bytes 3932164
  301.0 3.5 %collective-permute-start.6 = (f32[32,1024]{1,0:T(8,128)}, f32[32,1024]{1,0:T(8,128)S(1)}, u32[]{:S(2)}, u32[]{:S(2)}) collective-permute-start(f32[32,1024]{1,0:T(8,128)} %get-tuple-element.38), channel_id=1, source_target_pairs={{0,32},{32,0},{1,33},{33,1},{2,34},{34,2},{3,35},{35,3},{4,36},{36... | collective-permute-start | bytes 393224 | tf_op jit(solution)/shard_map/ppermute | solution.py:428
  317.7 15.5 %collective-permute-start.9 = (bf16[32,2048]{1,0:T(8,128)(2,1)S(1)}, bf16[32,2048]{1,0:T(8,128)(2,1)S(1)}, u32[]{:S(2)}, u32[]{:S(2)}) collective-permute-start(bf16[32,2048]{1,0:T(8,128)(2,1)S(1)} %pad_maximum_fusion.6.right_ref), channel_id=1, source_target_pairs={{0,257},{1,256},{64,321},{65,320},{128,385},{129,384},{192,449},{1... | collective-permute-start | bytes 393224 | tf_op jit(solution)/shard_map/ppermute | solution.py:292
  321.5 11.7 %collective-permute-start.8 = (bf16[32,2048]{1,0:T(8,128)(2,1)S(1)}, bf16[32,2048]{1,0:T(8,128)(2,1)S(1)}, u32[]{:S(2)}, u32[]{:S(2)}) collective-permute-start(bf16[32,2048]{1,0:T(8,128)(2,1)S(1)} %pad_maximum_fusion.6.right_ref), channel_id=1, source_target_pairs={{0,1},{1,0},{64,65},{65,64},{128,129},{129,128},{192,193},{193,192... | collective-permute-start | bytes 393224 | tf_op jit(solution)/shard_map/ppermute | solution.py:292
  324.1 9.1 %collective-permute-start.7 = (bf16[32,2048]{1,0:T(8,128)(2,1)S(1)}, bf16[32,2048]{1,0:T(8,128)(2,1)}, u32[]{:S(2)}, u32[]{:S(2)}) collective-permute-start(bf16[32,2048]{1,0:T(8,128)(2,1)S(1)} %pad_maximum_fusion.6.right_ref), channel_id=1, source_target_pairs={{0,256},{1,257},{64,320},{65,321},{128,384},{129,385},{192,448},{1... | collective-permute-start | bytes 393224 | tf_op jit(solution)/shard_map/ppermute | solution.py:292
  332.3 0.9 copy-start.4
Sparse Core Ops, SparseCore 0:
  20.5 73.1 all-gather.4
  274.5 52.4 all-gather.6
